TPU v7x, 32 devices: a whole 2x2x4 slice. The times are simulated.
32 devices in a mesh: row: 4 (over y, x), col: 8 (over z, core).
Axes of the slice: x: 2, y: 2, z: 4, core: 2. Of those that a mesh axis runs over, the one named last changes fastest.
Arguments:
- block_values: float32 [4, 8, 40, 128, 128], P('row', 'col'), may hold values from 7.8125e-06 to 0.00078125
- block_index: int32 [4, 8, 2, 40], P('row', 'col'), may hold values from 0 to 15, as said below
- block_count: int32 [4, 8], P('row', 'col'), may hold values from 1 to 40, as said below
- strength: float32 [32], replicated, may hold values from 1 to 30
- raw_scores: float32 [64, 32, 128], P(('row', 'col')), may hold values from -24 to 24
Outputs:
- smoothed: float32 [64, 32, 128], P(('row', 'col'))
- final_residual: float32 [64, 32, 128], P(('row', 'col'))
Inputs may be any that keep to these rules, and one draw needn't show every extreme that they name: `block_count`: some device has exactly 40 live slots; the others hold between half and all of their share of the upper triangle, scaled to 40. `block_index`: the live slots of one device name distinct blocks, each with global block row at most its global block column; slots at or above the count hold pairs in range that are ignored.
All inputs are finite; a program needn't handle non-finite values.
Results may differ from a plain program's by a relative error of at most 0.0003.
Values sent between devices are 32-bit elements; how exact they have to be, the bound alone decides.
No kernel may reach another device: no remote copies, remote signals or barrier semaphores. Data moves between devices by JAX's collectives and lax.ppermute only.
A program may use at most 64 MiB of HBM per device.

v0:
```python
import jax
import jax.numpy as jnp
from jax import lax
from jax.sharding import PartitionSpec as P

ITERS = 3


def local_terms(values, row_index, col_index, panel_rows, panel_cols):
    picked_cols = jnp.take(panel_cols, col_index, axis=0)
    picked_rows = jnp.take(panel_rows, row_index, axis=0)
    to_rows = jnp.einsum("crk,cik->cri", picked_cols, values, precision=lax.Precision.HIGHEST)
    to_cols = jnp.einsum("cri,cik->crk", picked_rows, values, precision=lax.Precision.HIGHEST)
    row_part = jax.ops.segment_sum(to_rows, row_index, num_segments=panel_rows.shape[0])
    col_part = jax.ops.segment_sum(to_cols, col_index, num_segments=panel_cols.shape[0])
    return (row_part, col_part)


def fold_terms(row_part, col_part):
    return lax.psum_scatter(row_part, "col", scatter_dimension=0, tiled=True) + lax.psum_scatter(
        col_part, "row", scatter_dimension=0, tiled=True
    )


def total(field):
    return jnp.sum(field, axis=(0, 2))


def global_sum(partial_sum):
    return lax.psum(partial_sum, ("row", "col"))


def shards(block_values, block_index, block_count, strength, raw_scores):
    values = block_values[0, 0]
    row_index = block_index[0, 0, 0]
    col_index = block_index[0, 0, 1]
    live_mask = (jnp.arange(values.shape[0], dtype=jnp.int32) < block_count[0, 0]).astype(
        jnp.float32
    )
    masked = values * live_mask[:, None, None]
    segment = raw_scores.shape[0]
    block_size = raw_scores.shape[2]
    rows_here = lax.axis_size("col") * segment
    cols_here = lax.axis_size("row") * segment
    ones_rows = jnp.ones((rows_here, 1, block_size), jnp.float32)
    ones_cols = jnp.ones((cols_here, 1, block_size), jnp.float32)
    degree_rows, degree_cols = local_terms(masked, row_index, col_index, ones_rows, ones_cols)
    degree = fold_terms(degree_rows, degree_cols)
    gains = strength[None, :, None]
    smoothed = jnp.zeros_like(raw_scores)
    residual = raw_scores
    direction = raw_scores
    norm_now = global_sum(total(residual * residual))
    for iteration in range(ITERS):
        panel_rows = lax.all_gather(direction, "col", axis=0, tiled=True)
        panel_cols = lax.all_gather(direction, "row", axis=0, tiled=True)
        row_part, col_part = local_terms(masked, row_index, col_index, panel_rows, panel_cols)
        product = fold_terms(row_part, col_part)
        image = direction + gains * (degree * direction - product)
        step_size = norm_now / global_sum(total(direction * image))
        smoothed = smoothed + step_size[None, :, None] * direction
        residual = residual - step_size[None, :, None] * image
        norm_next = global_sum(total(residual * residual))
        direction = residual + (norm_next / norm_now)[None, :, None] * direction
        norm_now = norm_next
    return (smoothed, residual)


def solution(mesh):
    placed = (
        P("row", "col", None, None, None),
        P("row", "col", None, None),
        P("row", "col"),
        P(),
        P(("row", "col"), None, None),
    )
    return jax.shard_map(
        shards,
        mesh=mesh,
        in_specs=placed,
        out_specs=(P(("row", "col"), None, None), P(("row", "col"), None, None)),
        check_vma=False,
    )
```

profile of v0, /device:TPU:0, one launch (start us, length us, event | category | flops | bytes accessed | tf_op | source)
XLA Modules:
  0.0 485.0 jit_solution(13181248574564258557)
XLA Ops:
  10.0 16.1 %all_gather.19 = f32[16,32,128]{2,1,0:T(8,128)S(1)} all-gather(f32[2,32,128]{2,1,0:T(8,128)} %param.13), channel_id=1, replica_groups=mesh['row'=4,'col'=8] {'col'}, dimensions={0}, use_global_device_ids=true | all-gather | bytes 294912 | tf_op jit(solution)/shard_map/all_gather | solution.py:55
  34.3 8.5 %all_gather.18 = f32[8,32,128]{2,1,0:T(8,128)S(1)} all-gather(f32[2,32,128]{2,1,0:T(8,128)S(1)} %copy-done.9), channel_id=1, replica_groups=mesh['row'=4,'col'=8] {'row'}, dimensions={0}, use_global_device_ids=true | all-gather | bytes 163840 | tf_op jit(solution)/shard_map/all_gather | solution.py:56
  44.2 5.3 %fusion.5 = f32[40,32,128]{2,1,0:T(8,128)S(1)} fusion(f32[1,1,40,128,128]{4,3,2,1,0:T(8,128)S(1)} %copy-done, f32[40]{0:T(128)S(1)} %compare_convert_fusion, f32[40,32,128]{2,1,0:T(8,128)} %gather_fusion.2, pred[40]{0:T(512)(128)(4,1)S(1)} %get-tuple-element.20), kind=kOutput, calls=%fused_computation.22 | convolution fusion | flops 252477440 | bytes 3932360 | tf_op jit(solution)/shard_map/crk,cik->cri/dot_general | solution.py:12
  65.2 9.1 %all-reduce.1 = f32[8,1,128]{2,0,1:T(8,128)S(1)} all-reduce(f32[8,1,128]{2,0,1:T(8,128)S(1)} %bitcast.53), channel_id=3, replica_groups=mesh['row'=4,'col'=8] {'row'}, use_global_device_ids=true, to_apply=%region_5.6.clone | all-reduce | flops 1024 | bytes 8192
  74.2 13.9 %all-reduce = f32[16,1,128]{2,0,1:T(8,128)S(1)} all-reduce(f32[16,1,128]{2,0,1:T(8,128)S(1)} %bitcast.50), channel_id=2, replica_groups=mesh['row'=4,'col'=8] {'col'}, use_global_device_ids=true, to_apply=%region_3.4.clone | all-reduce | flops 2048 | bytes 16384
  93.2 37.7 %all-reduce.2 = (f32[32]{0:T(128)S(1)}, f32[32]{0:T(128)S(1)}) all-reduce(f32[32]{0:T(128)S(1)} %get-tuple-element.5, f32[32]{0:T(128)S(1)} %get-tuple-element.4), channel_id=1, replica_groups=mesh['row'=4,'col'=8] {'row','col'}, use_global_device_ids=true, to_apply=%region_1.2 | all-reduce | flops 64 | bytes 512 | tf_op jit(solution)/shard_map/psum | solution.py:30
  131.9 41.4 %psum.44 = f32[32]{0:T(128)S(1)} all-reduce(f32[32]{0:T(128)S(1)} %get-tuple-element.10), channel_id=1, replica_groups=mesh['row'=4,'col'=8] {'row','col'}, use_global_device_ids=true, to_apply=%region_13.16 | all-reduce | flops 32 | bytes 256 | tf_op jit(solution)/shard_map/psum | solution.py:30
  173.4 9.2 %all_gather.20 = f32[8,32,128]{2,1,0:T(8,128)S(1)} all-gather(f32[2,32,128]{2,1,0:T(8,128)S(1)} %multiply_add_fusion.4), channel_id=1, replica_groups=mesh['row'=4,'col'=8] {'row'}, dimensions={0}, use_global_device_ids=true | all-gather | bytes 163840 | tf_op jit(solution)/shard_map/all_gather | solution.py:56
  182.6 14.2 %all_gather.21 = f32[16,32,128]{2,1,0:T(8,128)S(1)} all-gather(f32[2,32,128]{2,1,0:T(8,128)S(1)} %multiply_add_fusion.4), channel_id=1, replica_groups=mesh['row'=4,'col'=8] {'col'}, dimensions={0}, use_global_device_ids=true | all-gather | bytes 294912 | tf_op jit(solution)/shard_map/all_gather | solution.py:55
  204.4 4.7 scatter_fusion.3
  209.8 5.1 %fusion.3 = f32[40,32,128]{2,1,0:T(8,128)} fusion(f32[1,1,40,128,128]{4,3,2,1,0:T(8,128)S(1)} %copy-done, f32[40]{0:T(128)S(1)} %compare_convert_fusion, f32[40,32,128]{2,1,0:T(8,128)S(1)} %copy-done.8, pred[40]{0:T(512)(128)(4,1)S(1)} %get-tuple-element.20), kind=kOutput, calls=%fused_computation.20 | convolution fusion | flops 252477440 | bytes 3932360 | tf_op jit(solution)/shard_map/crk,cik->cri/dot_general | solution.py:12
  214.9 4.7 scatter_fusion.2
  220.6 11.4 %reduce-scatter.15.cloned.1.call-done = f32[2,32,128]{2,1,0:T(8,128)} async-done(((f32[8,32,128]{2,1,0:T(8,128)}), f32[2,32,128]{2,1,0:T(8,128)}) %reduce-scatter.15.cloned.1.call-update) | async-done | bytes 32784 | tf_op jit(solution)/shard_map/reduce_scatter | solution.py:20
  232.0 32.6 %reduce-scatter.13.cloned.1.call-done = f32[2,32,128]{2,1,0:T(8,128)} async-done(((f32[16,32,128]{2,1,0:T(8,128)}), f32[2,32,128]{2,1,0:T(8,128)}) %reduce-scatter.13.cloned.1.call-update) | async-done | bytes 32784 | tf_op jit(solution)/shard_map/reduce_scatter | solution.py:20
  265.6 37.7 %psum.45 = f32[32]{0:T(128)S(1)} all-reduce(f32[32]{0:T(128)S(1)} %multiply_reduce_fusion.2), channel_id=1, replica_groups=mesh['row'=4,'col'=8] {'row','col'}, use_global_device_ids=true, to_apply=%region_19.22 | all-reduce | flops 32 | bytes 256 | tf_op jit(solution)/shard_map/psum | solution.py:30
  304.3 41.4 %psum.46 = f32[32]{0:T(128)S(1)} all-reduce(f32[32]{0:T(128)S(1)} %get-tuple-element.8), channel_id=1, replica_groups=mesh['row'=4,'col'=8] {'row','col'}, use_global_device_ids=true, to_apply=%region_21.24 | all-reduce | flops 32 | bytes 256 | tf_op jit(solution)/shard_map/psum | solution.py:30
  346.5 9.2 %all_gather.22 = f32[8,32,128]{2,1,0:T(8,128)S(1)} all-gather(f32[2,32,128]{2,1,0:T(8,128)S(1)} %multiply_add_fusion.2), channel_id=1, replica_groups=mesh['row'=4,'col'=8] {'row'}, dimensions={0}, use_global_device_ids=true | all-gather | bytes 163840 | tf_op jit(solution)/shard_map/all_gather | solution.py:56
  355.7 14.2 %all_gather.23 = f32[16,32,128]{2,1,0:T(8,128)S(1)} all-gather(f32[2,32,128]{2,1,0:T(8,128)S(1)} %multiply_add_fusion.2), channel_id=1, replica_groups=mesh['row'=4,'col'=8] {'col'}, dimensions={0}, use_global_device_ids=true | all-gather | bytes 294912 | tf_op jit(solution)/shard_map/all_gather | solution.py:55
  377.5 4.9 %scatter_fusion.5 = f32[8,32,128]{2,1,0:T(8,128)S(1)} fusion(f32[8,32,128]{2,1,0:T(8,128)S(1)} %broadcast.85, s32[40]{0:T(128)} %copy-done.17, f32[40,32,128]{2,1,0:T(8,128)} %fusion), kind=kCustom, calls=%fused_computation.15 | custom fusion | flops 163840 | bytes 1966240 | tf_op jit(solution)/shard_map/scatter-add | solution.py:15
  383.1 5.1 %fusion.1 = f32[40,32,128]{2,1,0:T(8,128)} fusion(f32[1,1,40,128,128]{4,3,2,1,0:T(8,128)S(1)} %copy-done, f32[40]{0:T(128)S(1)} %compare_convert_fusion, f32[40,32,128]{2,1,0:T(8,128)S(1)} %copy-done.7, pred[40]{0:T(512)(128)(4,1)S(1)} %get-tuple-element.20), kind=kOutput, calls=%fused_computation.18 | convolution fusion | flops 252477440 | bytes 3932360 | tf_op jit(solution)/shard_map/crk,cik->cri/dot_general | solution.py:12
  388.2 4.8 scatter_fusion.4
  393.8 11.6 %reduce-scatter.19.cloned.1.call-done = f32[2,32,128]{2,1,0:T(8,128)} async-done(((f32[8,32,128]{2,1,0:T(8,128)}), f32[2,32,128]{2,1,0:T(8,128)}) %reduce-scatter.19.cloned.1.call-update) | async-done | bytes 32784 | tf_op jit(solution)/shard_map/reduce_scatter | solution.py:20
  405.3 32.7 %reduce-scatter.17.cloned.1.call-done = f32[2,32,128]{2,1,0:T(8,128)} async-done(((f32[16,32,128]{2,1,0:T(8,128)}), f32[2,32,128]{2,1,0:T(8,128)}) %reduce-scatter.17.cloned.1.call-update) | async-done | bytes 32784 | tf_op jit(solution)/shard_map/reduce_scatter | solution.py:20
  438.9 37.7 %psum.47 = f32[32]{0:T(128)S(1)} all-reduce(f32[32]{0:T(128)S(1)} %multiply_reduce_fusion), channel_id=1, replica_groups=mesh['row'=4,'col'=8] {'row','col'}, use_global_device_ids=true, to_apply=%region_27.30 | all-reduce | flops 32 | bytes 256 | tf_op jit(solution)/shard_map/psum | solution.py:30
  (124 shorter events, 55.4 us)
Async XLA Ops:
  7.2 81.0 %reduce-scatter.11.cloned.1.call-start = ((), (), s32[]{:S(2)}) async-start(), calls=%async_computation.7 | async-start | bytes 163840 | tf_op jit(solution)/shard_map/reduce_scatter | solution.py:20
  8.0 46.4 %copy-start.12 = (pred[40]{0:T(512)(128)(4,1)}, pred[40]{0:T(512)(128)(4,1)S(1)}, u32[]{:S(2)}) copy-start(pred[40]{0:T(512)(128)(4,1)S(1)} %get-tuple-element.12) | copy-start | bytes 124
  9.3 21.6 %copy-start.17 = (s32[40]{0:T(128)}, s32[40]{0:T(128)S(1)}, u32[]{:S(2)}) copy-start(s32[40]{0:T(128)S(1)} %get-tuple-element.22) | copy-start | bytes 484
  10.0 20.9 %copy-start.19 = (s32[1024]{0:T(1024)}, s32[1024]{0:T(1024)S(1)}, u32[]{:S(2)}) copy-start(s32[1024]{0:T(1024)S(1)} %pad_clamp_fusion) | copy-start | bytes 12292
  30.8 13.4 %copy-start = (f32[1,1,40,128,128]{4,3,2,1,0:T(8,128)S(1)}, f32[1,1,40,128,128]{4,3,2,1,0:T(8,128)}, u32[]{:S(2)}) copy-start(f32[1,1,40,128,128]{4,3,2,1,0:T(8,128)} %param.9) | copy-start | bytes 7864324
  34.2 58.0 %reduce-scatter.9.cloned.1.call-start = ((), (), s32[]{:S(2)}) async-start(), calls=%async_computation.6 | async-start | bytes 294912 | tf_op jit(solution)/shard_map/reduce_scatter | solution.py:20
  44.2 8.9 %copy-start.15 = (s32[1,1,2,40]{3,2,1,0:T(2,128)S(1)}, s32[1,1,2,40]{3,2,1,0:T(2,128)}, u32[]{:S(2)}) copy-start(s32[1,1,2,40]{3,2,1,0:T(2,128)} %param.10) | copy-start | bytes 964
  53.1 178.9 %reduce-scatter.15.cloned.1.call-start = ((), (), s32[]{:S(2)}) async-start(), calls=%async_computation.9 | async-start | bytes 163840 | tf_op jit(solution)/shard_map/reduce_scatter | solution.py:20
  54.5 9.9 %copy-start.18 = (s32[40]{0:T(128)S(1)}, s32[40]{0:T(128)}, u32[]{:S(2)}) copy-start(s32[40]{0:T(128)} %copy-done.17) | copy-start | bytes 484
  54.5 37.7 %copy-start.10 = (f32[2,32,128]{2,1,0:T(8,128)S(1)}, f32[2,32,128]{2,1,0:T(8,128)}, u32[]{:S(2)}) copy-start(f32[2,32,128]{2,1,0:T(8,128)} %param.13) | copy-start | bytes 98308
  54.5 37.7 %copy-start.11 = (f32[32]{0:T(128)S(1)}, f32[32]{0:T(128)}, u32[]{:S(2)}) copy-start(f32[32]{0:T(128)} %param.12) | copy-start | bytes 388
  62.1 137.8 %copy-start.13 = (pred[40]{0:T(512)(128)(4,1)S(1)}, pred[40]{0:T(512)(128)(4,1)}, u32[]{:S(2)}) copy-start(pred[40]{0:T(512)(128)(4,1)} %copy-done.12) | copy-start | bytes 124
  130.9 73.4 %copy-start.21 = (f32[32]{0:T(128)}, f32[32]{0:T(128)S(1)}, u32[]{:S(2)}) copy-start(f32[32]{0:T(128)S(1)} %div.15) | copy-start | bytes 388
  173.3 130.1 %copy-start.27 = (f32[32]{0:T(128)}, f32[32]{0:T(128)S(1)}, u32[]{:S(2)}) copy-start(f32[32]{0:T(128)S(1)} %psum.44) | copy-start | bytes 388
  199.9 9.9 %copy-start.8 = (f32[40,32,128]{2,1,0:T(8,128)S(1)}, f32[40,32,128]{2,1,0:T(8,128)}, u32[]{:S(2)}) copy-start(f32[40,32,128]{2,1,0:T(8,128)} %gather_fusion.4) | copy-start | bytes 1966084
  209.8 54.9 %reduce-scatter.13.cloned.1.call-start = ((), (), s32[]{:S(2)}) async-start(), calls=%async_computation.8 | async-start | bytes 294912 | tf_op jit(solution)/shard_map/reduce_scatter | solution.py:20
  214.9 158.1 %copy-start.14 = (pred[40]{0:T(512)(128)(4,1)S(1)}, pred[40]{0:T(512)(128)(4,1)}, u32[]{:S(2)}) copy-start(pred[40]{0:T(512)(128)(4,1)} %copy-done.12) | copy-start | bytes 124
  220.4 184.9 %reduce-scatter.19.cloned.1.call-start = ((), (), s32[]{:S(2)}) async-start(), calls=%async_computation.11 | async-start | bytes 163840 | tf_op jit(solution)/shard_map/reduce_scatter | solution.py:20
  303.4 69.7 %copy-start.23 = (f32[32]{0:T(128)}, f32[32]{0:T(128)S(1)}, u32[]{:S(2)}) copy-start(f32[32]{0:T(128)S(1)} %div.17) | copy-start | bytes 388
  373.0 10.0 %copy-start.7 = (f32[40,32,128]{2,1,0:T(8,128)S(1)}, f32[40,32,128]{2,1,0:T(8,128)}, u32[]{:S(2)}) copy-start(f32[40,32,128]{2,1,0:T(8,128)} %gather_fusion.6) | copy-start | bytes 1966084
  383.0 93.7 %copy-start.29 = (f32[32]{0:T(128)S(1)}, f32[32]{0:T(128)}, u32[]{:S(2)}) copy-start(f32[32]{0:T(128)} %copy-done.28) | copy-start | bytes 388
  383.0 93.7 %copy-start.22 = (f32[32]{0:T(128)S(1)}, f32[32]{0:T(128)}, u32[]{:S(2)}) copy-start(f32[32]{0:T(128)} %copy-done.21) | copy-start | bytes 388
  383.0 93.6 %copy-start.24 = (f32[32]{0:T(128)S(1)}, f32[32]{0:T(128)}, u32[]{:S(2)}) copy-start(f32[32]{0:T(128)} %copy-done.23) | copy-start | bytes 388
  383.0 54.9 %reduce-scatter.17.cloned.1.call-start = ((), (), s32[]{:S(2)}) async-start(), calls=%async_computation.10 | async-start | bytes 294912 | tf_op jit(solution)/shard_map/reduce_scatter | solution.py:20
  (12 other events, 35.8 us)
Sparse Core Ops, SparseCore 0:
  34.4 24.9 reduce-scatter.10
  61.7 30.4 reduce-scatter.8
  209.9 22.1 reduce-scatter.14
  234.2 30.4 reduce-scatter.12
  383.1 22.1 reduce-scatter.18
  407.5 30.4 reduce-scatter.16
where the time goes:
time: 487 us; the launch traced here: 485 us
  blocking collectives  290 us (60%)
  waiting for transfers between devices  92.4 us (19%)
  matrix products  35 us (7%)
  other arithmetic  34.3 us (7%)
  between operations  16.4 us (3%)
  local copies, waits for them, and re-layouts  16 us (3%)
    psum x5, blocking collectives, global_sum(): return lax.psum(partial_sum, ('row', 'col'))  196 us
    reduce_scatter x3, waiting for transfers between devices, fold_terms(): lax.psum_scatter(row_part, 'col', scatter_dimension=0, tiled=True)  69.3 us
    all_gather x3, blocking collectives, shards(): panel_rows = lax.all_gather(direction, 'col', axis=0, tiled=True)  44.4 us
    all_gather x3, blocking collectives, shards(): panel_cols = lax.all_gather(direction, 'row', axis=0, tiled=True)  26.9 us
    reduce_scatter x3, waiting for transfers between devices, fold_terms(): lax.psum_scatter(col_part, 'row', scatter_dimension=0, tiled=True)  23 us
    unnamed x2, blocking collectives  22.9 us
    dot_general x4, matrix products, local_terms(): jnp.einsum('crk,cik->cri', picked_cols, values, precision=lax.Precision.H...  19.8 us
    dot_general x4, matrix products, local_terms(): jnp.einsum('cri,cik->crk', picked_rows, values, precision=lax.Precision.H...  15.3 us
  transfers between devices with their start and end apart: 6, of which 5 were waited for; matrix products, arithmetic and copies ran while one was open for 8% of the time, Pallas kernels for 0%

commit v1 on v0

v1 whole, which is shorter than its diff:
```python
import functools
import jax
import jax.numpy as jnp
from jax import lax
from jax.experimental import pallas as pl
from jax.experimental.pallas import tpu as pltpu
from jax.sharding import PartitionSpec as P

BF = jnp.bfloat16
F32 = jnp.float32
VMEM = pl.BlockSpec(memory_space=pltpu.VMEM)
SMEM = pl.BlockSpec(memory_space=pltpu.SMEM)
GROUP = 8


def split_kernel(meta_ref, values_ref, out_ref):
    first = pl.program_id(0) * values_ref.shape[0]
    size = values_ref.shape[1]

    def write(turn):
        for slot in range(values_ref.shape[0]):
            block = values_ref[slot]
            block = jnp.where(first + slot < meta_ref[1], block, 0.0)
            block = block.T if turn else block
            high = block.astype(BF)
            out_ref[slot, :size] = high
            out_ref[slot, size:] = (block - high.astype(F32)).astype(BF)

    @pl.when(meta_ref[0] == 0)
    def _():
        write(True)

    @pl.when(meta_ref[0] != 0)
    def _():
        write(False)


def split_blocks(values, core, count):
    slots, size, _ = values.shape
    step = GROUP
    return pl.pallas_call(
        split_kernel,
        grid=(slots // step,),
        in_specs=[SMEM, pl.BlockSpec((step, size, size), lambda i: (i, 0, 0))],
        out_specs=pl.BlockSpec((step, 2 * size, size), lambda i: (i, 0, 0)),
        out_shape=jax.ShapeDtypeStruct((slots, 2 * size, size), BF),
        compiler_params=pltpu.CompilerParams(vmem_limit_bytes=32 * 2**20),
        cost_estimate=pl.CostEstimate(
            flops=slots * size * size * 4, bytes_accessed=slots * size * size * 8, transcendentals=0
        ),
    )(jnp.stack([core, count]), values)


def apply_kernel(parts, with_degree, with_aux, *refs):
    meta_ref, own_ref, other_ref = refs[:3]
    fields = refs[3 : 3 + parts]
    outs = refs[3 + parts : 3 + 2 * parts]
    stack_ref, sum_ref = refs[3 + 2 * parts :]
    per = outs[0].shape[0] - 1
    width, size = fields[0].shape[1:]
    for part in range(parts):
        for j in range(per):
            x = fields[part][j]
            high = x.astype(BF)
            low = (x - high.astype(F32)).astype(BF)
            f = part * per + j
            for half in range(2):
                cut = slice(half * size, (half + 1) * size)
                stack_ref[f, :width, cut] = high
                stack_ref[f, width : 2 * width, cut] = low
            if with_degree:
                stack_ref[f, 2 * width :, :] = jnp.ones((16, 2 * size), BF)
    sum_ref[...] = jnp.zeros_like(sum_ref)
    slots = own_ref.shape[0]

    def sweep(values_ref, base, count):
        def group(g, carry):
            products = []
            for i in range(GROUP):
                q = g * GROUP + i
                products.append(
                    jnp.dot(
                        stack_ref[meta_ref[0, base + q]],
                        values_ref[q],
                        preferred_element_type=F32,
                    )
                )
            for i in range(GROUP):
                to = meta_ref[1, base + g * GROUP + i]
                whole = products[i]
                sum_ref[to, :width] += whole[:width] + whole[width : 2 * width]
                if with_degree:
                    sum_ref[to, width:] += whole[2 * width : 2 * width + 8]
            return carry

        lax.fori_loop(0, (count + GROUP - 1) // GROUP, group, 0)

    sweep(own_ref, 0, meta_ref[2, 0])
    sweep(other_ref, slots, meta_ref[2, 1])
    if with_aux:
        aux = fields[0][per]
        for part in range(1, parts):
            aux = aux + fields[part][per]
    for part in range(parts):
        for j in range(per):
            outs[part][j] = sum_ref[part * per + j, :width]
        if with_aux:
            outs[part][per] = aux
        else:
            outs[part][per] = jnp.zeros((width, size), F32)
            for j in range(per):
                outs[part][per, j : j + 1, :] = sum_ref[part * per + j, width : width + 1]


def apply_blocks(meta, own, other, fields, with_degree, with_aux):
    parts = len(fields)
    width, size = fields[0].shape[1:]
    per = fields[0].shape[0] - (1 if with_aux else 0)
    rows = 2 * width + (16 if with_degree else 0)
    sums = width + (8 if with_degree else 0)
    slots = own.shape[0]
    return pl.pallas_call(
        functools.partial(apply_kernel, parts, with_degree, with_aux),
        in_specs=[SMEM] + [VMEM] * (2 + parts),
        out_specs=[VMEM] * parts,
        out_shape=[jax.ShapeDtypeStruct((per + 1, width, size), F32)] * parts,
        scratch_shapes=[
            pltpu.VMEM((parts * per, rows, 2 * size), BF),
            pltpu.VMEM((parts * per, sums, size), F32),
        ],
        compiler_params=pltpu.CompilerParams(vmem_limit_bytes=40 * 2**20),
        cost_estimate=pl.CostEstimate(
            flops=2 * slots * 4 * rows * size * size,
            bytes_accessed=4 * slots * size * size * 2,
            transcendentals=0,
        ),
    )(meta, own, other, *fields)


def dots(*pairs):
    lane = lax.broadcasted_iota(jnp.int32, pairs[0][0].shape[1:], 1)
    aux = jnp.zeros(pairs[0][0].shape[1:], F32)
    for n, (a, b) in enumerate(pairs):
        aux = jnp.where(lane == n, jnp.sum(a * b, axis=(0, 2))[:, None], aux)
    return aux


def lane_of(aux, n):
    return aux[None, :, n : n + 1]


def build(n_row, n_col):
    n_line = n_col // 2
    parts = max(n_row, n_line)

    def joint(array, offset, row_core):
        pairs = []
        for r in range(n_row):
            for z in range(n_line):
                for k in range(2):
                    to_r, to_z = (r ^ offset, z) if k == row_core else (r, z ^ offset)
                    if to_r < n_row and to_z < n_line:
                        pairs.append((r * n_col + z * 2 + k, to_r * n_col + to_z * 2 + k))
        return lax.ppermute(array, ("row", "col"), pairs)

    def swap(array):
        return lax.ppermute(array, "col", [(c, c ^ 1) for c in range(n_col)])

    def gather(field):
        return [field] + [joint(field, offset, 0) for offset in range(1, parts)]

    def collect(sent):
        return sent[0] + sum(joint(sent[offset], offset, 1) for offset in range(1, parts))

    def shards(block_values, block_index, block_count, strength, raw_scores):
        values = block_values[0, 0]
        index = block_index[0, 0]
        count = block_count[0, 0]
        row = lax.axis_index("row").astype(jnp.int32)
        col = lax.axis_index("col").astype(jnp.int32)
        line, core = col // 2, col % 2
        seg = raw_scores.shape[0]
        per = 2 * seg
        raw_other = swap(raw_scores)
        ints = jnp.concatenate([index, jnp.full((1, index.shape[1]), count, jnp.int32)], axis=0)
        ints_other = swap(ints)
        values_other = swap(values)

        def places(pair, home):
            row_place = ((pair[0] // per) ^ line) * per + pair[0] % per
            col_place = ((pair[1] // seg) ^ row) * per + home * seg + pair[1] % seg
            return jnp.where(
                core == 0, jnp.stack([col_place, row_place]), jnp.stack([row_place, col_place])
            )

        counts = jnp.zeros((1, 2 * index.shape[1]), jnp.int32)
        counts = counts.at[0, 0].set(count).at[0, 1].set(ints_other[2, 0])
        meta = jnp.concatenate(
            [jnp.concatenate([places(index, core), places(ints_other, 1 - core)], axis=1), counts],
            axis=0,
        )
        raw = jnp.where(
            core == 0,
            jnp.concatenate([raw_scores, raw_other]),
            jnp.concatenate([raw_other, raw_scores]),
        )
        gains = strength[None, :, None]
        gathered = gather(raw)
        own = split_blocks(values, core, count)
        other = split_blocks(values_other, core, ints_other[2, 0])

        mine = collect(apply_blocks(meta, own, other, gathered, True, False))
        both = mine + swap(mine)
        degree = both[per, :per, None, :]
        w0 = raw + gains * (degree * raw - both[:per])

        def with_aux(field, *pairs):
            return jnp.concatenate([field, dots(*pairs)[None]])

        mine = collect(
            apply_blocks(meta, own, other, gather(with_aux(w0, (raw, raw), (raw, w0))), False, True)
        )
        sums = mine[per]
        product = mine[:per] + swap(mine[:per])
        q0 = w0 + gains * (degree * w0 - product)
        gamma0, delta0 = lane_of(sums, 0), lane_of(sums, 1)
        step0 = gamma0 / delta0
        r1 = raw - step0 * w0
        w1 = w0 - step0 * q0
        h = r1 - step0 * w1

        pairs = (
            (r1, r1),
            (r1, w1),
            (r1, w0),
            (h, h),
            (h, w1),
            (h, w0),
            (w1, w1),
            (w1, w0),
            (w0, w0),
            (h, q0),
            (w1, q0),
            (w0, q0),
        )
        mine = collect(apply_blocks(meta, own, other, gather(with_aux(h, *pairs)), False, True))
        sums = mine[per]
        product = mine[:per] + swap(mine[:per])
        qh = h + gains * (degree * h - product)
        tail = dots((h, qh))
        tail = sum(gather(tail))
        tail = collect([tail] * parts)
        g11, r1w1, r1w0, hh, hw1, hw0, w11, w10, w00, a_h0, a_10, a_00 = (
            lane_of(sums, n) for n in range(len(pairs))
        )
        a_hh = lane_of(tail, 0)
        ratio0 = g11 / gamma0
        curve1 = r1w1 + 2.0 * ratio0 * r1w0 + ratio0 * ratio0 * delta0
        step1 = g11 / curve1
        e = step0 - step1
        f = -step1 * ratio0
        g22 = hh + 2.0 * (e * hw1 + f * hw0 + e * f * w10) + e * e * w11 + f * f * w00
        ratio1 = g22 / g11
        r2w1 = hw1 + e * w11 + f * w10
        r2w0 = hw0 + e * w10 + f * w00
        a_h1 = (hw1 - a_hh) / step0
        a_11 = (w11 - a_h1) / step0
        curve2 = a_hh + e * e * a_11 + f * f * a_00
        curve2 = curve2 + 2.0 * (e * a_h1 + f * a_h0 + e * f * a_10)
        curve2 = curve2 + 2.0 * ratio1 * (r2w1 + ratio0 * r2w0) + ratio1 * ratio1 * curve1
        step2 = g22 / curve2
        p1 = r1 + ratio0 * raw
        s1 = w1 + ratio0 * w0
        r2 = h + e * w1 + f * w0
        p2 = r2 + ratio1 * p1
        s2 = qh + e * (w1 - qh) / step0 + f * q0 + ratio1 * s1
        smoothed = step0 * raw + step1 * p1 + step2 * p2
        residual = r2 - step2 * s2

        def pick(field):
            return jnp.where(core == 0, field[:seg], field[seg:])

        return (pick(smoothed), pick(residual))

    return shards


def solution(mesh):
    placed = (
        P("row", "col", None, None, None),
        P("row", "col", None, None),
        P("row", "col"),
        P(),
        P(("row", "col"), None, None),
    )
    return jax.shard_map(
        build(mesh.shape["row"], mesh.shape["col"]),
        mesh=mesh,
        in_specs=placed,
        out_specs=(P(("row", "col"), None, None), P(("row", "col"), None, None)),
        check_vma=False,
    )
```

time: 487 us -> 94.1 us (0.19)
  blocking collectives: 290 us -> 0 us
  waiting for transfers between devices: 92.4 us -> 31.8 us
  matrix products: 35 us -> 0 us
  starting transfers between devices: 0.47 us -> 34.3 us
  other arithmetic: 34.3 us -> 7.54 us
  between operations: 16.4 us -> 2.29 us
  Pallas kernels: 0 us -> 12.6 us
  local copies, waits for them, and re-layouts: 16 us -> 5.5 us
    psum x5 -> x0, blocking collectives: 196 us -> none  [global_sum(): return lax.psum(partial_sum, ('row', 'col'))]
    reduce_scatter x6 -> x0, waiting for transfers between devices: 92.3 us -> none  [the longest x3 69.3 us: fold_terms(): lax.psum_scatter(row_part, 'col', scatter_dimension=0, tiled=True)]
    all_gather x6 -> x0, blocking collectives: 71.4 us -> none  [the longest x3 44.4 us: shards(): panel_rows = lax.all_gather(direction, 'col', axis=0, tiled=True)]
    dot_general x8 -> x0, matrix products: 35 us -> none  [the longest x4 19.8 us: local_terms(): jnp.einsum('crk,cik->cri', picked_cols, values, precision=lax.Precision.H...]
    ppermute x0 -> x30, starting transfers between devices: none -> 34.3 us  [the longest x24 33.1 us: joint(): return lax.ppermute(array, ('row', 'col'), pairs)]
    ppermute x0 -> x30, waiting for transfers between devices: none -> 31.8 us  [the longest x24 28.2 us: joint(): return lax.ppermute(array, ('row', 'col'), pairs)]
    scatter-add x8 -> x0, other arithmetic: 26.3 us -> none  [the longest x4 13.2 us: local_terms(): jax.ops.segment_sum(to_rows, row_index, num_segments=panel_rows.shape[0])]
    unnamed x2 -> x0, blocking collectives: 22.9 us -> none
  transfers between devices with their start and end apart: 6 -> 30, of which waited for: 5 -> 22; matrix products, arithmetic and copies ran while one was open for 8% -> 10% of each run, Pallas kernels for 0% -> 6%
where the time goes in v1:
time: 94.1 us; the launch traced here: 94 us
  starting transfers between devices  34.3 us (36%)
  waiting for transfers between devices  31.8 us (34%)
  Pallas kernels  12.6 us (13%)
  other arithmetic  7.54 us (8%)
  local copies, waits for them, and re-layouts  5.5 us (6%)
  between operations  2.29 us (2%)
    ppermute x24, starting transfers between devices, joint(): return lax.ppermute(array, ('row', 'col'), pairs)  33.1 us
    ppermute x24, waiting for transfers between devices, joint(): return lax.ppermute(array, ('row', 'col'), pairs)  28.2 us
    pallas_call x3, Pallas kernels, apply_blocks(): pl.pallas_call(functools.partial(apply_kernel, parts, with_degree, with_a...  6.99 us
    pallas_call x2, Pallas kernels, split_blocks(): pl.pallas_call(split_kernel, grid=(slots // step,), in_specs=[SMEM, pl.Bl...  5.6 us
    another operation x3, other arithmetic  3.75 us
    ppermute x6, waiting for transfers between devices, swap(): return lax.ppermute(array, 'col', [(c, c ^ 1) for c in range(n_col)])  3.54 us
  transfers between devices with their start and end apart: 30, of which 22 were waited for; matrix products, arithmetic and copies ran while one was open for 10% of the time, Pallas kernels for 6%

profile of v1, /device:TPU:0, one launch (start us, length us, event | category | flops | bytes accessed | tf_op | source)
XLA Modules:
  0.0 94.0 jit_solution(12930315641115853385)
XLA Ops:
  6.5 1.7 %copy-done = f32[1,1,40,128,128]{4,3,2,1,0:T(8,128)S(1)} copy-done((f32[1,1,40,128,128]{4,3,2,1,0:T(8,128)S(1)}, f32[1,1,40,128,128]{4,3,2,1,0:T(8,128)}, u32[]{:S(2)}) %copy-start) | copy-done | bytes 2621464
  8.3 1.7 %shard_map.68.refs_1_ = bf16[40,256,128]{2,1,0:T(8,128)(2,1)S(1)} custom-call(s32[2]{0:T(128)S(1)} %pad_add_fusion.1.meta_ref, f32[40,128,128]{2,1,0:T(8,128)S(1)} %bitcast.48), custom_call_target="tpu_custom_call" | custom-call | flops 2621440 | bytes 5242880 | tf_op jit(solution)/shard_map/pallas_call | solution.py:41
  10.6 2.5 %fusion.8 = s32[1,1]{1,0:T(1,128)} fusion(pred[1,1]{1,0:T(4,128)(4,1)} %bitcast.5, s32[1,1]{1,0:T(1,128)} %slice.138, s32[]{:T(128)} %bitcast.6, s32[1,1]{1,0:T(1,128)S(6)} %select.100), kind=kLoop, calls=%fused_computation.110 | loop fusion | flops 1 | bytes 17 | tf_op jit(solution)/shard_map/select.3
  14.5 2.6 %collective-permute-start.3 = (f32[4,32,128]{2,1,0:T(8,128)S(1)}, f32[4,32,128]{2,1,0:T(8,128)S(1)}, u32[]{:S(2)}, u32[]{:S(2)}) collective-permute-start(f32[4,32,128]{2,1,0:T(8,128)S(1)} %maximum_select_fusion.refs_3_), channel_id=1, source_target_pairs={{0,8},{1,3},{2,10},{3,1},{4,12},{5,7},{6,14},{7,5},{8,0},{9,11},{1... | collective-permute-start | bytes 196616 | tf_op jit(solution)/shard_map/ppermute | solution.py:164
  19.3 3.9 %shard_map.69.refs_2_ = bf16[40,256,128]{2,1,0:T(8,128)(2,1)S(1)} custom-call(s32[2]{0:T(128)S(1)} %pad_add_fusion.2.meta_ref, f32[40,128,128]{2,1,0:T(8,128)} %collective-permute-done.1.values_ref), custom_call_target="tpu_custom_call" | custom-call | flops 2621440 | bytes 5242880 | tf_op jit(solution)/shard_map/pallas_call | solution.py:41
  23.7 2.5 %shard_map.70 = (f32[5,32,128]{2,1,0:T(8,128)S(1)}, f32[5,32,128]{2,1,0:T(8,128)S(1)}, f32[5,32,128]{2,1,0:T(8,128)S(1)}, f32[5,32,128]{2,1,0:T(8,128)S(1)}) custom-call(s32[3,80]{1,0:T(4,128)S(1)} %pad_add_fusion.refs_0_, bf16[40,256,128]{2,1,0:T(8,128)(2,1)S(1)} %shard_map.68.refs_1_, bf16[40,256,128]{2,1,0:T(8,128)(2,1)S(1)} %shard_map.69.refs_2_, ...), custom_call_target="tpu_custom_call" | custom-call | flops 419430400 | bytes 5242880 | tf_op jit(solution)/shard_map/pallas_call | solution.py:122
  27.8 3.3 %collective-permute-start.7 = (f32[5,32,128]{2,1,0:T(8,128)S(1)}, f32[5,32,128]{2,1,0:T(8,128)S(1)}, u32[]{:S(2)}, u32[]{:S(2)}) collective-permute-start(f32[5,32,128]{2,1,0:T(8,128)S(1)} %get-tuple-element.40), channel_id=1, source_target_pairs={{0,4},{1,17},{2,6},{3,19},{4,0},{5,21},{6,2},{7,23},{8,12},{9,25},... | collective-permute-start | bytes 245768 | tf_op jit(solution)/shard_map/ppermute | solution.py:164
  31.2 3.3 %collective-permute-done.7 = f32[5,32,128]{2,1,0:T(8,128)S(1)} collective-permute-done((f32[5,32,128]{2,1,0:T(8,128)S(1)}, f32[5,32,128]{2,1,0:T(8,128)S(1)}, u32[]{:S(2)}, u32[]{:S(2)}) %collective-permute-start.7) | collective-permute-done | bytes 81952 | tf_op jit(solution)/shard_map/ppermute | solution.py:164
  34.5 2.9 %collective-permute-done.8 = f32[5,32,128]{2,1,0:T(8,128)S(1)} collective-permute-done((f32[5,32,128]{2,1,0:T(8,128)S(1)}, f32[5,32,128]{2,1,0:T(8,128)S(1)}, u32[]{:S(2)}, u32[]{:S(2)}) %collective-permute-start.8) | collective-permute-done | bytes 81952 | tf_op jit(solution)/shard_map/ppermute | solution.py:164
  40.1 2.6 %collective-permute-start.12 = (f32[5,32,128]{2,1,0:T(8,128)S(1)}, f32[5,32,128]{2,1,0:T(8,128)S(1)}, u32[]{:S(2)}, u32[]{:S(2)}) collective-permute-start(f32[5,32,128]{2,1,0:T(8,128)S(1)} %pad_maximum_fusion.refs_3_), channel_id=1, source_target_pairs={{0,24},{1,7},{2,26},{3,5},{4,28},{5,3},{6,30},{7,1},{8,16},{9,15},... | collective-permute-start | bytes 245768 | tf_op jit(solution)/shard_map/ppermute | solution.py:164
  45.4 2.3 %shard_map.71 = (f32[5,32,128]{2,1,0:T(8,128)S(1)}, f32[5,32,128]{2,1,0:T(8,128)S(1)}, f32[5,32,128]{2,1,0:T(8,128)S(1)}, f32[5,32,128]{2,1,0:T(8,128)S(1)}) custom-call(s32[3,80]{1,0:T(4,128)S(1)} %pad_add_fusion.refs_0_, bf16[40,256,128]{2,1,0:T(8,128)(2,1)S(1)} %shard_map.68.refs_1_, bf16[40,256,128]{2,1,0:T(8,128)(2,1)S(1)} %shard_map.69.refs_2_, ...), custom_call_target="tpu_custom_call" | custom-call | flops 335544320 | bytes 5242880 | tf_op jit(solution)/shard_map/pallas_call | solution.py:122
  47.8 2.2 %collective-permute-start.14 = (f32[5,32,128]{2,1,0:T(8,128)S(1)}, f32[5,32,128]{2,1,0:T(8,128)S(1)}, u32[]{:S(2)}, u32[]{:S(2)}) collective-permute-start(f32[5,32,128]{2,1,0:T(8,128)S(1)} %get-tuple-element.44), channel_id=1, source_target_pairs={{0,4},{1,17},{2,6},{3,19},{4,0},{5,21},{6,2},{7,23},{8,12},{9,25},... | collective-permute-start | bytes 245768 | tf_op jit(solution)/shard_map/ppermute | solution.py:164
  50.0 2.2 %collective-permute-start.15 = (f32[5,32,128]{2,1,0:T(8,128)S(1)}, f32[5,32,128]{2,1,0:T(8,128)S(1)}, u32[]{:S(2)}, u32[]{:S(2)}) collective-permute-start(f32[5,32,128]{2,1,0:T(8,128)S(1)} %get-tuple-element.45), channel_id=1, source_target_pairs={{0,6},{1,25},{2,4},{3,27},{4,2},{5,29},{6,0},{7,31},{8,14},{9,17},... | collective-permute-start | bytes 245768 | tf_op jit(solution)/shard_map/ppermute | solution.py:164
  53.2 3.1 %collective-permute-done.15 = f32[5,32,128]{2,1,0:T(8,128)S(1)} collective-permute-done((f32[5,32,128]{2,1,0:T(8,128)S(1)}, f32[5,32,128]{2,1,0:T(8,128)S(1)}, u32[]{:S(2)}, u32[]{:S(2)}) %collective-permute-start.15) | collective-permute-done | bytes 81952 | tf_op jit(solution)/shard_map/ppermute | solution.py:164
  59.6 2.2 %collective-permute-start.19 = (f32[5,32,128]{2,1,0:T(8,128)S(1)}, f32[5,32,128]{2,1,0:T(8,128)S(1)}, u32[]{:S(2)}, u32[]{:S(2)}) collective-permute-start(f32[5,32,128]{2,1,0:T(8,128)S(1)} %pad_maximum_fusion.1.refs_3_), channel_id=1, source_target_pairs={{0,24},{1,7},{2,26},{3,5},{4,28},{5,3},{6,30},{7,1},{8,16},{9,15},... | collective-permute-start | bytes 245768 | tf_op jit(solution)/shard_map/ppermute | solution.py:164
  63.0 2.0 %collective-permute-done.19.refs_6_ = f32[5,32,128]{2,1,0:T(8,128)S(1)} collective-permute-done((f32[5,32,128]{2,1,0:T(8,128)S(1)}, f32[5,32,128]{2,1,0:T(8,128)S(1)}, u32[]{:S(2)}, u32[]{:S(2)}) %collective-permute-start.19) | collective-permute-done | bytes 81952 | tf_op jit(solution)/shard_map/ppermute | solution.py:164
  64.9 2.3 %shard_map.72 = (f32[5,32,128]{2,1,0:T(8,128)S(1)}, f32[5,32,128]{2,1,0:T(8,128)S(1)}, f32[5,32,128]{2,1,0:T(8,128)S(1)}, f32[5,32,128]{2,1,0:T(8,128)S(1)}) custom-call(s32[3,80]{1,0:T(4,128)S(1)} %pad_add_fusion.refs_0_, bf16[40,256,128]{2,1,0:T(8,128)(2,1)S(1)} %shard_map.68.refs_1_, bf16[40,256,128]{2,1,0:T(8,128)(2,1)S(1)} %shard_map.69.refs_2_, ...), custom_call_target="tpu_custom_call" | custom-call | flops 335544320 | bytes 5242880 | tf_op jit(solution)/shard_map/pallas_call | solution.py:122
  68.1 3.2 %collective-permute-start.21 = (f32[5,32,128]{2,1,0:T(8,128)S(1)}, f32[5,32,128]{2,1,0:T(8,128)S(1)}, u32[]{:S(2)}, u32[]{:S(2)}) collective-permute-start(f32[5,32,128]{2,1,0:T(8,128)S(1)} %get-tuple-element.48), channel_id=1, source_target_pairs={{0,4},{1,17},{2,6},{3,19},{4,0},{5,21},{6,2},{7,23},{8,12},{9,25},... | collective-permute-start | bytes 245768 | tf_op jit(solution)/shard_map/ppermute | solution.py:164
  71.7 2.9 %collective-permute-done.21 = f32[5,32,128]{2,1,0:T(8,128)S(1)} collective-permute-done((f32[5,32,128]{2,1,0:T(8,128)S(1)}, f32[5,32,128]{2,1,0:T(8,128)S(1)}, u32[]{:S(2)}, u32[]{:S(2)}) %collective-permute-start.21) | collective-permute-done | bytes 81952 | tf_op jit(solution)/shard_map/ppermute | solution.py:164
  74.6 2.9 %collective-permute-done.22 = f32[5,32,128]{2,1,0:T(8,128)S(1)} collective-permute-done((f32[5,32,128]{2,1,0:T(8,128)S(1)}, f32[5,32,128]{2,1,0:T(8,128)S(1)}, u32[]{:S(2)}, u32[]{:S(2)}) %collective-permute-start.22) | collective-permute-done | bytes 81952 | tf_op jit(solution)/shard_map/ppermute | solution.py:164
  79.5 3.2 %collective-permute-start.26 = (f32[32,128]{0,1:T(8,128)S(1)}, f32[32,128]{0,1:T(8,128)S(1)}, u32[]{:S(2)}, u32[]{:S(2)}) collective-permute-start(f32[32,128]{0,1:T(8,128)S(1)} %broadcast_select_fusion), channel_id=1, source_target_pairs={{0,24},{1,7},{2,26},{3,5},{4,28},{5,3},{6,30},{7,1},{8,16},{9,15},... | collective-permute-start | bytes 49160 | tf_op jit(solution)/shard_map/ppermute | solution.py:164
  85.1 2.0 %collective-permute-start.28 = (f32[32,128]{0,1:T(8,128)S(1)}, f32[32,128]{0,1:T(8,128)S(1)}, u32[]{:S(2)}, u32[]{:S(2)}) collective-permute-start(f32[32,128]{0,1:T(8,128)S(1)} %add_add_fusion.3), channel_id=1, source_target_pairs={{0,4},{1,17},{2,6},{3,19},{4,0},{5,21},{6,2},{7,23},{8,12},{9,25},... | collective-permute-start | bytes 49160 | tf_op jit(solution)/shard_map/ppermute | solution.py:164
  87.1 2.4 %collective-permute-start.29 = (f32[32,128]{0,1:T(8,128)S(1)}, f32[32,128]{0,1:T(8,128)S(1)}, u32[]{:S(2)}, u32[]{:S(2)}) collective-permute-start(f32[32,128]{0,1:T(8,128)S(1)} %add_add_fusion.3), channel_id=1, source_target_pairs={{0,6},{1,25},{2,4},{3,27},{4,2},{5,29},{6,0},{7,31},{8,14},{9,17},... | collective-permute-start | bytes 49160 | tf_op jit(solution)/shard_map/ppermute | solution.py:164
  90.4 2.8 %collective-permute-done.29 = f32[32,128]{0,1:T(8,128)S(1)} collective-permute-done((f32[32,128]{0,1:T(8,128)S(1)}, f32[32,128]{0,1:T(8,128)S(1)}, u32[]{:S(2)}, u32[]{:S(2)}) %collective-permute-start.29) | collective-permute-done | bytes 16416 | tf_op jit(solution)/shard_map/ppermute | solution.py:164
  (101 shorter events, 29.1 us)
Async XLA Ops:
  0.6 18.6 %collective-permute-start.1 = (f32[40,128,128]{2,1,0:T(8,128)}, f32[40,128,128]{2,1,0:T(8,128)}, u32[]{:S(2)}, u32[]{:S(2)}) collective-permute-start(f32[40,128,128]{2,1,0:T(8,128)} %bitcast.47), channel_id=1, source_target_pairs={{0,1},{1,0},{2,3},{3,2},{4,5},{5,4},{6,7},{7,6},{8,9},{9,8},{10,11... | collective-permute-start | bytes 7864328 | tf_op jit(solution)/shard_map/ppermute | solution.py:167
  2.5 7.5 %collective-permute-start = (s32[3,40]{1,0:T(4,128)S(1)}, s32[3,40]{1,0:T(4,128)S(1)}, u32[]{:S(2)}, u32[]{:S(2)}) collective-permute-start(s32[3,40]{1,0:T(4,128)S(1)} %concatenate.25), channel_id=1, source_target_pairs={{0,1},{1,0},{2,3},{3,2},{4,5},{5,4},{6,7},{7,6},{8,9},{9,8},{10,11... | collective-permute-start | bytes 1448 | tf_op jit(solution)/shard_map/ppermute | solution.py:167
  2.5 11.9 %collective-permute-start.2 = (f32[2,32,128]{2,1,0:T(8,128)}, f32[2,32,128]{2,1,0:T(8,128)S(1)}, u32[]{:S(2)}, u32[]{:S(2)}) collective-permute-start(f32[2,32,128]{2,1,0:T(8,128)} %param.13), channel_id=1, source_target_pairs={{0,1},{1,0},{2,3},{3,2},{4,5},{5,4},{6,7},{7,6},{8,9},{9,8},{10,11... | collective-permute-start | bytes 98312 | tf_op jit(solution)/shard_map/ppermute | solution.py:167
  14.5 8.7 %collective-permute-start.3 = (f32[4,32,128]{2,1,0:T(8,128)S(1)}, f32[4,32,128]{2,1,0:T(8,128)S(1)}, u32[]{:S(2)}, u32[]{:S(2)}) collective-permute-start(f32[4,32,128]{2,1,0:T(8,128)S(1)} %maximum_select_fusion.refs_3_), channel_id=1, source_target_pairs={{0,8},{1,3},{2,10},{3,1},{4,12},{5,7},{6,14},{7,5},{8,0},{9,11},{1... | collective-permute-start | bytes 196616 | tf_op jit(solution)/shard_map/ppermute | solution.py:164
  17.0 6.1 %collective-permute-start.4 = (f32[4,32,128]{2,1,0:T(8,128)S(1)}, f32[4,32,128]{2,1,0:T(8,128)S(1)}, u32[]{:S(2)}, u32[]{:S(2)}) collective-permute-start(f32[4,32,128]{2,1,0:T(8,128)S(1)} %maximum_select_fusion.refs_3_), channel_id=1, source_target_pairs={{0,16},{1,5},{2,18},{3,7},{4,20},{5,1},{6,22},{7,3},{8,24},{9,13},... | collective-permute-start | bytes 196616 | tf_op jit(solution)/shard_map/ppermute | solution.py:164
  18.5 5.2 %collective-permute-start.5 = (f32[4,32,128]{2,1,0:T(8,128)S(1)}, f32[4,32,128]{2,1,0:T(8,128)S(1)}, u32[]{:S(2)}, u32[]{:S(2)}) collective-permute-start(f32[4,32,128]{2,1,0:T(8,128)S(1)} %maximum_select_fusion.refs_3_), channel_id=1, source_target_pairs={{0,24},{1,7},{2,26},{3,5},{4,28},{5,3},{6,30},{7,1},{8,16},{9,15},... | collective-permute-start | bytes 196616 | tf_op jit(solution)/shard_map/ppermute | solution.py:164
  26.2 5.0 %collective-permute-start.6 = (f32[5,32,128]{2,1,0:T(8,128)S(1)}, f32[5,32,128]{2,1,0:T(8,128)S(1)}, u32[]{:S(2)}, u32[]{:S(2)}) collective-permute-start(f32[5,32,128]{2,1,0:T(8,128)S(1)} %get-tuple-element.39), channel_id=1, source_target_pairs={{0,2},{1,9},{2,0},{3,11},{4,6},{5,13},{6,4},{7,15},{8,10},{9,1},{1... | collective-permute-start | bytes 245768 | tf_op jit(solution)/shard_map/ppermute | solution.py:164
  27.8 6.6 %collective-permute-start.7 = (f32[5,32,128]{2,1,0:T(8,128)S(1)}, f32[5,32,128]{2,1,0:T(8,128)S(1)}, u32[]{:S(2)}, u32[]{:S(2)}) collective-permute-start(f32[5,32,128]{2,1,0:T(8,128)S(1)} %get-tuple-element.40), channel_id=1, source_target_pairs={{0,4},{1,17},{2,6},{3,19},{4,0},{5,21},{6,2},{7,23},{8,12},{9,25},... | collective-permute-start | bytes 245768 | tf_op jit(solution)/shard_map/ppermute | solution.py:164
  31.2 6.2 %collective-permute-start.8 = (f32[5,32,128]{2,1,0:T(8,128)S(1)}, f32[5,32,128]{2,1,0:T(8,128)S(1)}, u32[]{:S(2)}, u32[]{:S(2)}) collective-permute-start(f32[5,32,128]{2,1,0:T(8,128)S(1)} %get-tuple-element.41), channel_id=1, source_target_pairs={{0,6},{1,25},{2,4},{3,27},{4,2},{5,29},{6,0},{7,31},{8,14},{9,17},... | collective-permute-start | bytes 245768 | tf_op jit(solution)/shard_map/ppermute | solution.py:164
  39.1 4.5 %collective-permute-start.10 = (f32[5,32,128]{2,1,0:T(8,128)S(1)}, f32[5,32,128]{2,1,0:T(8,128)S(1)}, u32[]{:S(2)}, u32[]{:S(2)}) collective-permute-start(f32[5,32,128]{2,1,0:T(8,128)S(1)} %pad_maximum_fusion.refs_3_), channel_id=1, source_target_pairs={{0,8},{1,3},{2,10},{3,1},{4,12},{5,7},{6,14},{7,5},{8,0},{9,11},{1... | collective-permute-start | bytes 245768 | tf_op jit(solution)/shard_map/ppermute | solution.py:164
  39.6 4.4 %collective-permute-start.11 = (f32[5,32,128]{2,1,0:T(8,128)S(1)}, f32[5,32,128]{2,1,0:T(8,128)S(1)}, u32[]{:S(2)}, u32[]{:S(2)}) collective-permute-start(f32[5,32,128]{2,1,0:T(8,128)S(1)} %pad_maximum_fusion.refs_3_), channel_id=1, source_target_pairs={{0,16},{1,5},{2,18},{3,7},{4,20},{5,1},{6,22},{7,3},{8,24},{9,13},... | collective-permute-start | bytes 245768 | tf_op jit(solution)/shard_map/ppermute | solution.py:164
  40.1 5.3 %collective-permute-start.12 = (f32[5,32,128]{2,1,0:T(8,128)S(1)}, f32[5,32,128]{2,1,0:T(8,128)S(1)}, u32[]{:S(2)}, u32[]{:S(2)}) collective-permute-start(f32[5,32,128]{2,1,0:T(8,128)S(1)} %pad_maximum_fusion.refs_3_), channel_id=1, source_target_pairs={{0,24},{1,7},{2,26},{3,5},{4,28},{5,3},{6,30},{7,1},{8,16},{9,15},... | collective-permute-start | bytes 245768 | tf_op jit(solution)/shard_map/ppermute | solution.py:164
  47.7 4.5 %collective-permute-start.13 = (f32[5,32,128]{2,1,0:T(8,128)S(1)}, f32[5,32,128]{2,1,0:T(8,128)S(1)}, u32[]{:S(2)}, u32[]{:S(2)}) collective-permute-start(f32[5,32,128]{2,1,0:T(8,128)S(1)} %get-tuple-element.43), channel_id=1, source_target_pairs={{0,2},{1,9},{2,0},{3,11},{4,6},{5,13},{6,4},{7,15},{8,10},{9,1},{1... | collective-permute-start | bytes 245768 | tf_op jit(solution)/shard_map/ppermute | solution.py:164
  47.8 5.4 %collective-permute-start.14 = (f32[5,32,128]{2,1,0:T(8,128)S(1)}, f32[5,32,128]{2,1,0:T(8,128)S(1)}, u32[]{:S(2)}, u32[]{:S(2)}) collective-permute-start(f32[5,32,128]{2,1,0:T(8,128)S(1)} %get-tuple-element.44), channel_id=1, source_target_pairs={{0,4},{1,17},{2,6},{3,19},{4,0},{5,21},{6,2},{7,23},{8,12},{9,25},... | collective-permute-start | bytes 245768 | tf_op jit(solution)/shard_map/ppermute | solution.py:164
  50.0 6.3 %collective-permute-start.15 = (f32[5,32,128]{2,1,0:T(8,128)S(1)}, f32[5,32,128]{2,1,0:T(8,128)S(1)}, u32[]{:S(2)}, u32[]{:S(2)}) collective-permute-start(f32[5,32,128]{2,1,0:T(8,128)S(1)} %get-tuple-element.45), channel_id=1, source_target_pairs={{0,6},{1,25},{2,4},{3,27},{4,2},{5,29},{6,0},{7,31},{8,14},{9,17},... | collective-permute-start | bytes 245768 | tf_op jit(solution)/shard_map/ppermute | solution.py:164
  58.2 4.5 %collective-permute-start.17 = (f32[5,32,128]{2,1,0:T(8,128)S(1)}, f32[5,32,128]{2,1,0:T(8,128)S(1)}, u32[]{:S(2)}, u32[]{:S(2)}) collective-permute-start(f32[5,32,128]{2,1,0:T(8,128)S(1)} %pad_maximum_fusion.1.refs_3_), channel_id=1, source_target_pairs={{0,8},{1,3},{2,10},{3,1},{4,12},{5,7},{6,14},{7,5},{8,0},{9,11},{1... | collective-permute-start | bytes 245768 | tf_op jit(solution)/shard_map/ppermute | solution.py:164
  59.6 5.3 %collective-permute-start.19 = (f32[5,32,128]{2,1,0:T(8,128)S(1)}, f32[5,32,128]{2,1,0:T(8,128)S(1)}, u32[]{:S(2)}, u32[]{:S(2)}) collective-permute-start(f32[5,32,128]{2,1,0:T(8,128)S(1)} %pad_maximum_fusion.1.refs_3_), channel_id=1, source_target_pairs={{0,24},{1,7},{2,26},{3,5},{4,28},{5,3},{6,30},{7,1},{8,16},{9,15},... | collective-permute-start | bytes 245768 | tf_op jit(solution)/shard_map/ppermute | solution.py:164
  67.2 4.5 %collective-permute-start.20 = (f32[5,32,128]{2,1,0:T(8,128)S(1)}, f32[5,32,128]{2,1,0:T(8,128)S(1)}, u32[]{:S(2)}, u32[]{:S(2)}) collective-permute-start(f32[5,32,128]{2,1,0:T(8,128)S(1)} %get-tuple-element.47), channel_id=1, source_target_pairs={{0,2},{1,9},{2,0},{3,11},{4,6},{5,13},{6,4},{7,15},{8,10},{9,1},{1... | collective-permute-start | bytes 245768 | tf_op jit(solution)/shard_map/ppermute | solution.py:164
  68.1 6.5 %collective-permute-start.21 = (f32[5,32,128]{2,1,0:T(8,128)S(1)}, f32[5,32,128]{2,1,0:T(8,128)S(1)}, u32[]{:S(2)}, u32[]{:S(2)}) collective-permute-start(f32[5,32,128]{2,1,0:T(8,128)S(1)} %get-tuple-element.48), channel_id=1, source_target_pairs={{0,4},{1,17},{2,6},{3,19},{4,0},{5,21},{6,2},{7,23},{8,12},{9,25},... | collective-permute-start | bytes 245768 | tf_op jit(solution)/shard_map/ppermute | solution.py:164
  71.3 6.2 %collective-permute-start.22 = (f32[5,32,128]{2,1,0:T(8,128)S(1)}, f32[5,32,128]{2,1,0:T(8,128)S(1)}, u32[]{:S(2)}, u32[]{:S(2)}) collective-permute-start(f32[5,32,128]{2,1,0:T(8,128)S(1)} %get-tuple-element.49), channel_id=1, source_target_pairs={{0,6},{1,25},{2,4},{3,27},{4,2},{5,29},{6,0},{7,31},{8,14},{9,17},... | collective-permute-start | bytes 245768 | tf_op jit(solution)/shard_map/ppermute | solution.py:164
  79.5 5.5 %collective-permute-start.26 = (f32[32,128]{0,1:T(8,128)S(1)}, f32[32,128]{0,1:T(8,128)S(1)}, u32[]{:S(2)}, u32[]{:S(2)}) collective-permute-start(f32[32,128]{0,1:T(8,128)S(1)} %broadcast_select_fusion), channel_id=1, source_target_pairs={{0,24},{1,7},{2,26},{3,5},{4,28},{5,3},{6,30},{7,1},{8,16},{9,15},... | collective-permute-start | bytes 49160 | tf_op jit(solution)/shard_map/ppermute | solution.py:164
  85.0 4.5 %collective-permute-start.27 = (f32[32,128]{0,1:T(8,128)S(1)}, f32[32,128]{0,1:T(8,128)S(1)}, u32[]{:S(2)}, u32[]{:S(2)}) collective-permute-start(f32[32,128]{0,1:T(8,128)S(1)} %add_add_fusion.3), channel_id=1, source_target_pairs={{0,2},{1,9},{2,0},{3,11},{4,6},{5,13},{6,4},{7,15},{8,10},{9,1},{1... | collective-permute-start | bytes 49160 | tf_op jit(solution)/shard_map/ppermute | solution.py:164
  85.1 5.2 %collective-permute-start.28 = (f32[32,128]{0,1:T(8,128)S(1)}, f32[32,128]{0,1:T(8,128)S(1)}, u32[]{:S(2)}, u32[]{:S(2)}) collective-permute-start(f32[32,128]{0,1:T(8,128)S(1)} %add_add_fusion.3), channel_id=1, source_target_pairs={{0,4},{1,17},{2,6},{3,19},{4,0},{5,21},{6,2},{7,23},{8,12},{9,25},... | collective-permute-start | bytes 49160 | tf_op jit(solution)/shard_map/ppermute | solution.py:164
  87.1 6.1 %collective-permute-start.29 = (f32[32,128]{0,1:T(8,128)S(1)}, f32[32,128]{0,1:T(8,128)S(1)}, u32[]{:S(2)}, u32[]{:S(2)}) collective-permute-start(f32[32,128]{0,1:T(8,128)S(1)} %add_add_fusion.3), channel_id=1, source_target_pairs={{0,6},{1,25},{2,4},{3,27},{4,2},{5,29},{6,0},{7,31},{8,14},{9,17},... | collective-permute-start | bytes 49160 | tf_op jit(solution)/shard_map/ppermute | solution.py:164
  (9 other events, 40.7 us)

commit v2 on v1

--- a/solution.py
+++ b/solution.py
@@ -13,49 +13,101 @@
 GROUP = 8
 
 
-def split_kernel(meta_ref, values_ref, out_ref):
-    first = pl.program_id(0) * values_ref.shape[0]
-    size = values_ref.shape[1]
+def core_here():
+    return lax.rem(lax.axis_index("col").astype(jnp.int32), 2)
+
+
+def places_kernel(seg, index_ref, count_ref, raw_ref, out_ref, raw_out_ref):
+    raw_out_ref[...] = raw_ref[...]
+    row = lax.axis_index("row").astype(jnp.int32)
+    col = lax.axis_index("col").astype(jnp.int32)
+    line, core = lax.div(col, 2), lax.rem(col, 2)
+    per = 2 * seg
+    seg_bits, per_bits = seg.bit_length() - 1, per.bit_length() - 1
+    u = index_ref[0, 0, 0:1]
+    v = index_ref[0, 0, 1:2]
+    out_ref[0:1] = ((u >> per_bits) ^ line) * per + (u & (per - 1))
+    out_ref[1:2] = ((v >> seg_bits) ^ row) * per + core * seg + (v & (seg - 1))
+    out_ref[2:3] = jnp.zeros_like(u) + count_ref[0, 0]
+
+
+def find_places(block_index, block_count, raw):
+    return pl.pallas_call(
+        functools.partial(places_kernel, raw.shape[0]),
+        in_specs=[VMEM, SMEM, VMEM],
+        out_specs=[VMEM, VMEM],
+        out_shape=[
+            pltpu.VMEM((3, block_index.shape[3]), jnp.int32),
+            pltpu.VMEM(raw.shape, F32),
+        ],
+    )(block_index, block_count, raw)
+
+
+def split_kernel(own_places, other_places, own_hbm, other_in, own_out, other_out, own_in, sems):
+    slots, size, _ = own_in.shape
+    core = core_here()
+    copies = []
+    for chunk in range(slots // GROUP):
+        cut = pl.ds(chunk * GROUP, GROUP)
+        copies.append(pltpu.make_async_copy(own_hbm.at[cut], own_in.at[cut], sems.at[chunk]))
+    for copy in copies:
+        copy.start()
 
     def write(turn):
-        for slot in range(values_ref.shape[0]):
-            block = values_ref[slot]
-            block = jnp.where(first + slot < meta_ref[1], block, 0.0)
-            block = block.T if turn else block
-            high = block.astype(BF)
-            out_ref[slot, :size] = high
-            out_ref[slot, size:] = (block - high.astype(F32)).astype(BF)
-
-    @pl.when(meta_ref[0] == 0)
+        def sweep(places, source, target, chunk):
+            @pl.when(chunk * GROUP < places[2, 0])
+            def _():
+                for i in range(GROUP):
+                    slot = chunk * GROUP + i
+                    block = jnp.where(slot < places[2, 0], source[slot], 0.0)
+                    block = block.T if turn else block
+                    high = block.astype(BF)
+                    target[slot, :size] = high
+                    target[slot, size:] = (block - high.astype(F32)).astype(BF)
+
+        for chunk in range(slots // GROUP):
+            sweep(other_places, other_in, other_out, chunk)
+        for chunk in range(slots // GROUP):
+            copies[chunk].wait()
+            sweep(own_places, own_in, own_out, chunk)
+
+    @pl.when(core == 0)
     def _():
         write(True)
 
-    @pl.when(meta_ref[0] != 0)
+    @pl.when(core != 0)
     def _():
         write(False)
 
 
-def split_blocks(values, core, count):
+def split_blocks(places, places_other, values, values_other):
     slots, size, _ = values.shape
-    step = GROUP
     return pl.pallas_call(
         split_kernel,
-        grid=(slots // step,),
-        in_specs=[SMEM, pl.BlockSpec((step, size, size), lambda i: (i, 0, 0))],
-        out_specs=pl.BlockSpec((step, 2 * size, size), lambda i: (i, 0, 0)),
-        out_shape=jax.ShapeDtypeStruct((slots, 2 * size, size), BF),
+        in_specs=[SMEM, SMEM, pl.BlockSpec(memory_space=pltpu.HBM), VMEM],
+        out_specs=[VMEM, VMEM],
+        out_shape=[pltpu.VMEM((slots, 2 * size, size), BF)] * 2,
+        scratch_shapes=[
+            pltpu.VMEM((slots, size, size), F32),
+            pltpu.SemaphoreType.DMA((slots // GROUP,)),
+        ],
         compiler_params=pltpu.CompilerParams(vmem_limit_bytes=32 * 2**20),
         cost_estimate=pl.CostEstimate(
-            flops=slots * size * size * 4, bytes_accessed=slots * size * size * 8, transcendentals=0
+            flops=slots * size * size * 8, bytes_accessed=slots * size * size * 16, transcendentals=0
         ),
-    )(jnp.stack([core, count]), values)
+    )(
+        places,
+        places_other,
+        pltpu.with_memory_space_constraint(values, pltpu.HBM),
+        pltpu.with_memory_space_constraint(values_other, pltpu.VMEM),
+    )
 
 
 def apply_kernel(parts, with_degree, with_aux, *refs):
-    meta_ref, own_ref, other_ref = refs[:3]
-    fields = refs[3 : 3 + parts]
-    outs = refs[3 + parts : 3 + 2 * parts]
-    stack_ref, sum_ref = refs[3 + 2 * parts :]
+    own_places, other_places, own_ref, other_ref = refs[:4]
+    fields = refs[4 : 4 + parts]
+    outs = refs[4 + parts : 4 + 2 * parts]
+    stack_ref, sum_ref = refs[4 + 2 * parts :]
     per = outs[0].shape[0] - 1
     width, size = fields[0].shape[1:]
     for part in range(parts):
@@ -71,22 +123,24 @@
             if with_degree:
                 stack_ref[f, 2 * width :, :] = jnp.ones((16, 2 * size), BF)
     sum_ref[...] = jnp.zeros_like(sum_ref)
-    slots = own_ref.shape[0]
-
-    def sweep(values_ref, base, count):
+    core = core_here()
+
+    def sweep(values_ref, places):
+        count = places[2, 0]
+
         def group(g, carry):
             products = []
             for i in range(GROUP):
                 q = g * GROUP + i
                 products.append(
                     jnp.dot(
-                        stack_ref[meta_ref[0, base + q]],
+                        stack_ref[places[1 - core, q]],
                         values_ref[q],
                         preferred_element_type=F32,
                     )
                 )
             for i in range(GROUP):
-                to = meta_ref[1, base + g * GROUP + i]
+                to = places[core, g * GROUP + i]
                 whole = products[i]
                 sum_ref[to, :width] += whole[:width] + whole[width : 2 * width]
                 if with_degree:
@@ -95,8 +149,8 @@
 
         lax.fori_loop(0, (count + GROUP - 1) // GROUP, group, 0)
 
-    sweep(own_ref, 0, meta_ref[2, 0])
-    sweep(other_ref, slots, meta_ref[2, 1])
+    sweep(own_ref, own_places)
+    sweep(other_ref, other_places)
     if with_aux:
         aux = fields[0][per]
         for part in range(1, parts):
@@ -112,16 +166,16 @@
                 outs[part][per, j : j + 1, :] = sum_ref[part * per + j, width : width + 1]
 
 
-def apply_blocks(meta, own, other, fields, with_degree, with_aux):
+def apply_blocks(matrix, fields, with_degree, with_aux):
     parts = len(fields)
     width, size = fields[0].shape[1:]
     per = fields[0].shape[0] - (1 if with_aux else 0)
     rows = 2 * width + (16 if with_degree else 0)
     sums = width + (8 if with_degree else 0)
-    slots = own.shape[0]
+    slots = matrix[2].shape[0]
     return pl.pallas_call(
         functools.partial(apply_kernel, parts, with_degree, with_aux),
-        in_specs=[SMEM] + [VMEM] * (2 + parts),
+        in_specs=[SMEM] * 2 + [VMEM] * (2 + parts),
         out_specs=[VMEM] * parts,
         out_shape=[jax.ShapeDtypeStruct((per + 1, width, size), F32)] * parts,
         scratch_shapes=[
@@ -134,7 +188,7 @@
             bytes_accessed=4 * slots * size * size * 2,
             transcendentals=0,
         ),
-    )(meta, own, other, *fields)
+    )(*matrix, *fields)
 
 
 def dots(*pairs):
@@ -174,42 +228,27 @@
 
     def shards(block_values, block_index, block_count, strength, raw_scores):
         values = block_values[0, 0]
-        index = block_index[0, 0]
-        count = block_count[0, 0]
-        row = lax.axis_index("row").astype(jnp.int32)
-        col = lax.axis_index("col").astype(jnp.int32)
-        line, core = col // 2, col % 2
+        core = core_here()
         seg = raw_scores.shape[0]
         per = 2 * seg
         raw_other = swap(raw_scores)
-        ints = jnp.concatenate([index, jnp.full((1, index.shape[1]), count, jnp.int32)], axis=0)
-        ints_other = swap(ints)
-        values_other = swap(values)
-
-        def places(pair, home):
-            row_place = ((pair[0] // per) ^ line) * per + pair[0] % per
-            col_place = ((pair[1] // seg) ^ row) * per + home * seg + pair[1] % seg
-            return jnp.where(
-                core == 0, jnp.stack([col_place, row_place]), jnp.stack([row_place, col_place])
-            )
-
-        counts = jnp.zeros((1, 2 * index.shape[1]), jnp.int32)
-        counts = counts.at[0, 0].set(count).at[0, 1].set(ints_other[2, 0])
-        meta = jnp.concatenate(
-            [jnp.concatenate([places(index, core), places(ints_other, 1 - core)], axis=1), counts],
-            axis=0,
-        )
+        places, raw_own = find_places(block_index, block_count, raw_scores)
+        raw_other, raw_own, later_values = lax.optimization_barrier((raw_other, raw_own, values))
+        values_other = swap(later_values)
         raw = jnp.where(
             core == 0,
-            jnp.concatenate([raw_scores, raw_other]),
-            jnp.concatenate([raw_other, raw_scores]),
-        )
+            jnp.concatenate([raw_own, raw_other]),
+            jnp.concatenate([raw_other, raw_own]),
+        )
+        places_other = swap(places)
         gains = strength[None, :, None]
         gathered = gather(raw)
-        own = split_blocks(values, core, count)
-        other = split_blocks(values_other, core, ints_other[2, 0])
-
-        mine = collect(apply_blocks(meta, own, other, gathered, True, False))
+        values, values_other = lax.optimization_barrier((values, values_other))
+        matrix = (places, places_other) + tuple(
+            split_blocks(places, places_other, values, values_other)
+        )
+
+        mine = collect(apply_blocks(matrix, gathered, True, False))
         both = mine + swap(mine)
         degree = both[per, :per, None, :]
         w0 = raw + gains * (degree * raw - both[:per])
@@ -218,7 +257,7 @@
             return jnp.concatenate([field, dots(*pairs)[None]])
 
         mine = collect(
-            apply_blocks(meta, own, other, gather(with_aux(w0, (raw, raw), (raw, w0))), False, True)
+            apply_blocks(matrix, gather(with_aux(w0, (raw, raw), (raw, w0))), False, True)
         )
         sums = mine[per]
         product = mine[:per] + swap(mine[:per])
@@ -243,7 +282,7 @@
             (w1, q0),
             (w0, q0),
         )
-        mine = collect(apply_blocks(meta, own, other, gather(with_aux(h, *pairs)), False, True))
+        mine = collect(apply_blocks(matrix, gather(with_aux(h, *pairs)), False, True))
         sums = mine[per]
         product = mine[:per] + swap(mine[:per])
         qh = h + gains * (degree * h - product)

time: 94.1 us -> 80.7 us (0.86)
  other arithmetic: 7.54 us -> 2.13 us
  local copies, waits for them, and re-layouts: 5.5 us -> 0.59 us
  Pallas kernels: 12.6 us -> 10.4 us
    another operation x5 -> x0, other arithmetic: 4.52 us -> none
    pallas_call x2, Pallas kernels: 5.6 us -> 3.32 us  [the longest x1 2.53 us: split_blocks(): pl.pallas_call(split_kernel, in_specs=[SMEM, SMEM, pl.BlockSpec(memory_sp...]
    unnamed x6 -> x2, local copies, waits for them, and re-layouts: 1.75 us -> 0.01 us
    scatter x2 -> x0, local copies, waits for them, and re-layouts: 1.31 us -> none  [shards(): counts = counts.at[0, 0].set(count).at[0, 1].set(ints_other[2, 0])]
  transfers between devices with their start and end apart: 30 -> 30, of which waited for: 22 -> 25; matrix products, arithmetic and copies ran while one was open for 10% -> 1% of each run, Pallas kernels for 6% -> 4%
where the time goes in v2:
time: 80.7 us; the launch traced here: 80.5 us
  starting transfers between devices  34 us (42%)
  waiting for transfers between devices  31.8 us (39%)
  Pallas kernels  10.4 us (13%)
  other arithmetic  2.13 us (3%)
  between operations  1.57 us (2%)
    ppermute x24, starting transfers between devices, joint(): return lax.ppermute(array, ('row', 'col'), pairs)  32.7 us
    ppermute x24, waiting for transfers between devices, joint(): return lax.ppermute(array, ('row', 'col'), pairs)  27.9 us
    pallas_call x3, Pallas kernels, apply_blocks(): pl.pallas_call(functools.partial(apply_kernel, parts, with_degree, with_a...  7.07 us
    ppermute x6, waiting for transfers between devices, swap(): return lax.ppermute(array, 'col', [(c, c ^ 1) for c in range(n_col)])  3.88 us
    pallas_call x1, Pallas kernels, split_blocks(): pl.pallas_call(split_kernel, in_specs=[SMEM, SMEM, pl.BlockSpec(memory_sp...  2.53 us
  transfers between devices with their start and end apart: 30, of which 25 were waited for; matrix products, arithmetic and copies ran while one was open for 1% of the time, Pallas kernels for 4%

profile of v2, /device:TPU:0, one launch (start us, length us, event | category | flops | bytes accessed | tf_op | source)
XLA Modules:
  0.0 80.5 jit_solution(15520631776420198306)
XLA Ops:
  3.3 2.6 %collective-permute-start.3 = (f32[4,32,128]{2,1,0:T(8,128)S(1)}, f32[4,32,128]{2,1,0:T(8,128)S(1)}, u32[]{:S(2)}, u32[]{:S(2)}) collective-permute-start(f32[4,32,128]{2,1,0:T(8,128)S(1)} %maximum_select_fusion.refs_4_), channel_id=1, source_target_pairs={{0,8},{1,3},{2,10},{3,1},{4,12},{5,7},{6,14},{7,5},{8,0},{9,11},{1... | collective-permute-start | bytes 196616 | tf_op jit(solution)/shard_map/ppermute | solution.py:218
  7.8 2.5 %shard_map.69 = (bf16[40,256,128]{2,1,0:T(8,128)(2,1)S(1)}, bf16[40,256,128]{2,1,0:T(8,128)(2,1)S(1)}) custom-call(s32[3,40]{1,0:T(4,128)S(1)} %get-tuple-element.23.own_places.refs_0_, s32[3,40]{1,0:T(4,128)S(1)} %collective-permute-done.other_places.refs_1_, f32[40,128,128]{2,1,0:T(8,128)} %bitcast.12, f32[40,128,128]{2,1,0:T(8,128)S(1)} %collective-permute-done.2.other_in), custom_call_target="tpu_custom_call" | custom-call | flops 5242880 | bytes 10485760 | tf_op jit(solution)/shard_map/pallas_call | solution.py:85
  10.4 2.2 %collective-permute-done.5.refs_7_ = f32[4,32,128]{2,1,0:T(8,128)S(1)} collective-permute-done((f32[4,32,128]{2,1,0:T(8,128)S(1)}, f32[4,32,128]{2,1,0:T(8,128)S(1)}, u32[]{:S(2)}, u32[]{:S(2)}) %collective-permute-start.5) | collective-permute-done | bytes 65568 | tf_op jit(solution)/shard_map/ppermute | solution.py:218
  12.6 2.5 %shard_map.70 = (f32[5,32,128]{2,1,0:T(8,128)S(1)}, f32[5,32,128]{2,1,0:T(8,128)S(1)}, f32[5,32,128]{2,1,0:T(8,128)S(1)}, f32[5,32,128]{2,1,0:T(8,128)S(1)}) custom-call(s32[3,40]{1,0:T(4,128)S(1)} %get-tuple-element.23.own_places.refs_0_, s32[3,40]{1,0:T(4,128)S(1)} %collective-permute-done.other_places.refs_1_, ...), custom_call_target="tpu_custom_call" | custom-call | flops 419430400 | bytes 5242880 | tf_op jit(solution)/shard_map/pallas_call | solution.py:176
  15.1 3.9 %collective-permute-start.8 = (f32[5,32,128]{2,1,0:T(8,128)S(1)}, f32[5,32,128]{2,1,0:T(8,128)S(1)}, u32[]{:S(2)}, u32[]{:S(2)}) collective-permute-start(f32[5,32,128]{2,1,0:T(8,128)S(1)} %get-tuple-element.35), channel_id=1, source_target_pairs={{0,6},{1,25},{2,4},{3,27},{4,2},{5,29},{6,0},{7,31},{8,14},{9,17},... | collective-permute-start | bytes 245768 | tf_op jit(solution)/shard_map/ppermute | solution.py:218
  19.6 1.9 %collective-permute-done.8 = f32[5,32,128]{2,1,0:T(8,128)S(1)} collective-permute-done((f32[5,32,128]{2,1,0:T(8,128)S(1)}, f32[5,32,128]{2,1,0:T(8,128)S(1)}, u32[]{:S(2)}, u32[]{:S(2)}) %collective-permute-start.8) | collective-permute-done | bytes 81952 | tf_op jit(solution)/shard_map/ppermute | solution.py:218
  21.5 1.9 %collective-permute-done.6 = f32[5,32,128]{2,1,0:T(8,128)S(1)} collective-permute-done((f32[5,32,128]{2,1,0:T(8,128)S(1)}, f32[5,32,128]{2,1,0:T(8,128)S(1)}, u32[]{:S(2)}, u32[]{:S(2)}) %collective-permute-start.6) | collective-permute-done | bytes 81952 | tf_op jit(solution)/shard_map/ppermute | solution.py:218
  26.4 3.2 %collective-permute-start.12 = (f32[5,32,128]{2,1,0:T(8,128)S(1)}, f32[5,32,128]{2,1,0:T(8,128)S(1)}, u32[]{:S(2)}, u32[]{:S(2)}) collective-permute-start(f32[5,32,128]{2,1,0:T(8,128)S(1)} %pad_maximum_fusion.refs_4_), channel_id=1, source_target_pairs={{0,24},{1,7},{2,26},{3,5},{4,28},{5,3},{6,30},{7,1},{8,16},{9,15},... | collective-permute-start | bytes 245768 | tf_op jit(solution)/shard_map/ppermute | solution.py:218
  32.0 2.3 %shard_map.71 = (f32[5,32,128]{2,1,0:T(8,128)S(1)}, f32[5,32,128]{2,1,0:T(8,128)S(1)}, f32[5,32,128]{2,1,0:T(8,128)S(1)}, f32[5,32,128]{2,1,0:T(8,128)S(1)}) custom-call(s32[3,40]{1,0:T(4,128)S(1)} %get-tuple-element.23.own_places.refs_0_, s32[3,40]{1,0:T(4,128)S(1)} %collective-permute-done.other_places.refs_1_, ...), custom_call_target="tpu_custom_call" | custom-call | flops 335544320 | bytes 5242880 | tf_op jit(solution)/shard_map/pallas_call | solution.py:176
  34.3 2.1 %collective-permute-start.15 = (f32[5,32,128]{2,1,0:T(8,128)S(1)}, f32[5,32,128]{2,1,0:T(8,128)S(1)}, u32[]{:S(2)}, u32[]{:S(2)}) collective-permute-start(f32[5,32,128]{2,1,0:T(8,128)S(1)} %get-tuple-element.39), channel_id=1, source_target_pairs={{0,6},{1,25},{2,4},{3,27},{4,2},{5,29},{6,0},{7,31},{8,14},{9,17},... | collective-permute-start | bytes 245768 | tf_op jit(solution)/shard_map/ppermute | solution.py:218
  37.1 1.6 %collective-permute-start.14 = (f32[5,32,128]{2,1,0:T(8,128)S(1)}, f32[5,32,128]{2,1,0:T(8,128)S(1)}, u32[]{:S(2)}, u32[]{:S(2)}) collective-permute-start(f32[5,32,128]{2,1,0:T(8,128)S(1)} %get-tuple-element.38), channel_id=1, source_target_pairs={{0,4},{1,17},{2,6},{3,19},{4,0},{5,21},{6,2},{7,23},{8,12},{9,25},... | collective-permute-start | bytes 245768 | tf_op jit(solution)/shard_map/ppermute | solution.py:218
  38.8 2.0 %collective-permute-done.15 = f32[5,32,128]{2,1,0:T(8,128)S(1)} collective-permute-done((f32[5,32,128]{2,1,0:T(8,128)S(1)}, f32[5,32,128]{2,1,0:T(8,128)S(1)}, u32[]{:S(2)}, u32[]{:S(2)}) %collective-permute-start.15) | collective-permute-done | bytes 81952 | tf_op jit(solution)/shard_map/ppermute | solution.py:218
  41.6 1.8 %collective-permute-done.14 = f32[5,32,128]{2,1,0:T(8,128)S(1)} collective-permute-done((f32[5,32,128]{2,1,0:T(8,128)S(1)}, f32[5,32,128]{2,1,0:T(8,128)S(1)}, u32[]{:S(2)}, u32[]{:S(2)}) %collective-permute-start.14) | collective-permute-done | bytes 81952 | tf_op jit(solution)/shard_map/ppermute | solution.py:218
  46.7 2.1 %collective-permute-start.19 = (f32[5,32,128]{2,1,0:T(8,128)S(1)}, f32[5,32,128]{2,1,0:T(8,128)S(1)}, u32[]{:S(2)}, u32[]{:S(2)}) collective-permute-start(f32[5,32,128]{2,1,0:T(8,128)S(1)} %pad_maximum_fusion.1.refs_4_), channel_id=1, source_target_pairs={{0,24},{1,7},{2,26},{3,5},{4,28},{5,3},{6,30},{7,1},{8,16},{9,15},... | collective-permute-start | bytes 245768 | tf_op jit(solution)/shard_map/ppermute | solution.py:218
  49.8 2.2 %collective-permute-done.19.refs_7_ = f32[5,32,128]{2,1,0:T(8,128)S(1)} collective-permute-done((f32[5,32,128]{2,1,0:T(8,128)S(1)}, f32[5,32,128]{2,1,0:T(8,128)S(1)}, u32[]{:S(2)}, u32[]{:S(2)}) %collective-permute-start.19) | collective-permute-done | bytes 81952 | tf_op jit(solution)/shard_map/ppermute | solution.py:218
  52.0 2.3 %shard_map.72 = (f32[5,32,128]{2,1,0:T(8,128)S(1)}, f32[5,32,128]{2,1,0:T(8,128)S(1)}, f32[5,32,128]{2,1,0:T(8,128)S(1)}, f32[5,32,128]{2,1,0:T(8,128)S(1)}) custom-call(s32[3,40]{1,0:T(4,128)S(1)} %get-tuple-element.23.own_places.refs_0_, s32[3,40]{1,0:T(4,128)S(1)} %collective-permute-done.other_places.refs_1_, ...), custom_call_target="tpu_custom_call" | custom-call | flops 335544320 | bytes 5242880 | tf_op jit(solution)/shard_map/pallas_call | solution.py:176
  54.3 3.5 %collective-permute-start.22 = (f32[5,32,128]{2,1,0:T(8,128)S(1)}, f32[5,32,128]{2,1,0:T(8,128)S(1)}, u32[]{:S(2)}, u32[]{:S(2)}) collective-permute-start(f32[5,32,128]{2,1,0:T(8,128)S(1)} %get-tuple-element.43), channel_id=1, source_target_pairs={{0,6},{1,25},{2,4},{3,27},{4,2},{5,29},{6,0},{7,31},{8,14},{9,17},... | collective-permute-start | bytes 245768 | tf_op jit(solution)/shard_map/ppermute | solution.py:218
  58.8 1.9 %collective-permute-done.22 = f32[5,32,128]{2,1,0:T(8,128)S(1)} collective-permute-done((f32[5,32,128]{2,1,0:T(8,128)S(1)}, f32[5,32,128]{2,1,0:T(8,128)S(1)}, u32[]{:S(2)}, u32[]{:S(2)}) %collective-permute-start.22) | collective-permute-done | bytes 81952 | tf_op jit(solution)/shard_map/ppermute | solution.py:218
  60.6 1.6 %collective-permute-done.20 = f32[5,32,128]{2,1,0:T(8,128)S(1)} collective-permute-done((f32[5,32,128]{2,1,0:T(8,128)S(1)}, f32[5,32,128]{2,1,0:T(8,128)S(1)}, u32[]{:S(2)}, u32[]{:S(2)}) %collective-permute-start.20) | collective-permute-done | bytes 81952 | tf_op jit(solution)/shard_map/ppermute | solution.py:218
  65.1 1.7 %collective-permute-start.25 = (f32[32,128]{0,1:T(8,128)S(1)}, f32[32,128]{0,1:T(8,128)S(1)}, u32[]{:S(2)}, u32[]{:S(2)}) collective-permute-start(f32[32,128]{0,1:T(8,128)S(1)} %broadcast_select_fusion), channel_id=1, source_target_pairs={{0,16},{1,5},{2,18},{3,7},{4,20},{5,1},{6,22},{7,3},{8,24},{9,13},... | collective-permute-start | bytes 49160 | tf_op jit(solution)/shard_map/ppermute | solution.py:218
  71.2 1.8 %collective-permute-start.29 = (f32[32,128]{0,1:T(8,128)S(1)}, f32[32,128]{0,1:T(8,128)S(1)}, u32[]{:S(2)}, u32[]{:S(2)}) collective-permute-start(f32[32,128]{0,1:T(8,128)S(1)} %add_add_fusion.3), channel_id=1, source_target_pairs={{0,6},{1,25},{2,4},{3,27},{4,2},{5,29},{6,0},{7,31},{8,14},{9,17},... | collective-permute-start | bytes 49160 | tf_op jit(solution)/shard_map/ppermute | solution.py:218
  73.0 1.7 %collective-permute-start.28 = (f32[32,128]{0,1:T(8,128)S(1)}, f32[32,128]{0,1:T(8,128)S(1)}, u32[]{:S(2)}, u32[]{:S(2)}) collective-permute-start(f32[32,128]{0,1:T(8,128)S(1)} %add_add_fusion.3), channel_id=1, source_target_pairs={{0,4},{1,17},{2,6},{3,19},{4,0},{5,21},{6,2},{7,23},{8,12},{9,25},... | collective-permute-start | bytes 49160 | tf_op jit(solution)/shard_map/ppermute | solution.py:218
  75.6 1.8 %collective-permute-done.29 = f32[32,128]{0,1:T(8,128)S(1)} collective-permute-done((f32[32,128]{0,1:T(8,128)S(1)}, f32[32,128]{0,1:T(8,128)S(1)}, u32[]{:S(2)}, u32[]{:S(2)}) %collective-permute-start.29) | collective-permute-done | bytes 16416 | tf_op jit(solution)/shard_map/ppermute | solution.py:218
  77.4 1.8 %collective-permute-done.28 = f32[32,128]{0,1:T(8,128)S(1)} collective-permute-done((f32[32,128]{0,1:T(8,128)S(1)}, f32[32,128]{0,1:T(8,128)S(1)}, u32[]{:S(2)}, u32[]{:S(2)}) %collective-permute-start.28) | collective-permute-done | bytes 16416 | tf_op jit(solution)/shard_map/ppermute | solution.py:218
  (81 shorter events, 26.0 us)
Async XLA Ops:
  2.6 5.2 %collective-permute-start.2 = (f32[40,128,128]{2,1,0:T(8,128)}, f32[40,128,128]{2,1,0:T(8,128)S(1)}, u32[]{:S(2)}, u32[]{:S(2)}) collective-permute-start(f32[40,128,128]{2,1,0:T(8,128)} %bitcast.11), channel_id=1, source_target_pairs={{0,1},{1,0},{2,3},{3,2},{4,5},{5,4},{6,7},{7,6},{8,9},{9,8},{10,11... | collective-permute-start | bytes 7864328 | tf_op jit(solution)/shard_map/ppermute | solution.py:221
  2.7 5.1 %collective-permute-start = (s32[3,40]{1,0:T(4,128)S(1)}, s32[3,40]{1,0:T(4,128)S(1)}, u32[]{:S(2)}, u32[]{:S(2)}) collective-permute-start(s32[3,40]{1,0:T(4,128)S(1)} %get-tuple-element.23.own_places.refs_0_), channel_id=1, source_target_pairs={{0,1},{1,0},{2,3},{3,2},{4,5},{5,4},{6,7},{7,6},{8,9},{9,8},{10,11... | collective-permute-start | bytes 1448 | tf_op jit(solution)/shard_map/ppermute | solution.py:221
  3.3 7.1 %collective-permute-start.3 = (f32[4,32,128]{2,1,0:T(8,128)S(1)}, f32[4,32,128]{2,1,0:T(8,128)S(1)}, u32[]{:S(2)}, u32[]{:S(2)}) collective-permute-start(f32[4,32,128]{2,1,0:T(8,128)S(1)} %maximum_select_fusion.refs_4_), channel_id=1, source_target_pairs={{0,8},{1,3},{2,10},{3,1},{4,12},{5,7},{6,14},{7,5},{8,0},{9,11},{1... | collective-permute-start | bytes 196616 | tf_op jit(solution)/shard_map/ppermute | solution.py:218
  5.9 4.4 %collective-permute-start.4 = (f32[4,32,128]{2,1,0:T(8,128)S(1)}, f32[4,32,128]{2,1,0:T(8,128)S(1)}, u32[]{:S(2)}, u32[]{:S(2)}) collective-permute-start(f32[4,32,128]{2,1,0:T(8,128)S(1)} %maximum_select_fusion.refs_4_), channel_id=1, source_target_pairs={{0,16},{1,5},{2,18},{3,7},{4,20},{5,1},{6,22},{7,3},{8,24},{9,13},... | collective-permute-start | bytes 196616 | tf_op jit(solution)/shard_map/ppermute | solution.py:218
  7.4 5.2 %collective-permute-start.5 = (f32[4,32,128]{2,1,0:T(8,128)S(1)}, f32[4,32,128]{2,1,0:T(8,128)S(1)}, u32[]{:S(2)}, u32[]{:S(2)}) collective-permute-start(f32[4,32,128]{2,1,0:T(8,128)S(1)} %maximum_select_fusion.refs_4_), channel_id=1, source_target_pairs={{0,24},{1,7},{2,26},{3,5},{4,28},{5,3},{6,30},{7,1},{8,16},{9,15},... | collective-permute-start | bytes 196616 | tf_op jit(solution)/shard_map/ppermute | solution.py:218
  15.1 6.4 %collective-permute-start.8 = (f32[5,32,128]{2,1,0:T(8,128)S(1)}, f32[5,32,128]{2,1,0:T(8,128)S(1)}, u32[]{:S(2)}, u32[]{:S(2)}) collective-permute-start(f32[5,32,128]{2,1,0:T(8,128)S(1)} %get-tuple-element.35), channel_id=1, source_target_pairs={{0,6},{1,25},{2,4},{3,27},{4,2},{5,29},{6,0},{7,31},{8,14},{9,17},... | collective-permute-start | bytes 245768 | tf_op jit(solution)/shard_map/ppermute | solution.py:218
  19.0 4.4 %collective-permute-start.6 = (f32[5,32,128]{2,1,0:T(8,128)S(1)}, f32[5,32,128]{2,1,0:T(8,128)S(1)}, u32[]{:S(2)}, u32[]{:S(2)}) collective-permute-start(f32[5,32,128]{2,1,0:T(8,128)S(1)} %get-tuple-element.33), channel_id=1, source_target_pairs={{0,2},{1,9},{2,0},{3,11},{4,6},{5,13},{6,4},{7,15},{8,10},{9,1},{1... | collective-permute-start | bytes 245768 | tf_op jit(solution)/shard_map/ppermute | solution.py:218
  19.0 5.3 %collective-permute-start.7 = (f32[5,32,128]{2,1,0:T(8,128)S(1)}, f32[5,32,128]{2,1,0:T(8,128)S(1)}, u32[]{:S(2)}, u32[]{:S(2)}) collective-permute-start(f32[5,32,128]{2,1,0:T(8,128)S(1)} %get-tuple-element.34), channel_id=1, source_target_pairs={{0,4},{1,17},{2,6},{3,19},{4,0},{5,21},{6,2},{7,23},{8,12},{9,25},... | collective-permute-start | bytes 245768 | tf_op jit(solution)/shard_map/ppermute | solution.py:218
  26.0 4.5 %collective-permute-start.10 = (f32[5,32,128]{2,1,0:T(8,128)S(1)}, f32[5,32,128]{2,1,0:T(8,128)S(1)}, u32[]{:S(2)}, u32[]{:S(2)}) collective-permute-start(f32[5,32,128]{2,1,0:T(8,128)S(1)} %pad_maximum_fusion.refs_4_), channel_id=1, source_target_pairs={{0,8},{1,3},{2,10},{3,1},{4,12},{5,7},{6,14},{7,5},{8,0},{9,11},{1... | collective-permute-start | bytes 245768 | tf_op jit(solution)/shard_map/ppermute | solution.py:218
  26.4 4.4 %collective-permute-start.11 = (f32[5,32,128]{2,1,0:T(8,128)S(1)}, f32[5,32,128]{2,1,0:T(8,128)S(1)}, u32[]{:S(2)}, u32[]{:S(2)}) collective-permute-start(f32[5,32,128]{2,1,0:T(8,128)S(1)} %pad_maximum_fusion.refs_4_), channel_id=1, source_target_pairs={{0,16},{1,5},{2,18},{3,7},{4,20},{5,1},{6,22},{7,3},{8,24},{9,13},... | collective-permute-start | bytes 245768 | tf_op jit(solution)/shard_map/ppermute | solution.py:218
  26.4 5.6 %collective-permute-start.12 = (f32[5,32,128]{2,1,0:T(8,128)S(1)}, f32[5,32,128]{2,1,0:T(8,128)S(1)}, u32[]{:S(2)}, u32[]{:S(2)}) collective-permute-start(f32[5,32,128]{2,1,0:T(8,128)S(1)} %pad_maximum_fusion.refs_4_), channel_id=1, source_target_pairs={{0,24},{1,7},{2,26},{3,5},{4,28},{5,3},{6,30},{7,1},{8,16},{9,15},... | collective-permute-start | bytes 245768 | tf_op jit(solution)/shard_map/ppermute | solution.py:218
  34.3 6.5 %collective-permute-start.15 = (f32[5,32,128]{2,1,0:T(8,128)S(1)}, f32[5,32,128]{2,1,0:T(8,128)S(1)}, u32[]{:S(2)}, u32[]{:S(2)}) collective-permute-start(f32[5,32,128]{2,1,0:T(8,128)S(1)} %get-tuple-element.39), channel_id=1, source_target_pairs={{0,6},{1,25},{2,4},{3,27},{4,2},{5,29},{6,0},{7,31},{8,14},{9,17},... | collective-permute-start | bytes 245768 | tf_op jit(solution)/shard_map/ppermute | solution.py:218
  36.4 5.2 %collective-permute-start.13 = (f32[5,32,128]{2,1,0:T(8,128)S(1)}, f32[5,32,128]{2,1,0:T(8,128)S(1)}, u32[]{:S(2)}, u32[]{:S(2)}) collective-permute-start(f32[5,32,128]{2,1,0:T(8,128)S(1)} %get-tuple-element.37), channel_id=1, source_target_pairs={{0,2},{1,9},{2,0},{3,11},{4,6},{5,13},{6,4},{7,15},{8,10},{9,1},{1... | collective-permute-start | bytes 245768 | tf_op jit(solution)/shard_map/ppermute | solution.py:218
  37.1 6.2 %collective-permute-start.14 = (f32[5,32,128]{2,1,0:T(8,128)S(1)}, f32[5,32,128]{2,1,0:T(8,128)S(1)}, u32[]{:S(2)}, u32[]{:S(2)}) collective-permute-start(f32[5,32,128]{2,1,0:T(8,128)S(1)} %get-tuple-element.38), channel_id=1, source_target_pairs={{0,4},{1,17},{2,6},{3,19},{4,0},{5,21},{6,2},{7,23},{8,12},{9,25},... | collective-permute-start | bytes 245768 | tf_op jit(solution)/shard_map/ppermute | solution.py:218
  45.2 4.5 %collective-permute-start.17 = (f32[5,32,128]{2,1,0:T(8,128)S(1)}, f32[5,32,128]{2,1,0:T(8,128)S(1)}, u32[]{:S(2)}, u32[]{:S(2)}) collective-permute-start(f32[5,32,128]{2,1,0:T(8,128)S(1)} %pad_maximum_fusion.1.refs_4_), channel_id=1, source_target_pairs={{0,8},{1,3},{2,10},{3,1},{4,12},{5,7},{6,14},{7,5},{8,0},{9,11},{1... | collective-permute-start | bytes 245768 | tf_op jit(solution)/shard_map/ppermute | solution.py:218
  45.3 4.5 %collective-permute-start.18 = (f32[5,32,128]{2,1,0:T(8,128)S(1)}, f32[5,32,128]{2,1,0:T(8,128)S(1)}, u32[]{:S(2)}, u32[]{:S(2)}) collective-permute-start(f32[5,32,128]{2,1,0:T(8,128)S(1)} %pad_maximum_fusion.1.refs_4_), channel_id=1, source_target_pairs={{0,16},{1,5},{2,18},{3,7},{4,20},{5,1},{6,22},{7,3},{8,24},{9,13},... | collective-permute-start | bytes 245768 | tf_op jit(solution)/shard_map/ppermute | solution.py:218
  46.7 5.3 %collective-permute-start.19 = (f32[5,32,128]{2,1,0:T(8,128)S(1)}, f32[5,32,128]{2,1,0:T(8,128)S(1)}, u32[]{:S(2)}, u32[]{:S(2)}) collective-permute-start(f32[5,32,128]{2,1,0:T(8,128)S(1)} %pad_maximum_fusion.1.refs_4_), channel_id=1, source_target_pairs={{0,24},{1,7},{2,26},{3,5},{4,28},{5,3},{6,30},{7,1},{8,16},{9,15},... | collective-permute-start | bytes 245768 | tf_op jit(solution)/shard_map/ppermute | solution.py:218
  54.3 6.3 %collective-permute-start.22 = (f32[5,32,128]{2,1,0:T(8,128)S(1)}, f32[5,32,128]{2,1,0:T(8,128)S(1)}, u32[]{:S(2)}, u32[]{:S(2)}) collective-permute-start(f32[5,32,128]{2,1,0:T(8,128)S(1)} %get-tuple-element.43), channel_id=1, source_target_pairs={{0,6},{1,25},{2,4},{3,27},{4,2},{5,29},{6,0},{7,31},{8,14},{9,17},... | collective-permute-start | bytes 245768 | tf_op jit(solution)/shard_map/ppermute | solution.py:218
  57.8 5.3 %collective-permute-start.21 = (f32[5,32,128]{2,1,0:T(8,128)S(1)}, f32[5,32,128]{2,1,0:T(8,128)S(1)}, u32[]{:S(2)}, u32[]{:S(2)}) collective-permute-start(f32[5,32,128]{2,1,0:T(8,128)S(1)} %get-tuple-element.42), channel_id=1, source_target_pairs={{0,4},{1,17},{2,6},{3,19},{4,0},{5,21},{6,2},{7,23},{8,12},{9,25},... | collective-permute-start | bytes 245768 | tf_op jit(solution)/shard_map/ppermute | solution.py:218
  64.8 5.3 %collective-permute-start.26 = (f32[32,128]{0,1:T(8,128)S(1)}, f32[32,128]{0,1:T(8,128)S(1)}, u32[]{:S(2)}, u32[]{:S(2)}) collective-permute-start(f32[32,128]{0,1:T(8,128)S(1)} %broadcast_select_fusion), channel_id=1, source_target_pairs={{0,24},{1,7},{2,26},{3,5},{4,28},{5,3},{6,30},{7,1},{8,16},{9,15},... | collective-permute-start | bytes 49160 | tf_op jit(solution)/shard_map/ppermute | solution.py:218
  65.1 5.0 %collective-permute-start.25 = (f32[32,128]{0,1:T(8,128)S(1)}, f32[32,128]{0,1:T(8,128)S(1)}, u32[]{:S(2)}, u32[]{:S(2)}) collective-permute-start(f32[32,128]{0,1:T(8,128)S(1)} %broadcast_select_fusion), channel_id=1, source_target_pairs={{0,16},{1,5},{2,18},{3,7},{4,20},{5,1},{6,22},{7,3},{8,24},{9,13},... | collective-permute-start | bytes 49160 | tf_op jit(solution)/shard_map/ppermute | solution.py:218
  71.2 6.2 %collective-permute-start.29 = (f32[32,128]{0,1:T(8,128)S(1)}, f32[32,128]{0,1:T(8,128)S(1)}, u32[]{:S(2)}, u32[]{:S(2)}) collective-permute-start(f32[32,128]{0,1:T(8,128)S(1)} %add_add_fusion.3), channel_id=1, source_target_pairs={{0,6},{1,25},{2,4},{3,27},{4,2},{5,29},{6,0},{7,31},{8,14},{9,17},... | collective-permute-start | bytes 49160 | tf_op jit(solution)/shard_map/ppermute | solution.py:218
  73.0 6.2 %collective-permute-start.28 = (f32[32,128]{0,1:T(8,128)S(1)}, f32[32,128]{0,1:T(8,128)S(1)}, u32[]{:S(2)}, u32[]{:S(2)}) collective-permute-start(f32[32,128]{0,1:T(8,128)S(1)} %add_add_fusion.3), channel_id=1, source_target_pairs={{0,4},{1,17},{2,6},{3,19},{4,0},{5,21},{6,2},{7,23},{8,12},{9,25},... | collective-permute-start | bytes 49160 | tf_op jit(solution)/shard_map/ppermute | solution.py:218
  74.7 5.0 %collective-permute-start.27 = (f32[32,128]{0,1:T(8,128)S(1)}, f32[32,128]{0,1:T(8,128)S(1)}, u32[]{:S(2)}, u32[]{:S(2)}) collective-permute-start(f32[32,128]{0,1:T(8,128)S(1)} %add_add_fusion.3), channel_id=1, source_target_pairs={{0,2},{1,9},{2,0},{3,11},{4,6},{5,13},{6,4},{7,15},{8,10},{9,1},{1... | collective-permute-start | bytes 49160 | tf_op jit(solution)/shard_map/ppermute | solution.py:218
  (7 other events, 27.8 us)

commit v3 on v2

--- a/solution.py
+++ b/solution.py
@@ -281,18 +281,27 @@
             (h, q0),
             (w1, q0),
             (w0, q0),
-        )
-        mine = collect(apply_blocks(matrix, gather(with_aux(h, *pairs)), False, True))
+            (degree * h, h),
+        )
+        gathered = gather(with_aux(h, *pairs))
+        crossed = swap(jnp.concatenate(gathered[1:]))
+        crossed = [gathered[0]] + jnp.split(crossed, parts - 1)
+        sent = apply_blocks(matrix, gathered, False, True)
+        cross = sum(
+            jnp.sum(out[:per] * part[:per], axis=(0, 2)) for out, part in zip(sent, crossed)
+        )
+        lane = lax.broadcasted_iota(jnp.int32, h.shape[1:], 1)
+        cross = jnp.where(lane == len(pairs), cross[:, None], 0.0)
+        sent = [jnp.concatenate([out[:per], (out[per] + cross)[None]]) for out in sent]
+        mine = collect(sent)
         sums = mine[per]
+        tail = sum(gather(sums))
         product = mine[:per] + swap(mine[:per])
         qh = h + gains * (degree * h - product)
-        tail = dots((h, qh))
-        tail = sum(gather(tail))
-        tail = collect([tail] * parts)
-        g11, r1w1, r1w0, hh, hw1, hw0, w11, w10, w00, a_h0, a_10, a_00 = (
+        g11, r1w1, r1w0, hh, hw1, hw0, w11, w10, w00, a_h0, a_10, a_00, hdh = (
             lane_of(sums, n) for n in range(len(pairs))
         )
-        a_hh = lane_of(tail, 0)
+        a_hh = hh + gains * (hdh - 2.0 * lane_of(tail, len(pairs)))
         ratio0 = g11 / gamma0
         curve1 = r1w1 + 2.0 * ratio0 * r1w0 + ratio0 * ratio0 * delta0
         step1 = g11 / curve1

time: 80.7 us -> 71 us (0.88)
  waiting for transfers between devices: 31.8 us -> 26.2 us
  starting transfers between devices: 34 us -> 30.4 us
  Pallas kernels: 10.4 us -> 9.49 us
    ppermute x24 -> x21, waiting for transfers between devices: 27.9 us -> 23.6 us  [joint(): return lax.ppermute(array, ('row', 'col'), pairs)]
    ppermute x24 -> x21, starting transfers between devices: 32.7 us -> 28.5 us  [joint(): return lax.ppermute(array, ('row', 'col'), pairs)]
    ppermute x6 -> x7, waiting for transfers between devices: 3.88 us -> 2.65 us  [swap(): return lax.ppermute(array, 'col', [(c, c ^ 1) for c in range(n_col)])]
    ppermute x6 -> x7, starting transfers between devices: 1.31 us -> 1.91 us  [swap(): return lax.ppermute(array, 'col', [(c, c ^ 1) for c in range(n_col)])]
  transfers between devices with their start and end apart: 30 -> 28, of which waited for: 25 -> 20; matrix products, arithmetic and copies ran while one was open for 1% -> 1% of each run, Pallas kernels for 4% -> 7%
where the time goes in v3:
time: 71 us; the launch traced here: 70.6 us
  starting transfers between devices  30.4 us (43%)
  waiting for transfers between devices  26.2 us (37%)
  Pallas kernels  9.49 us (13%)
  other arithmetic  2.69 us (4%)
  between operations  1.58 us (2%)
    ppermute x21, starting transfers between devices, joint(): return lax.ppermute(array, ('row', 'col'), pairs)  28.5 us
    ppermute x21, waiting for transfers between devices, joint(): return lax.ppermute(array, ('row', 'col'), pairs)  23.6 us
    pallas_call x3, Pallas kernels, apply_blocks(): pl.pallas_call(functools.partial(apply_kernel, parts, with_degree, with_a...  6.38 us
    ppermute x7, waiting for transfers between devices, swap(): return lax.ppermute(array, 'col', [(c, c ^ 1) for c in range(n_col)])  2.65 us
    pallas_call x1, Pallas kernels, split_blocks(): pl.pallas_call(split_kernel, in_specs=[SMEM, SMEM, pl.BlockSpec(memory_sp...  2.33 us
    ppermute x7, starting transfers between devices, swap(): return lax.ppermute(array, 'col', [(c, c ^ 1) for c in range(n_col)])  1.91 us
  transfers between devices with their start and end apart: 28, of which 20 were waited for; matrix products, arithmetic and copies ran while one was open for 1% of the time, Pallas kernels for 7%

profile of v3, /device:TPU:0, one launch (start us, length us, event | category | flops | bytes accessed | tf_op | source)
XLA Modules:
  0.0 70.6 jit_solution(16228975489796510924)
XLA Ops:
  3.3 2.6 %collective-permute-start.3 = (f32[4,32,128]{2,1,0:T(8,128)S(1)}, f32[4,32,128]{2,1,0:T(8,128)S(1)}, u32[]{:S(2)}, u32[]{:S(2)}) collective-permute-start(f32[4,32,128]{2,1,0:T(8,128)S(1)} %maximum_select_fusion.refs_4_), channel_id=1, source_target_pairs={{0,8},{1,3},{2,10},{3,1},{4,12},{5,7},{6,14},{7,5},{8,0},{9,11},{1... | collective-permute-start | bytes 196616 | tf_op jit(solution)/shard_map/ppermute | solution.py:218
  5.9 1.5 %collective-permute-start.4 = (f32[4,32,128]{2,1,0:T(8,128)S(1)}, f32[4,32,128]{2,1,0:T(8,128)S(1)}, u32[]{:S(2)}, u32[]{:S(2)}) collective-permute-start(f32[4,32,128]{2,1,0:T(8,128)S(1)} %maximum_select_fusion.refs_4_), channel_id=1, source_target_pairs={{0,16},{1,5},{2,18},{3,7},{4,20},{5,1},{6,22},{7,3},{8,24},{9,13},... | collective-permute-start | bytes 196616 | tf_op jit(solution)/shard_map/ppermute | solution.py:218
  7.8 2.3 %shard_map.69 = (bf16[40,256,128]{2,1,0:T(8,128)(2,1)S(1)}, bf16[40,256,128]{2,1,0:T(8,128)(2,1)S(1)}) custom-call(s32[3,40]{1,0:T(4,128)S(1)} %get-tuple-element.23.own_places.refs_0_, s32[3,40]{1,0:T(4,128)S(1)} %collective-permute-done.other_places.refs_1_, f32[40,128,128]{2,1,0:T(8,128)} %bitcast.8, f32[40,128,128]{2,1,0:T(8,128)S(1)} %collective-permute-done.2.other_in), custom_call_target="tpu_custom_call" | custom-call | flops 5242880 | bytes 10485760 | tf_op jit(solution)/shard_map/pallas_call | solution.py:85
  10.2 2.4 %collective-permute-done.5.refs_7_ = f32[4,32,128]{2,1,0:T(8,128)S(1)} collective-permute-done((f32[4,32,128]{2,1,0:T(8,128)S(1)}, f32[4,32,128]{2,1,0:T(8,128)S(1)}, u32[]{:S(2)}, u32[]{:S(2)}) %collective-permute-start.5) | collective-permute-done | bytes 65568 | tf_op jit(solution)/shard_map/ppermute | solution.py:218
  12.6 2.2 %shard_map.70 = (f32[5,32,128]{2,1,0:T(8,128)S(1)}, f32[5,32,128]{2,1,0:T(8,128)S(1)}, f32[5,32,128]{2,1,0:T(8,128)S(1)}, f32[5,32,128]{2,1,0:T(8,128)S(1)}) custom-call(s32[3,40]{1,0:T(4,128)S(1)} %get-tuple-element.23.own_places.refs_0_, s32[3,40]{1,0:T(4,128)S(1)} %collective-permute-done.other_places.refs_1_, ...), custom_call_target="tpu_custom_call" | custom-call | flops 419430400 | bytes 5242880 | tf_op jit(solution)/shard_map/pallas_call | solution.py:176
  14.8 4.1 %collective-permute-start.8 = (f32[5,32,128]{2,1,0:T(8,128)S(1)}, f32[5,32,128]{2,1,0:T(8,128)S(1)}, u32[]{:S(2)}, u32[]{:S(2)}) collective-permute-start(f32[5,32,128]{2,1,0:T(8,128)S(1)} %get-tuple-element.35), channel_id=1, source_target_pairs={{0,6},{1,25},{2,4},{3,27},{4,2},{5,29},{6,0},{7,31},{8,14},{9,17},... | collective-permute-start | bytes 245768 | tf_op jit(solution)/shard_map/ppermute | solution.py:218
  19.6 1.8 %collective-permute-done.8 = f32[5,32,128]{2,1,0:T(8,128)S(1)} collective-permute-done((f32[5,32,128]{2,1,0:T(8,128)S(1)}, f32[5,32,128]{2,1,0:T(8,128)S(1)}, u32[]{:S(2)}, u32[]{:S(2)}) %collective-permute-start.8) | collective-permute-done | bytes 81952 | tf_op jit(solution)/shard_map/ppermute | solution.py:218
  21.5 1.9 %collective-permute-done.6 = f32[5,32,128]{2,1,0:T(8,128)S(1)} collective-permute-done((f32[5,32,128]{2,1,0:T(8,128)S(1)}, f32[5,32,128]{2,1,0:T(8,128)S(1)}, u32[]{:S(2)}, u32[]{:S(2)}) %collective-permute-start.6) | collective-permute-done | bytes 81952 | tf_op jit(solution)/shard_map/ppermute | solution.py:218
  24.4 1.3 %collective-permute-done.9 = f32[5,32,128]{2,1,0:T(8,128)S(1)} collective-permute-done((f32[5,32,128]{2,1,0:T(8,128)S(1)}, f32[5,32,128]{2,1,0:T(8,128)S(1)}, u32[]{:S(2)}, u32[]{:S(2)}) %collective-permute-start.9) | collective-permute-done | bytes 81952 | tf_op jit(solution)/shard_map/ppermute | solution.py:221
  26.6 3.0 %collective-permute-start.12 = (f32[5,32,128]{2,1,0:T(8,128)S(1)}, f32[5,32,128]{2,1,0:T(8,128)S(1)}, u32[]{:S(2)}, u32[]{:S(2)}) collective-permute-start(f32[5,32,128]{2,1,0:T(8,128)S(1)} %pad_maximum_fusion.1.refs_4_), channel_id=1, source_target_pairs={{0,24},{1,7},{2,26},{3,5},{4,28},{5,3},{6,30},{7,1},{8,16},{9,15},... | collective-permute-start | bytes 245768 | tf_op jit(solution)/shard_map/ppermute | solution.py:218
  30.6 1.4 %collective-permute-done.12.refs_7_ = f32[5,32,128]{2,1,0:T(8,128)S(1)} collective-permute-done((f32[5,32,128]{2,1,0:T(8,128)S(1)}, f32[5,32,128]{2,1,0:T(8,128)S(1)}, u32[]{:S(2)}, u32[]{:S(2)}) %collective-permute-start.12) | collective-permute-done | bytes 81952 | tf_op jit(solution)/shard_map/ppermute | solution.py:218
  32.0 2.1 %shard_map.71 = (f32[5,32,128]{2,1,0:T(8,128)S(1)}, f32[5,32,128]{2,1,0:T(8,128)S(1)}, f32[5,32,128]{2,1,0:T(8,128)S(1)}, f32[5,32,128]{2,1,0:T(8,128)S(1)}) custom-call(s32[3,40]{1,0:T(4,128)S(1)} %get-tuple-element.23.own_places.refs_0_, s32[3,40]{1,0:T(4,128)S(1)} %collective-permute-done.other_places.refs_1_, ...), custom_call_target="tpu_custom_call" | custom-call | flops 335544320 | bytes 5242880 | tf_op jit(solution)/shard_map/pallas_call | solution.py:176
  34.1 2.3 %collective-permute-start.15 = (f32[5,32,128]{2,1,0:T(8,128)S(1)}, f32[5,32,128]{2,1,0:T(8,128)S(1)}, u32[]{:S(2)}, u32[]{:S(2)}) collective-permute-start(f32[5,32,128]{2,1,0:T(8,128)S(1)} %get-tuple-element.39), channel_id=1, source_target_pairs={{0,6},{1,25},{2,4},{3,27},{4,2},{5,29},{6,0},{7,31},{8,14},{9,17},... | collective-permute-start | bytes 245768 | tf_op jit(solution)/shard_map/ppermute | solution.py:218
  36.7 1.8 %collective-permute-start.14 = (f32[5,32,128]{2,1,0:T(8,128)S(1)}, f32[5,32,128]{2,1,0:T(8,128)S(1)}, u32[]{:S(2)}, u32[]{:S(2)}) collective-permute-start(f32[5,32,128]{2,1,0:T(8,128)S(1)} %get-tuple-element.38), channel_id=1, source_target_pairs={{0,4},{1,17},{2,6},{3,19},{4,0},{5,21},{6,2},{7,23},{8,12},{9,25},... | collective-permute-start | bytes 245768 | tf_op jit(solution)/shard_map/ppermute | solution.py:218
  38.5 2.0 %collective-permute-done.15 = f32[5,32,128]{2,1,0:T(8,128)S(1)} collective-permute-done((f32[5,32,128]{2,1,0:T(8,128)S(1)}, f32[5,32,128]{2,1,0:T(8,128)S(1)}, u32[]{:S(2)}, u32[]{:S(2)}) %collective-permute-start.15) | collective-permute-done | bytes 81952 | tf_op jit(solution)/shard_map/ppermute | solution.py:218
  40.5 1.7 %collective-permute-done.13 = f32[5,32,128]{2,1,0:T(8,128)S(1)} collective-permute-done((f32[5,32,128]{2,1,0:T(8,128)S(1)}, f32[5,32,128]{2,1,0:T(8,128)S(1)}, u32[]{:S(2)}, u32[]{:S(2)}) %collective-permute-start.13) | collective-permute-done | bytes 81952 | tf_op jit(solution)/shard_map/ppermute | solution.py:218
  44.2 2.0 %collective-permute-start.17 = (f32[5,32,128]{2,1,0:T(8,128)S(1)}, f32[5,32,128]{2,1,0:T(8,128)S(1)}, u32[]{:S(2)}, u32[]{:S(2)}) collective-permute-start(f32[5,32,128]{2,1,0:T(8,128)S(1)} %pad_maximum_fusion.2.refs_4_), channel_id=1, source_target_pairs={{0,8},{1,3},{2,10},{3,1},{4,12},{5,7},{6,14},{7,5},{8,0},{9,11},{1... | collective-permute-start | bytes 245768 | tf_op jit(solution)/shard_map/ppermute | solution.py:218
  48.7 1.9 %collective-permute-done.18.refs_6_ = f32[5,32,128]{2,1,0:T(8,128)S(1)} collective-permute-done((f32[5,32,128]{2,1,0:T(8,128)S(1)}, f32[5,32,128]{2,1,0:T(8,128)S(1)}, u32[]{:S(2)}, u32[]{:S(2)}) %collective-permute-start.18) | collective-permute-done | bytes 81952 | tf_op jit(solution)/shard_map/ppermute | solution.py:218
  50.6 1.6 %collective-permute-done.19.refs_7_ = f32[5,32,128]{2,1,0:T(8,128)S(1)} collective-permute-done((f32[5,32,128]{2,1,0:T(8,128)S(1)}, f32[5,32,128]{2,1,0:T(8,128)S(1)}, u32[]{:S(2)}, u32[]{:S(2)}) %collective-permute-start.19) | collective-permute-done | bytes 81952 | tf_op jit(solution)/shard_map/ppermute | solution.py:218
  52.9 2.1 %shard_map.72 = (f32[5,32,128]{2,1,0:T(8,128)S(1)}, f32[5,32,128]{2,1,0:T(8,128)S(1)}, f32[5,32,128]{2,1,0:T(8,128)S(1)}, f32[5,32,128]{2,1,0:T(8,128)S(1)}) custom-call(s32[3,40]{1,0:T(4,128)S(1)} %get-tuple-element.23.own_places.refs_0_, s32[3,40]{1,0:T(4,128)S(1)} %collective-permute-done.other_places.refs_1_, ...), custom_call_target="tpu_custom_call" | custom-call | flops 335544320 | bytes 5242880 | tf_op jit(solution)/shard_map/pallas_call | solution.py:176
  55.3 3.0 %collective-permute-start.23 = (f32[5,32,128]{2,1,0:T(8,128)S(1)}, f32[5,32,128]{2,1,0:T(8,128)S(1)}, u32[]{:S(2)}, u32[]{:S(2)}) collective-permute-start(f32[5,32,128]{2,1,0:T(8,128)S(1)} %pad_maximum_fusion.5), channel_id=1, source_target_pairs={{0,6},{1,25},{2,4},{3,27},{4,2},{5,29},{6,0},{7,31},{8,14},{9,17},... | collective-permute-start | bytes 245768 | tf_op jit(solution)/shard_map/ppermute | solution.py:218
  58.3 1.5 %collective-permute-start.22 = (f32[5,32,128]{2,1,0:T(8,128)S(1)}, f32[5,32,128]{2,1,0:T(8,128)S(1)}, u32[]{:S(2)}, u32[]{:S(2)}) collective-permute-start(f32[5,32,128]{2,1,0:T(8,128)S(1)} %pad_maximum_fusion.4), channel_id=1, source_target_pairs={{0,4},{1,17},{2,6},{3,19},{4,0},{5,21},{6,2},{7,23},{8,12},{9,25},... | collective-permute-start | bytes 245768 | tf_op jit(solution)/shard_map/ppermute | solution.py:218
  59.8 1.8 %collective-permute-done.23 = f32[5,32,128]{2,1,0:T(8,128)S(1)} collective-permute-done((f32[5,32,128]{2,1,0:T(8,128)S(1)}, f32[5,32,128]{2,1,0:T(8,128)S(1)}, u32[]{:S(2)}, u32[]{:S(2)}) %collective-permute-start.23) | collective-permute-done | bytes 81952 | tf_op jit(solution)/shard_map/ppermute | solution.py:218
  65.5 1.8 %collective-permute-start.24 = (f32[32,128]{1,0:T(8,128)S(1)}, f32[32,128]{1,0:T(8,128)S(1)}, u32[]{:S(2)}, u32[]{:S(2)}) collective-permute-start(f32[32,128]{1,0:T(8,128)S(1)} %slice_bitcast_fusion), channel_id=1, source_target_pairs={{0,8},{1,3},{2,10},{3,1},{4,12},{5,7},{6,14},{7,5},{8,0},{9,11},{1... | collective-permute-start | bytes 49160 | tf_op jit(solution)/shard_map/ppermute | solution.py:218
  (84 shorter events, 18.8 us)
Async XLA Ops:
  2.6 5.2 %collective-permute-start.2 = (f32[40,128,128]{2,1,0:T(8,128)}, f32[40,128,128]{2,1,0:T(8,128)S(1)}, u32[]{:S(2)}, u32[]{:S(2)}) collective-permute-start(f32[40,128,128]{2,1,0:T(8,128)} %bitcast.7), channel_id=1, source_target_pairs={{0,1},{1,0},{2,3},{3,2},{4,5},{5,4},{6,7},{7,6},{8,9},{9,8},{10,11... | collective-permute-start | bytes 7864328 | tf_op jit(solution)/shard_map/ppermute | solution.py:221
  2.7 5.1 %collective-permute-start = (s32[3,40]{1,0:T(4,128)S(1)}, s32[3,40]{1,0:T(4,128)S(1)}, u32[]{:S(2)}, u32[]{:S(2)}) collective-permute-start(s32[3,40]{1,0:T(4,128)S(1)} %get-tuple-element.23.own_places.refs_0_), channel_id=1, source_target_pairs={{0,1},{1,0},{2,3},{3,2},{4,5},{5,4},{6,7},{7,6},{8,9},{9,8},{10,11... | collective-permute-start | bytes 1448 | tf_op jit(solution)/shard_map/ppermute | solution.py:221
  3.3 6.9 %collective-permute-start.3 = (f32[4,32,128]{2,1,0:T(8,128)S(1)}, f32[4,32,128]{2,1,0:T(8,128)S(1)}, u32[]{:S(2)}, u32[]{:S(2)}) collective-permute-start(f32[4,32,128]{2,1,0:T(8,128)S(1)} %maximum_select_fusion.refs_4_), channel_id=1, source_target_pairs={{0,8},{1,3},{2,10},{3,1},{4,12},{5,7},{6,14},{7,5},{8,0},{9,11},{1... | collective-permute-start | bytes 196616 | tf_op jit(solution)/shard_map/ppermute | solution.py:218
  5.9 4.3 %collective-permute-start.4 = (f32[4,32,128]{2,1,0:T(8,128)S(1)}, f32[4,32,128]{2,1,0:T(8,128)S(1)}, u32[]{:S(2)}, u32[]{:S(2)}) collective-permute-start(f32[4,32,128]{2,1,0:T(8,128)S(1)} %maximum_select_fusion.refs_4_), channel_id=1, source_target_pairs={{0,16},{1,5},{2,18},{3,7},{4,20},{5,1},{6,22},{7,3},{8,24},{9,13},... | collective-permute-start | bytes 196616 | tf_op jit(solution)/shard_map/ppermute | solution.py:218
  7.4 5.2 %collective-permute-start.5 = (f32[4,32,128]{2,1,0:T(8,128)S(1)}, f32[4,32,128]{2,1,0:T(8,128)S(1)}, u32[]{:S(2)}, u32[]{:S(2)}) collective-permute-start(f32[4,32,128]{2,1,0:T(8,128)S(1)} %maximum_select_fusion.refs_4_), channel_id=1, source_target_pairs={{0,24},{1,7},{2,26},{3,5},{4,28},{5,3},{6,30},{7,1},{8,16},{9,15},... | collective-permute-start | bytes 196616 | tf_op jit(solution)/shard_map/ppermute | solution.py:218
  14.8 6.6 %collective-permute-start.8 = (f32[5,32,128]{2,1,0:T(8,128)S(1)}, f32[5,32,128]{2,1,0:T(8,128)S(1)}, u32[]{:S(2)}, u32[]{:S(2)}) collective-permute-start(f32[5,32,128]{2,1,0:T(8,128)S(1)} %get-tuple-element.35), channel_id=1, source_target_pairs={{0,6},{1,25},{2,4},{3,27},{4,2},{5,29},{6,0},{7,31},{8,14},{9,17},... | collective-permute-start | bytes 245768 | tf_op jit(solution)/shard_map/ppermute | solution.py:218
  19.0 4.4 %collective-permute-start.6 = (f32[5,32,128]{2,1,0:T(8,128)S(1)}, f32[5,32,128]{2,1,0:T(8,128)S(1)}, u32[]{:S(2)}, u32[]{:S(2)}) collective-permute-start(f32[5,32,128]{2,1,0:T(8,128)S(1)} %get-tuple-element.33), channel_id=1, source_target_pairs={{0,2},{1,9},{2,0},{3,11},{4,6},{5,13},{6,4},{7,15},{8,10},{9,1},{1... | collective-permute-start | bytes 245768 | tf_op jit(solution)/shard_map/ppermute | solution.py:218
  19.0 5.3 %collective-permute-start.7 = (f32[5,32,128]{2,1,0:T(8,128)S(1)}, f32[5,32,128]{2,1,0:T(8,128)S(1)}, u32[]{:S(2)}, u32[]{:S(2)}) collective-permute-start(f32[5,32,128]{2,1,0:T(8,128)S(1)} %get-tuple-element.34), channel_id=1, source_target_pairs={{0,4},{1,17},{2,6},{3,19},{4,0},{5,21},{6,2},{7,23},{8,12},{9,25},... | collective-permute-start | bytes 245768 | tf_op jit(solution)/shard_map/ppermute | solution.py:218
  26.0 4.5 %collective-permute-start.10 = (f32[5,32,128]{2,1,0:T(8,128)S(1)}, f32[5,32,128]{2,1,0:T(8,128)S(1)}, u32[]{:S(2)}, u32[]{:S(2)}) collective-permute-start(f32[5,32,128]{2,1,0:T(8,128)S(1)} %pad_maximum_fusion.1.refs_4_), channel_id=1, source_target_pairs={{0,8},{1,3},{2,10},{3,1},{4,12},{5,7},{6,14},{7,5},{8,0},{9,11},{1... | collective-permute-start | bytes 245768 | tf_op jit(solution)/shard_map/ppermute | solution.py:218
  26.1 4.5 %collective-permute-start.11 = (f32[5,32,128]{2,1,0:T(8,128)S(1)}, f32[5,32,128]{2,1,0:T(8,128)S(1)}, u32[]{:S(2)}, u32[]{:S(2)}) collective-permute-start(f32[5,32,128]{2,1,0:T(8,128)S(1)} %pad_maximum_fusion.1.refs_4_), channel_id=1, source_target_pairs={{0,16},{1,5},{2,18},{3,7},{4,20},{5,1},{6,22},{7,3},{8,24},{9,13},... | collective-permute-start | bytes 245768 | tf_op jit(solution)/shard_map/ppermute | solution.py:218
  26.6 5.4 %collective-permute-start.12 = (f32[5,32,128]{2,1,0:T(8,128)S(1)}, f32[5,32,128]{2,1,0:T(8,128)S(1)}, u32[]{:S(2)}, u32[]{:S(2)}) collective-permute-start(f32[5,32,128]{2,1,0:T(8,128)S(1)} %pad_maximum_fusion.1.refs_4_), channel_id=1, source_target_pairs={{0,24},{1,7},{2,26},{3,5},{4,28},{5,3},{6,30},{7,1},{8,16},{9,15},... | collective-permute-start | bytes 245768 | tf_op jit(solution)/shard_map/ppermute | solution.py:218
  34.1 6.5 %collective-permute-start.15 = (f32[5,32,128]{2,1,0:T(8,128)S(1)}, f32[5,32,128]{2,1,0:T(8,128)S(1)}, u32[]{:S(2)}, u32[]{:S(2)}) collective-permute-start(f32[5,32,128]{2,1,0:T(8,128)S(1)} %get-tuple-element.39), channel_id=1, source_target_pairs={{0,6},{1,25},{2,4},{3,27},{4,2},{5,29},{6,0},{7,31},{8,14},{9,17},... | collective-permute-start | bytes 245768 | tf_op jit(solution)/shard_map/ppermute | solution.py:218
  36.4 5.9 %collective-permute-start.13 = (f32[5,32,128]{2,1,0:T(8,128)S(1)}, f32[5,32,128]{2,1,0:T(8,128)S(1)}, u32[]{:S(2)}, u32[]{:S(2)}) collective-permute-start(f32[5,32,128]{2,1,0:T(8,128)S(1)} %get-tuple-element.37), channel_id=1, source_target_pairs={{0,2},{1,9},{2,0},{3,11},{4,6},{5,13},{6,4},{7,15},{8,10},{9,1},{1... | collective-permute-start | bytes 245768 | tf_op jit(solution)/shard_map/ppermute | solution.py:218
  36.7 5.6 %collective-permute-start.14 = (f32[5,32,128]{2,1,0:T(8,128)S(1)}, f32[5,32,128]{2,1,0:T(8,128)S(1)}, u32[]{:S(2)}, u32[]{:S(2)}) collective-permute-start(f32[5,32,128]{2,1,0:T(8,128)S(1)} %get-tuple-element.38), channel_id=1, source_target_pairs={{0,4},{1,17},{2,6},{3,19},{4,0},{5,21},{6,2},{7,23},{8,12},{9,25},... | collective-permute-start | bytes 245768 | tf_op jit(solution)/shard_map/ppermute | solution.py:218
  44.2 4.5 %collective-permute-start.17 = (f32[5,32,128]{2,1,0:T(8,128)S(1)}, f32[5,32,128]{2,1,0:T(8,128)S(1)}, u32[]{:S(2)}, u32[]{:S(2)}) collective-permute-start(f32[5,32,128]{2,1,0:T(8,128)S(1)} %pad_maximum_fusion.2.refs_4_), channel_id=1, source_target_pairs={{0,8},{1,3},{2,10},{3,1},{4,12},{5,7},{6,14},{7,5},{8,0},{9,11},{1... | collective-permute-start | bytes 245768 | tf_op jit(solution)/shard_map/ppermute | solution.py:218
  46.2 4.4 %collective-permute-start.18 = (f32[5,32,128]{2,1,0:T(8,128)S(1)}, f32[5,32,128]{2,1,0:T(8,128)S(1)}, u32[]{:S(2)}, u32[]{:S(2)}) collective-permute-start(f32[5,32,128]{2,1,0:T(8,128)S(1)} %pad_maximum_fusion.2.refs_4_), channel_id=1, source_target_pairs={{0,16},{1,5},{2,18},{3,7},{4,20},{5,1},{6,22},{7,3},{8,24},{9,13},... | collective-permute-start | bytes 245768 | tf_op jit(solution)/shard_map/ppermute | solution.py:218
  46.8 5.3 %collective-permute-start.19 = (f32[5,32,128]{2,1,0:T(8,128)S(1)}, f32[5,32,128]{2,1,0:T(8,128)S(1)}, u32[]{:S(2)}, u32[]{:S(2)}) collective-permute-start(f32[5,32,128]{2,1,0:T(8,128)S(1)} %pad_maximum_fusion.2.refs_4_), channel_id=1, source_target_pairs={{0,24},{1,7},{2,26},{3,5},{4,28},{5,3},{6,30},{7,1},{8,16},{9,15},... | collective-permute-start | bytes 245768 | tf_op jit(solution)/shard_map/ppermute | solution.py:218
  52.2 2.9 %collective-permute-start.20 = (f32[15,32,128]{2,1,0:T(8,128)S(1)}, f32[15,32,128]{2,1,0:T(8,128)S(1)}, u32[]{:S(2)}, u32[]{:S(2)}) collective-permute-start(f32[15,32,128]{2,1,0:T(8,128)S(1)} %pad_maximum_fusion), channel_id=1, source_target_pairs={{0,1},{1,0},{2,3},{3,2},{4,5},{5,4},{6,7},{7,6},{8,9},{9,8},{10,11... | collective-permute-start | bytes 737288 | tf_op jit(solution)/shard_map/ppermute | solution.py:221
  55.3 6.3 %collective-permute-start.23 = (f32[5,32,128]{2,1,0:T(8,128)S(1)}, f32[5,32,128]{2,1,0:T(8,128)S(1)}, u32[]{:S(2)}, u32[]{:S(2)}) collective-permute-start(f32[5,32,128]{2,1,0:T(8,128)S(1)} %pad_maximum_fusion.5), channel_id=1, source_target_pairs={{0,6},{1,25},{2,4},{3,27},{4,2},{5,29},{6,0},{7,31},{8,14},{9,17},... | collective-permute-start | bytes 245768 | tf_op jit(solution)/shard_map/ppermute | solution.py:218
  58.3 4.4 %collective-permute-start.21 = (f32[5,32,128]{2,1,0:T(8,128)S(1)}, f32[5,32,128]{2,1,0:T(8,128)S(1)}, u32[]{:S(2)}, u32[]{:S(2)}) collective-permute-start(f32[5,32,128]{2,1,0:T(8,128)S(1)} %pad_maximum_fusion.3), channel_id=1, source_target_pairs={{0,2},{1,9},{2,0},{3,11},{4,6},{5,13},{6,4},{7,15},{8,10},{9,1},{1... | collective-permute-start | bytes 245768 | tf_op jit(solution)/shard_map/ppermute | solution.py:218
  58.3 5.4 %collective-permute-start.22 = (f32[5,32,128]{2,1,0:T(8,128)S(1)}, f32[5,32,128]{2,1,0:T(8,128)S(1)}, u32[]{:S(2)}, u32[]{:S(2)}) collective-permute-start(f32[5,32,128]{2,1,0:T(8,128)S(1)} %pad_maximum_fusion.4), channel_id=1, source_target_pairs={{0,4},{1,17},{2,6},{3,19},{4,0},{5,21},{6,2},{7,23},{8,12},{9,25},... | collective-permute-start | bytes 245768 | tf_op jit(solution)/shard_map/ppermute | solution.py:218
  63.8 4.7 %collective-permute-start.26 = (f32[32,128]{1,0:T(8,128)S(1)}, f32[32,128]{1,0:T(8,128)S(1)}, u32[]{:S(2)}, u32[]{:S(2)}) collective-permute-start(f32[32,128]{1,0:T(8,128)S(1)} %slice_bitcast_fusion), channel_id=1, source_target_pairs={{0,24},{1,7},{2,26},{3,5},{4,28},{5,3},{6,30},{7,1},{8,16},{9,15},... | collective-permute-start | bytes 49160 | tf_op jit(solution)/shard_map/ppermute | solution.py:218
  64.4 4.1 %collective-permute-start.25 = (f32[32,128]{1,0:T(8,128)S(1)}, f32[32,128]{1,0:T(8,128)S(1)}, u32[]{:S(2)}, u32[]{:S(2)}) collective-permute-start(f32[32,128]{1,0:T(8,128)S(1)} %slice_bitcast_fusion), channel_id=1, source_target_pairs={{0,16},{1,5},{2,18},{3,7},{4,20},{5,1},{6,22},{7,3},{8,24},{9,13},... | collective-permute-start | bytes 49160 | tf_op jit(solution)/shard_map/ppermute | solution.py:218
  65.5 3.7 %collective-permute-start.24 = (f32[32,128]{1,0:T(8,128)S(1)}, f32[32,128]{1,0:T(8,128)S(1)}, u32[]{:S(2)}, u32[]{:S(2)}) collective-permute-start(f32[32,128]{1,0:T(8,128)S(1)} %slice_bitcast_fusion), channel_id=1, source_target_pairs={{0,8},{1,3},{2,10},{3,1},{4,12},{5,7},{6,14},{7,5},{8,0},{9,11},{1... | collective-permute-start | bytes 49160 | tf_op jit(solution)/shard_map/ppermute | solution.py:218
  (5 other events, 20.2 us)

commit v4 on v3

--- a/solution.py
+++ b/solution.py
@@ -10,7 +10,11 @@
 F32 = jnp.float32
 VMEM = pl.BlockSpec(memory_space=pltpu.VMEM)
 SMEM = pl.BlockSpec(memory_space=pltpu.SMEM)
-GROUP = 8
+COPY = 8
+
+
+def far_first(parts):
+    return list(range(2, parts)) + [1]
 
 
 def core_here():
@@ -47,27 +51,33 @@
     slots, size, _ = own_in.shape
     core = core_here()
     copies = []
-    for chunk in range(slots // GROUP):
-        cut = pl.ds(chunk * GROUP, GROUP)
+    for chunk in range(slots // COPY):
+        cut = pl.ds(chunk * COPY, COPY)
         copies.append(pltpu.make_async_copy(own_hbm.at[cut], own_in.at[cut], sems.at[chunk]))
     for copy in copies:
         copy.start()
 
     def write(turn):
         def sweep(places, source, target, chunk):
-            @pl.when(chunk * GROUP < places[2, 0])
+            live = chunk * COPY < places[2, 0]
+
+            @pl.when(live)
             def _():
-                for i in range(GROUP):
-                    slot = chunk * GROUP + i
+                for i in range(COPY):
+                    slot = chunk * COPY + i
                     block = jnp.where(slot < places[2, 0], source[slot], 0.0)
                     block = block.T if turn else block
                     high = block.astype(BF)
                     target[slot, :size] = high
                     target[slot, size:] = (block - high.astype(F32)).astype(BF)
 
-        for chunk in range(slots // GROUP):
+            @pl.when(jnp.logical_not(live))
+            def _():
+                target[pl.ds(chunk * COPY, COPY)] = jnp.zeros((COPY, 2 * size, size), BF)
+
+        for chunk in range(slots // COPY):
             sweep(other_places, other_in, other_out, chunk)
-        for chunk in range(slots // GROUP):
+        for chunk in range(slots // COPY):
             copies[chunk].wait()
             sweep(own_places, own_in, own_out, chunk)
 
@@ -89,7 +99,7 @@
         out_shape=[pltpu.VMEM((slots, 2 * size, size), BF)] * 2,
         scratch_shapes=[
             pltpu.VMEM((slots, size, size), F32),
-            pltpu.SemaphoreType.DMA((slots // GROUP,)),
+            pltpu.SemaphoreType.DMA((slots // COPY,)),
         ],
         compiler_params=pltpu.CompilerParams(vmem_limit_bytes=32 * 2**20),
         cost_estimate=pl.CostEstimate(
@@ -105,7 +115,9 @@
 
 def apply_kernel(parts, with_degree, with_aux, *refs):
     own_places, other_places, own_ref, other_ref = refs[:4]
-    fields = refs[4 : 4 + parts]
+    fields = [refs[4]] + [None] * (parts - 1)
+    for part, ref in zip(far_first(parts), refs[5:]):
+        fields[part] = ref
     outs = refs[4 + parts : 4 + 2 * parts]
     stack_ref, sum_ref = refs[4 + 2 * parts :]
     per = outs[0].shape[0] - 1
@@ -124,14 +136,15 @@
                 stack_ref[f, 2 * width :, :] = jnp.ones((16, 2 * size), BF)
     sum_ref[...] = jnp.zeros_like(sum_ref)
     core = core_here()
+    run = own_ref.shape[0]
 
     def sweep(values_ref, places):
         count = places[2, 0]
 
         def group(g, carry):
             products = []
-            for i in range(GROUP):
-                q = g * GROUP + i
+            for i in range(run):
+                q = g * run + i
                 products.append(
                     jnp.dot(
                         stack_ref[places[1 - core, q]],
@@ -139,15 +152,15 @@
                         preferred_element_type=F32,
                     )
                 )
-            for i in range(GROUP):
-                to = places[core, g * GROUP + i]
+            for i in range(run):
+                to = places[core, g * run + i]
                 whole = products[i]
                 sum_ref[to, :width] += whole[:width] + whole[width : 2 * width]
                 if with_degree:
                     sum_ref[to, width:] += whole[2 * width : 2 * width + 8]
             return carry
 
-        lax.fori_loop(0, (count + GROUP - 1) // GROUP, group, 0)
+        lax.fori_loop(0, (count + run - 1) // run, group, 0)
 
     sweep(own_ref, own_places)
     sweep(other_ref, other_places)
@@ -188,7 +201,7 @@
             bytes_accessed=4 * slots * size * size * 2,
             transcendentals=0,
         ),
-    )(*matrix, *fields)
+    )(*matrix, fields[0], *(fields[part] for part in far_first(parts)))
 
 
 def dots(*pairs):
@@ -224,7 +237,10 @@
         return [field] + [joint(field, offset, 0) for offset in range(1, parts)]
 
     def collect(sent):
-        return sent[0] + sum(joint(sent[offset], offset, 1) for offset in range(1, parts))
+        total = sent[0]
+        for offset in reversed(far_first(parts)):
+            total = total + joint(sent[offset], offset, 1)
+        return total
 
     def shards(block_values, block_index, block_count, strength, raw_scores):
         values = block_values[0, 0]

time: 71 us -> 69.3 us (0.976)
  starting transfers between devices: 30.4 us -> 27.8 us
  waiting for transfers between devices: 26.2 us -> 27.4 us
    ppermute x21, starting transfers between devices: 28.5 us -> 26.4 us  [joint(): return lax.ppermute(array, ('row', 'col'), pairs)]
    ppermute x21, waiting for transfers between devices: 23.6 us -> 24.8 us  [joint(): return lax.ppermute(array, ('row', 'col'), pairs)]
  transfers between devices with their start and end apart: 28 -> 28, of which waited for: 20 -> 22; matrix products, arithmetic and copies ran while one was open for 1% -> 1% of each run, Pallas kernels for 7% -> 8%
where the time goes in v4:
time: 69.3 us; the launch traced here: 68.9 us
  starting transfers between devices  27.8 us (40%)
  waiting for transfers between devices  27.4 us (40%)
  Pallas kernels  9.26 us (13%)
  other arithmetic  2.69 us (4%)
  between operations  1.56 us (2%)
    ppermute x21, starting transfers between devices, joint(): return lax.ppermute(array, ('row', 'col'), pairs)  26.4 us
    ppermute x21, waiting for transfers between devices, joint(): return lax.ppermute(array, ('row', 'col'), pairs)  24.8 us
    pallas_call x3, Pallas kernels, apply_blocks(): pl.pallas_call(functools.partial(apply_kernel, parts, with_degree, with_a...  5.99 us
    ppermute x7, waiting for transfers between devices, swap(): return lax.ppermute(array, 'col', [(c, c ^ 1) for c in range(n_col)])  2.62 us
    pallas_call x1, Pallas kernels, split_blocks(): pl.pallas_call(split_kernel, in_specs=[SMEM, SMEM, pl.BlockSpec(memory_sp...  2.48 us
    ppermute x7, starting transfers between devices, swap(): return lax.ppermute(array, 'col', [(c, c ^ 1) for c in range(n_col)])  1.42 us
  transfers between devices with their start and end apart: 28, of which 22 were waited for; matrix products, arithmetic and copies ran while one was open for 1% of the time, Pallas kernels for 8%

profile of v4, /device:TPU:0, one launch (start us, length us, event | category | flops | bytes accessed | tf_op | source)
XLA Modules:
  0.0 68.9 jit_solution(6199800213416509571)
XLA Ops:
  3.3 2.7 %collective-permute-start.3 = (f32[4,32,128]{2,1,0:T(8,128)S(1)}, f32[4,32,128]{2,1,0:T(8,128)S(1)}, u32[]{:S(2)}, u32[]{:S(2)}) collective-permute-start(f32[4,32,128]{2,1,0:T(8,128)S(1)} %maximum_select_fusion.refs_4_), channel_id=1, source_target_pairs={{0,16},{1,5},{2,18},{3,7},{4,20},{5,1},{6,22},{7,3},{8,24},{9,13},... | collective-permute-start | bytes 196616 | tf_op jit(solution)/shard_map/ppermute | solution.py:231
  5.9 1.4 %collective-permute-start.4 = (f32[4,32,128]{2,1,0:T(8,128)S(1)}, f32[4,32,128]{2,1,0:T(8,128)S(1)}, u32[]{:S(2)}, u32[]{:S(2)}) collective-permute-start(f32[4,32,128]{2,1,0:T(8,128)S(1)} %maximum_select_fusion.refs_4_), channel_id=1, source_target_pairs={{0,24},{1,7},{2,26},{3,5},{4,28},{5,3},{6,30},{7,1},{8,16},{9,15},... | collective-permute-start | bytes 196616 | tf_op jit(solution)/shard_map/ppermute | solution.py:231
  7.8 2.5 %shard_map.69 = (bf16[40,256,128]{2,1,0:T(8,128)(2,1)S(1)}, bf16[40,256,128]{2,1,0:T(8,128)(2,1)S(1)}) custom-call(s32[3,40]{1,0:T(4,128)S(1)} %get-tuple-element.23.own_places.refs_0_, s32[3,40]{1,0:T(4,128)S(1)} %collective-permute-done.other_places.refs_1_, f32[40,128,128]{2,1,0:T(8,128)} %bitcast.8, f32[40,128,128]{2,1,0:T(8,128)S(1)} %collective-permute-done.2.other_in), custom_call_target="tpu_custom_call" | custom-call | flops 5242880 | bytes 10485760 | tf_op jit(solution)/shard_map/pallas_call | solution.py:95
  11.6 2.1 %shard_map.70 = (f32[5,32,128]{2,1,0:T(8,128)S(1)}, f32[5,32,128]{2,1,0:T(8,128)S(1)}, f32[5,32,128]{2,1,0:T(8,128)S(1)}, f32[5,32,128]{2,1,0:T(8,128)S(1)}) custom-call(s32[3,40]{1,0:T(4,128)S(1)} %get-tuple-element.23.own_places.refs_0_, s32[3,40]{1,0:T(4,128)S(1)} %collective-permute-done.other_places.refs_1_, ...), custom_call_target="tpu_custom_call" | custom-call | flops 419430400 | bytes 5242880 | tf_op jit(solution)/shard_map/pallas_call | solution.py:189
  13.8 2.7 %collective-permute-start.8 = (f32[5,32,128]{2,1,0:T(8,128)S(1)}, f32[5,32,128]{2,1,0:T(8,128)S(1)}, u32[]{:S(2)}, u32[]{:S(2)}) collective-permute-start(f32[5,32,128]{2,1,0:T(8,128)S(1)} %get-tuple-element.35), channel_id=1, source_target_pairs={{0,4},{1,17},{2,6},{3,19},{4,0},{5,21},{6,2},{7,23},{8,12},{9,25},... | collective-permute-start | bytes 245768 | tf_op jit(solution)/shard_map/ppermute | solution.py:231
  16.4 1.3 %collective-permute-start.7 = (f32[5,32,128]{2,1,0:T(8,128)S(1)}, f32[5,32,128]{2,1,0:T(8,128)S(1)}, u32[]{:S(2)}, u32[]{:S(2)}) collective-permute-start(f32[5,32,128]{2,1,0:T(8,128)S(1)} %get-tuple-element.34), channel_id=1, source_target_pairs={{0,6},{1,25},{2,4},{3,27},{4,2},{5,29},{6,0},{7,31},{8,14},{9,17},... | collective-permute-start | bytes 245768 | tf_op jit(solution)/shard_map/ppermute | solution.py:231
  19.2 3.6 %collective-permute-done.7 = f32[5,32,128]{2,1,0:T(8,128)S(1)} collective-permute-done((f32[5,32,128]{2,1,0:T(8,128)S(1)}, f32[5,32,128]{2,1,0:T(8,128)S(1)}, u32[]{:S(2)}, u32[]{:S(2)}) %collective-permute-start.7) | collective-permute-done | bytes 81952 | tf_op jit(solution)/shard_map/ppermute | solution.py:231
  23.2 1.3 %collective-permute-done.9 = f32[5,32,128]{2,1,0:T(8,128)S(1)} collective-permute-done((f32[5,32,128]{2,1,0:T(8,128)S(1)}, f32[5,32,128]{2,1,0:T(8,128)S(1)}, u32[]{:S(2)}, u32[]{:S(2)}) %collective-permute-start.9) | collective-permute-done | bytes 81952 | tf_op jit(solution)/shard_map/ppermute | solution.py:234
  24.8 1.6 %collective-permute-start.10 = (f32[5,32,128]{2,1,0:T(8,128)S(1)}, f32[5,32,128]{2,1,0:T(8,128)S(1)}, u32[]{:S(2)}, u32[]{:S(2)}) collective-permute-start(f32[5,32,128]{2,1,0:T(8,128)S(1)} %pad_maximum_fusion.1.refs_4_), channel_id=1, source_target_pairs={{0,16},{1,5},{2,18},{3,7},{4,20},{5,1},{6,22},{7,3},{8,24},{9,13},... | collective-permute-start | bytes 245768 | tf_op jit(solution)/shard_map/ppermute | solution.py:231
  26.4 1.2 %collective-permute-start.11 = (f32[5,32,128]{2,1,0:T(8,128)S(1)}, f32[5,32,128]{2,1,0:T(8,128)S(1)}, u32[]{:S(2)}, u32[]{:S(2)}) collective-permute-start(f32[5,32,128]{2,1,0:T(8,128)S(1)} %pad_maximum_fusion.1.refs_4_), channel_id=1, source_target_pairs={{0,24},{1,7},{2,26},{3,5},{4,28},{5,3},{6,30},{7,1},{8,16},{9,15},... | collective-permute-start | bytes 245768 | tf_op jit(solution)/shard_map/ppermute | solution.py:231
  29.3 2.4 %collective-permute-done.11.refs_6_ = f32[5,32,128]{2,1,0:T(8,128)S(1)} collective-permute-done((f32[5,32,128]{2,1,0:T(8,128)S(1)}, f32[5,32,128]{2,1,0:T(8,128)S(1)}, u32[]{:S(2)}, u32[]{:S(2)}) %collective-permute-start.11) | collective-permute-done | bytes 81952 | tf_op jit(solution)/shard_map/ppermute | solution.py:231
  32.0 1.9 %shard_map.71 = (f32[5,32,128]{2,1,0:T(8,128)S(1)}, f32[5,32,128]{2,1,0:T(8,128)S(1)}, f32[5,32,128]{2,1,0:T(8,128)S(1)}, f32[5,32,128]{2,1,0:T(8,128)S(1)}) custom-call(s32[3,40]{1,0:T(4,128)S(1)} %get-tuple-element.23.own_places.refs_0_, s32[3,40]{1,0:T(4,128)S(1)} %collective-permute-done.other_places.refs_1_, ...), custom_call_target="tpu_custom_call" | custom-call | flops 335544320 | bytes 5242880 | tf_op jit(solution)/shard_map/pallas_call | solution.py:189
  33.9 1.5 %collective-permute-start.15 = (f32[5,32,128]{2,1,0:T(8,128)S(1)}, f32[5,32,128]{2,1,0:T(8,128)S(1)}, u32[]{:S(2)}, u32[]{:S(2)}) collective-permute-start(f32[5,32,128]{2,1,0:T(8,128)S(1)} %get-tuple-element.39), channel_id=1, source_target_pairs={{0,4},{1,17},{2,6},{3,19},{4,0},{5,21},{6,2},{7,23},{8,12},{9,25},... | collective-permute-start | bytes 245768 | tf_op jit(solution)/shard_map/ppermute | solution.py:231
  37.5 2.2 %collective-permute-done.15 = f32[5,32,128]{2,1,0:T(8,128)S(1)} collective-permute-done((f32[5,32,128]{2,1,0:T(8,128)S(1)}, f32[5,32,128]{2,1,0:T(8,128)S(1)}, u32[]{:S(2)}, u32[]{:S(2)}) %collective-permute-start.15) | collective-permute-done | bytes 81952 | tf_op jit(solution)/shard_map/ppermute | solution.py:231
  39.7 2.0 %collective-permute-done.14 = f32[5,32,128]{2,1,0:T(8,128)S(1)} collective-permute-done((f32[5,32,128]{2,1,0:T(8,128)S(1)}, f32[5,32,128]{2,1,0:T(8,128)S(1)}, u32[]{:S(2)}, u32[]{:S(2)}) %collective-permute-start.14) | collective-permute-done | bytes 81952 | tf_op jit(solution)/shard_map/ppermute | solution.py:231
  43.7 1.6 %collective-permute-start.17 = (f32[5,32,128]{2,1,0:T(8,128)S(1)}, f32[5,32,128]{2,1,0:T(8,128)S(1)}, u32[]{:S(2)}, u32[]{:S(2)}) collective-permute-start(f32[5,32,128]{2,1,0:T(8,128)S(1)} %pad_maximum_fusion.2.refs_4_), channel_id=1, source_target_pairs={{0,16},{1,5},{2,18},{3,7},{4,20},{5,1},{6,22},{7,3},{8,24},{9,13},... | collective-permute-start | bytes 245768 | tf_op jit(solution)/shard_map/ppermute | solution.py:231
  48.2 2.4 %collective-permute-done.18.refs_6_ = f32[5,32,128]{2,1,0:T(8,128)S(1)} collective-permute-done((f32[5,32,128]{2,1,0:T(8,128)S(1)}, f32[5,32,128]{2,1,0:T(8,128)S(1)}, u32[]{:S(2)}, u32[]{:S(2)}) %collective-permute-start.18) | collective-permute-done | bytes 81952 | tf_op jit(solution)/shard_map/ppermute | solution.py:231
  51.0 1.9 %shard_map.72 = (f32[5,32,128]{2,1,0:T(8,128)S(1)}, f32[5,32,128]{2,1,0:T(8,128)S(1)}, f32[5,32,128]{2,1,0:T(8,128)S(1)}, f32[5,32,128]{2,1,0:T(8,128)S(1)}) custom-call(s32[3,40]{1,0:T(4,128)S(1)} %get-tuple-element.23.own_places.refs_0_, s32[3,40]{1,0:T(4,128)S(1)} %collective-permute-done.other_places.refs_1_, ...), custom_call_target="tpu_custom_call" | custom-call | flops 335544320 | bytes 5242880 | tf_op jit(solution)/shard_map/pallas_call | solution.py:189
  53.3 1.5 %collective-permute-start.23 = (f32[5,32,128]{2,1,0:T(8,128)S(1)}, f32[5,32,128]{2,1,0:T(8,128)S(1)}, u32[]{:S(2)}, u32[]{:S(2)}) collective-permute-start(f32[5,32,128]{2,1,0:T(8,128)S(1)} %pad_maximum_fusion.5), channel_id=1, source_target_pairs={{0,4},{1,17},{2,6},{3,19},{4,0},{5,21},{6,2},{7,23},{8,12},{9,25},... | collective-permute-start | bytes 245768 | tf_op jit(solution)/shard_map/ppermute | solution.py:231
  54.8 1.2 %collective-permute-start.22 = (f32[5,32,128]{2,1,0:T(8,128)S(1)}, f32[5,32,128]{2,1,0:T(8,128)S(1)}, u32[]{:S(2)}, u32[]{:S(2)}) collective-permute-start(f32[5,32,128]{2,1,0:T(8,128)S(1)} %pad_maximum_fusion.4), channel_id=1, source_target_pairs={{0,6},{1,25},{2,4},{3,27},{4,2},{5,29},{6,0},{7,31},{8,14},{9,17},... | collective-permute-start | bytes 245768 | tf_op jit(solution)/shard_map/ppermute | solution.py:231
  56.9 2.4 %collective-permute-done.23 = f32[5,32,128]{2,1,0:T(8,128)S(1)} collective-permute-done((f32[5,32,128]{2,1,0:T(8,128)S(1)}, f32[5,32,128]{2,1,0:T(8,128)S(1)}, u32[]{:S(2)}, u32[]{:S(2)}) %collective-permute-start.23) | collective-permute-done | bytes 81952 | tf_op jit(solution)/shard_map/ppermute | solution.py:231
  59.3 1.9 %collective-permute-done.22 = f32[5,32,128]{2,1,0:T(8,128)S(1)} collective-permute-done((f32[5,32,128]{2,1,0:T(8,128)S(1)}, f32[5,32,128]{2,1,0:T(8,128)S(1)}, u32[]{:S(2)}, u32[]{:S(2)}) %collective-permute-start.22) | collective-permute-done | bytes 81952 | tf_op jit(solution)/shard_map/ppermute | solution.py:231
  61.4 1.9 %collective-permute-start.26 = (f32[32,128]{1,0:T(8,128)S(1)}, f32[32,128]{1,0:T(8,128)S(1)}, u32[]{:S(2)}, u32[]{:S(2)}) collective-permute-start(f32[32,128]{1,0:T(8,128)S(1)} %slice_bitcast_fusion), channel_id=1, source_target_pairs={{0,24},{1,7},{2,26},{3,5},{4,28},{5,3},{6,30},{7,1},{8,16},{9,15},... | collective-permute-start | bytes 49160 | tf_op jit(solution)/shard_map/ppermute | solution.py:231
  64.9 1.1 %collective-permute-done.26 = f32[32,128]{1,0:T(8,128)S(1)} collective-permute-done((f32[32,128]{1,0:T(8,128)S(1)}, f32[32,128]{1,0:T(8,128)S(1)}, u32[]{:S(2)}, u32[]{:S(2)}) %collective-permute-start.26) | collective-permute-done | bytes 16416 | tf_op jit(solution)/shard_map/ppermute | solution.py:231
  (84 shorter events, 21.0 us)
Async XLA Ops:
  2.6 5.2 %collective-permute-start.2 = (f32[40,128,128]{2,1,0:T(8,128)}, f32[40,128,128]{2,1,0:T(8,128)S(1)}, u32[]{:S(2)}, u32[]{:S(2)}) collective-permute-start(f32[40,128,128]{2,1,0:T(8,128)} %bitcast.7), channel_id=1, source_target_pairs={{0,1},{1,0},{2,3},{3,2},{4,5},{5,4},{6,7},{7,6},{8,9},{9,8},{10,11... | collective-permute-start | bytes 7864328 | tf_op jit(solution)/shard_map/ppermute | solution.py:234
  2.7 5.1 %collective-permute-start = (s32[3,40]{1,0:T(4,128)S(1)}, s32[3,40]{1,0:T(4,128)S(1)}, u32[]{:S(2)}, u32[]{:S(2)}) collective-permute-start(s32[3,40]{1,0:T(4,128)S(1)} %get-tuple-element.23.own_places.refs_0_), channel_id=1, source_target_pairs={{0,1},{1,0},{2,3},{3,2},{4,5},{5,4},{6,7},{7,6},{8,9},{9,8},{10,11... | collective-permute-start | bytes 1448 | tf_op jit(solution)/shard_map/ppermute | solution.py:234
  3.3 7.0 %collective-permute-start.3 = (f32[4,32,128]{2,1,0:T(8,128)S(1)}, f32[4,32,128]{2,1,0:T(8,128)S(1)}, u32[]{:S(2)}, u32[]{:S(2)}) collective-permute-start(f32[4,32,128]{2,1,0:T(8,128)S(1)} %maximum_select_fusion.refs_4_), channel_id=1, source_target_pairs={{0,16},{1,5},{2,18},{3,7},{4,20},{5,1},{6,22},{7,3},{8,24},{9,13},... | collective-permute-start | bytes 196616 | tf_op jit(solution)/shard_map/ppermute | solution.py:231
  5.9 5.2 %collective-permute-start.4 = (f32[4,32,128]{2,1,0:T(8,128)S(1)}, f32[4,32,128]{2,1,0:T(8,128)S(1)}, u32[]{:S(2)}, u32[]{:S(2)}) collective-permute-start(f32[4,32,128]{2,1,0:T(8,128)S(1)} %maximum_select_fusion.refs_4_), channel_id=1, source_target_pairs={{0,24},{1,7},{2,26},{3,5},{4,28},{5,3},{6,30},{7,1},{8,16},{9,15},... | collective-permute-start | bytes 196616 | tf_op jit(solution)/shard_map/ppermute | solution.py:231
  7.4 4.3 %collective-permute-start.5 = (f32[4,32,128]{2,1,0:T(8,128)S(1)}, f32[4,32,128]{2,1,0:T(8,128)S(1)}, u32[]{:S(2)}, u32[]{:S(2)}) collective-permute-start(f32[4,32,128]{2,1,0:T(8,128)S(1)} %maximum_select_fusion.refs_4_), channel_id=1, source_target_pairs={{0,8},{1,3},{2,10},{3,1},{4,12},{5,7},{6,14},{7,5},{8,0},{9,11},{1... | collective-permute-start | bytes 196616 | tf_op jit(solution)/shard_map/ppermute | solution.py:231
  13.8 5.4 %collective-permute-start.8 = (f32[5,32,128]{2,1,0:T(8,128)S(1)}, f32[5,32,128]{2,1,0:T(8,128)S(1)}, u32[]{:S(2)}, u32[]{:S(2)}) collective-permute-start(f32[5,32,128]{2,1,0:T(8,128)S(1)} %get-tuple-element.35), channel_id=1, source_target_pairs={{0,4},{1,17},{2,6},{3,19},{4,0},{5,21},{6,2},{7,23},{8,12},{9,25},... | collective-permute-start | bytes 245768 | tf_op jit(solution)/shard_map/ppermute | solution.py:231
  16.4 6.4 %collective-permute-start.7 = (f32[5,32,128]{2,1,0:T(8,128)S(1)}, f32[5,32,128]{2,1,0:T(8,128)S(1)}, u32[]{:S(2)}, u32[]{:S(2)}) collective-permute-start(f32[5,32,128]{2,1,0:T(8,128)S(1)} %get-tuple-element.34), channel_id=1, source_target_pairs={{0,6},{1,25},{2,4},{3,27},{4,2},{5,29},{6,0},{7,31},{8,14},{9,17},... | collective-permute-start | bytes 245768 | tf_op jit(solution)/shard_map/ppermute | solution.py:231
  17.8 5.3 %collective-permute-start.6 = (f32[5,32,128]{2,1,0:T(8,128)S(1)}, f32[5,32,128]{2,1,0:T(8,128)S(1)}, u32[]{:S(2)}, u32[]{:S(2)}) collective-permute-start(f32[5,32,128]{2,1,0:T(8,128)S(1)} %get-tuple-element.33), channel_id=1, source_target_pairs={{0,2},{1,9},{2,0},{3,11},{4,6},{5,13},{6,4},{7,15},{8,10},{9,1},{1... | collective-permute-start | bytes 245768 | tf_op jit(solution)/shard_map/ppermute | solution.py:231
  24.8 4.5 %collective-permute-start.10 = (f32[5,32,128]{2,1,0:T(8,128)S(1)}, f32[5,32,128]{2,1,0:T(8,128)S(1)}, u32[]{:S(2)}, u32[]{:S(2)}) collective-permute-start(f32[5,32,128]{2,1,0:T(8,128)S(1)} %pad_maximum_fusion.1.refs_4_), channel_id=1, source_target_pairs={{0,16},{1,5},{2,18},{3,7},{4,20},{5,1},{6,22},{7,3},{8,24},{9,13},... | collective-permute-start | bytes 245768 | tf_op jit(solution)/shard_map/ppermute | solution.py:231
  26.4 5.3 %collective-permute-start.11 = (f32[5,32,128]{2,1,0:T(8,128)S(1)}, f32[5,32,128]{2,1,0:T(8,128)S(1)}, u32[]{:S(2)}, u32[]{:S(2)}) collective-permute-start(f32[5,32,128]{2,1,0:T(8,128)S(1)} %pad_maximum_fusion.1.refs_4_), channel_id=1, source_target_pairs={{0,24},{1,7},{2,26},{3,5},{4,28},{5,3},{6,30},{7,1},{8,16},{9,15},... | collective-permute-start | bytes 245768 | tf_op jit(solution)/shard_map/ppermute | solution.py:231
  27.5 4.4 %collective-permute-start.12 = (f32[5,32,128]{2,1,0:T(8,128)S(1)}, f32[5,32,128]{2,1,0:T(8,128)S(1)}, u32[]{:S(2)}, u32[]{:S(2)}) collective-permute-start(f32[5,32,128]{2,1,0:T(8,128)S(1)} %pad_maximum_fusion.1.refs_4_), channel_id=1, source_target_pairs={{0,8},{1,3},{2,10},{3,1},{4,12},{5,7},{6,14},{7,5},{8,0},{9,11},{1... | collective-permute-start | bytes 245768 | tf_op jit(solution)/shard_map/ppermute | solution.py:231
  33.9 5.8 %collective-permute-start.15 = (f32[5,32,128]{2,1,0:T(8,128)S(1)}, f32[5,32,128]{2,1,0:T(8,128)S(1)}, u32[]{:S(2)}, u32[]{:S(2)}) collective-permute-start(f32[5,32,128]{2,1,0:T(8,128)S(1)} %get-tuple-element.39), channel_id=1, source_target_pairs={{0,4},{1,17},{2,6},{3,19},{4,0},{5,21},{6,2},{7,23},{8,12},{9,25},... | collective-permute-start | bytes 245768 | tf_op jit(solution)/shard_map/ppermute | solution.py:231
  35.4 6.3 %collective-permute-start.14 = (f32[5,32,128]{2,1,0:T(8,128)S(1)}, f32[5,32,128]{2,1,0:T(8,128)S(1)}, u32[]{:S(2)}, u32[]{:S(2)}) collective-permute-start(f32[5,32,128]{2,1,0:T(8,128)S(1)} %get-tuple-element.38), channel_id=1, source_target_pairs={{0,6},{1,25},{2,4},{3,27},{4,2},{5,29},{6,0},{7,31},{8,14},{9,17},... | collective-permute-start | bytes 245768 | tf_op jit(solution)/shard_map/ppermute | solution.py:231
  36.4 5.3 %collective-permute-start.13 = (f32[5,32,128]{2,1,0:T(8,128)S(1)}, f32[5,32,128]{2,1,0:T(8,128)S(1)}, u32[]{:S(2)}, u32[]{:S(2)}) collective-permute-start(f32[5,32,128]{2,1,0:T(8,128)S(1)} %get-tuple-element.37), channel_id=1, source_target_pairs={{0,2},{1,9},{2,0},{3,11},{4,6},{5,13},{6,4},{7,15},{8,10},{9,1},{1... | collective-permute-start | bytes 245768 | tf_op jit(solution)/shard_map/ppermute | solution.py:231
  43.7 4.5 %collective-permute-start.17 = (f32[5,32,128]{2,1,0:T(8,128)S(1)}, f32[5,32,128]{2,1,0:T(8,128)S(1)}, u32[]{:S(2)}, u32[]{:S(2)}) collective-permute-start(f32[5,32,128]{2,1,0:T(8,128)S(1)} %pad_maximum_fusion.2.refs_4_), channel_id=1, source_target_pairs={{0,16},{1,5},{2,18},{3,7},{4,20},{5,1},{6,22},{7,3},{8,24},{9,13},... | collective-permute-start | bytes 245768 | tf_op jit(solution)/shard_map/ppermute | solution.py:231
  45.2 5.3 %collective-permute-start.18 = (f32[5,32,128]{2,1,0:T(8,128)S(1)}, f32[5,32,128]{2,1,0:T(8,128)S(1)}, u32[]{:S(2)}, u32[]{:S(2)}) collective-permute-start(f32[5,32,128]{2,1,0:T(8,128)S(1)} %pad_maximum_fusion.2.refs_4_), channel_id=1, source_target_pairs={{0,24},{1,7},{2,26},{3,5},{4,28},{5,3},{6,30},{7,1},{8,16},{9,15},... | collective-permute-start | bytes 245768 | tf_op jit(solution)/shard_map/ppermute | solution.py:231
  46.3 4.4 %collective-permute-start.19 = (f32[5,32,128]{2,1,0:T(8,128)S(1)}, f32[5,32,128]{2,1,0:T(8,128)S(1)}, u32[]{:S(2)}, u32[]{:S(2)}) collective-permute-start(f32[5,32,128]{2,1,0:T(8,128)S(1)} %pad_maximum_fusion.2.refs_4_), channel_id=1, source_target_pairs={{0,8},{1,3},{2,10},{3,1},{4,12},{5,7},{6,14},{7,5},{8,0},{9,11},{1... | collective-permute-start | bytes 245768 | tf_op jit(solution)/shard_map/ppermute | solution.py:231
  53.3 6.0 %collective-permute-start.23 = (f32[5,32,128]{2,1,0:T(8,128)S(1)}, f32[5,32,128]{2,1,0:T(8,128)S(1)}, u32[]{:S(2)}, u32[]{:S(2)}) collective-permute-start(f32[5,32,128]{2,1,0:T(8,128)S(1)} %pad_maximum_fusion.5), channel_id=1, source_target_pairs={{0,4},{1,17},{2,6},{3,19},{4,0},{5,21},{6,2},{7,23},{8,12},{9,25},... | collective-permute-start | bytes 245768 | tf_op jit(solution)/shard_map/ppermute | solution.py:231
  54.8 6.3 %collective-permute-start.22 = (f32[5,32,128]{2,1,0:T(8,128)S(1)}, f32[5,32,128]{2,1,0:T(8,128)S(1)}, u32[]{:S(2)}, u32[]{:S(2)}) collective-permute-start(f32[5,32,128]{2,1,0:T(8,128)S(1)} %pad_maximum_fusion.4), channel_id=1, source_target_pairs={{0,6},{1,25},{2,4},{3,27},{4,2},{5,29},{6,0},{7,31},{8,14},{9,17},... | collective-permute-start | bytes 245768 | tf_op jit(solution)/shard_map/ppermute | solution.py:231
  56.0 5.3 %collective-permute-start.21 = (f32[5,32,128]{2,1,0:T(8,128)S(1)}, f32[5,32,128]{2,1,0:T(8,128)S(1)}, u32[]{:S(2)}, u32[]{:S(2)}) collective-permute-start(f32[5,32,128]{2,1,0:T(8,128)S(1)} %pad_maximum_fusion.3), channel_id=1, source_target_pairs={{0,2},{1,9},{2,0},{3,11},{4,6},{5,13},{6,4},{7,15},{8,10},{9,1},{1... | collective-permute-start | bytes 245768 | tf_op jit(solution)/shard_map/ppermute | solution.py:231
  61.4 4.7 %collective-permute-start.26 = (f32[32,128]{1,0:T(8,128)S(1)}, f32[32,128]{1,0:T(8,128)S(1)}, u32[]{:S(2)}, u32[]{:S(2)}) collective-permute-start(f32[32,128]{1,0:T(8,128)S(1)} %slice_bitcast_fusion), channel_id=1, source_target_pairs={{0,24},{1,7},{2,26},{3,5},{4,28},{5,3},{6,30},{7,1},{8,16},{9,15},... | collective-permute-start | bytes 49160 | tf_op jit(solution)/shard_map/ppermute | solution.py:231
  63.2 3.7 %collective-permute-start.25 = (f32[32,128]{1,0:T(8,128)S(1)}, f32[32,128]{1,0:T(8,128)S(1)}, u32[]{:S(2)}, u32[]{:S(2)}) collective-permute-start(f32[32,128]{1,0:T(8,128)S(1)} %slice_bitcast_fusion), channel_id=1, source_target_pairs={{0,16},{1,5},{2,18},{3,7},{4,20},{5,1},{6,22},{7,3},{8,24},{9,13},... | collective-permute-start | bytes 49160 | tf_op jit(solution)/shard_map/ppermute | solution.py:231
  63.8 3.7 %collective-permute-start.24 = (f32[32,128]{1,0:T(8,128)S(1)}, f32[32,128]{1,0:T(8,128)S(1)}, u32[]{:S(2)}, u32[]{:S(2)}) collective-permute-start(f32[32,128]{1,0:T(8,128)S(1)} %slice_bitcast_fusion), channel_id=1, source_target_pairs={{0,8},{1,3},{2,10},{3,1},{4,12},{5,7},{6,14},{7,5},{8,0},{9,11},{1... | collective-permute-start | bytes 49160 | tf_op jit(solution)/shard_map/ppermute | solution.py:231
  64.9 3.1 %collective-permute-start.27 = (f32[4,32,128]{2,1,0:T(8,128)S(1)}, f32[4,32,128]{2,1,0:T(8,128)S(1)}, u32[]{:S(2)}, u32[]{:S(2)}) collective-permute-start(f32[4,32,128]{2,1,0:T(8,128)S(1)} %slice.186), channel_id=1, source_target_pairs={{0,1},{1,0},{2,3},{3,2},{4,5},{5,4},{6,7},{7,6},{8,9},{9,8},{10,11... | collective-permute-start | bytes 196616 | tf_op jit(solution)/shard_map/ppermute | solution.py:234
  (5 other events, 19.7 us)

commit v5 on v4

--- a/solution.py
+++ b/solution.py
@@ -32,13 +32,13 @@
     v = index_ref[0, 0, 1:2]
     out_ref[0:1] = ((u >> per_bits) ^ line) * per + (u & (per - 1))
     out_ref[1:2] = ((v >> seg_bits) ^ row) * per + core * seg + (v & (seg - 1))
-    out_ref[2:3] = jnp.zeros_like(u) + count_ref[0, 0]
+    out_ref[2:3] = jnp.broadcast_to(count_ref[...], u.shape)
 
 
 def find_places(block_index, block_count, raw):
     return pl.pallas_call(
         functools.partial(places_kernel, raw.shape[0]),
-        in_specs=[VMEM, SMEM, VMEM],
+        in_specs=[VMEM, VMEM, VMEM],
         out_specs=[VMEM, VMEM],
         out_shape=[
             pltpu.VMEM((3, block_index.shape[3]), jnp.int32),
@@ -101,7 +101,7 @@
             pltpu.VMEM((slots, size, size), F32),
             pltpu.SemaphoreType.DMA((slots // COPY,)),
         ],
-        compiler_params=pltpu.CompilerParams(vmem_limit_bytes=32 * 2**20),
+        compiler_params=pltpu.CompilerParams(vmem_limit_bytes=16 * 2**20),
         cost_estimate=pl.CostEstimate(
             flops=slots * size * size * 8, bytes_accessed=slots * size * size * 16, transcendentals=0
         ),
@@ -113,18 +113,18 @@
     )
 
 
-def apply_kernel(parts, with_degree, with_aux, *refs):
+def apply_kernel(parts, per, width, with_degree, *refs):
     own_places, other_places, own_ref, other_ref = refs[:4]
     fields = [refs[4]] + [None] * (parts - 1)
     for part, ref in zip(far_first(parts), refs[5:]):
         fields[part] = ref
     outs = refs[4 + parts : 4 + 2 * parts]
     stack_ref, sum_ref = refs[4 + 2 * parts :]
-    per = outs[0].shape[0] - 1
-    width, size = fields[0].shape[1:]
+    size = fields[0].shape[1]
+    deep = per * width
     for part in range(parts):
         for j in range(per):
-            x = fields[part][j]
+            x = fields[part][j * width : (j + 1) * width]
             high = x.astype(BF)
             low = (x - high.astype(F32)).astype(BF)
             f = part * per + j
@@ -139,12 +139,10 @@
     run = own_ref.shape[0]
 
     def sweep(values_ref, places):
-        count = places[2, 0]
-
-        def group(g, carry):
+        @pl.when(places[2, 0] > 0)
+        def _():
             products = []
-            for i in range(run):
-                q = g * run + i
+            for q in range(run):
                 products.append(
                     jnp.dot(
                         stack_ref[places[1 - core, q]],
@@ -152,50 +150,48 @@
                         preferred_element_type=F32,
                     )
                 )
-            for i in range(run):
-                to = places[core, g * run + i]
-                whole = products[i]
+            for q in range(run):
+                to = places[core, q]
+                whole = products[q]
                 sum_ref[to, :width] += whole[:width] + whole[width : 2 * width]
                 if with_degree:
                     sum_ref[to, width:] += whole[2 * width : 2 * width + 8]
-            return carry
-
-        lax.fori_loop(0, (count + run - 1) // run, group, 0)
 
     sweep(own_ref, own_places)
     sweep(other_ref, other_places)
-    if with_aux:
-        aux = fields[0][per]
+    if not with_degree:
+        aux = fields[0][deep:]
         for part in range(1, parts):
-            aux = aux + fields[part][per]
+            aux = aux + fields[part][deep:]
     for part in range(parts):
         for j in range(per):
-            outs[part][j] = sum_ref[part * per + j, :width]
-        if with_aux:
-            outs[part][per] = aux
+            outs[part][j * width : (j + 1) * width] = sum_ref[part * per + j, :width]
+        if with_degree:
+            outs[part][deep:] = jnp.zeros((8, size), F32)
+            for j in range(per):
+                row = deep + j
+                outs[part][row : row + 1] = sum_ref[part * per + j, width : width + 1]
         else:
-            outs[part][per] = jnp.zeros((width, size), F32)
-            for j in range(per):
-                outs[part][per, j : j + 1, :] = sum_ref[part * per + j, width : width + 1]
-
-
-def apply_blocks(matrix, fields, with_degree, with_aux):
+            outs[part][deep:] = aux
+
+
+def apply_blocks(matrix, fields, per, width, with_degree):
     parts = len(fields)
-    width, size = fields[0].shape[1:]
-    per = fields[0].shape[0] - (1 if with_aux else 0)
+    size = fields[0].shape[1]
+    extra = 8 if with_degree else fields[0].shape[0] - per * width
     rows = 2 * width + (16 if with_degree else 0)
     sums = width + (8 if with_degree else 0)
     slots = matrix[2].shape[0]
     return pl.pallas_call(
-        functools.partial(apply_kernel, parts, with_degree, with_aux),
+        functools.partial(apply_kernel, parts, per, width, with_degree),
         in_specs=[SMEM] * 2 + [VMEM] * (2 + parts),
         out_specs=[VMEM] * parts,
-        out_shape=[jax.ShapeDtypeStruct((per + 1, width, size), F32)] * parts,
+        out_shape=[jax.ShapeDtypeStruct((per * width + extra, size), F32)] * parts,
         scratch_shapes=[
             pltpu.VMEM((parts * per, rows, 2 * size), BF),
             pltpu.VMEM((parts * per, sums, size), F32),
         ],
-        compiler_params=pltpu.CompilerParams(vmem_limit_bytes=40 * 2**20),
+        compiler_params=pltpu.CompilerParams(vmem_limit_bytes=16 * 2**20),
         cost_estimate=pl.CostEstimate(
             flops=2 * slots * 4 * rows * size * size,
             bytes_accessed=4 * slots * size * size * 2,
@@ -204,16 +200,94 @@
     )(*matrix, fields[0], *(fields[part] for part in far_first(parts)))
 
 
-def dots(*pairs):
-    lane = lax.broadcasted_iota(jnp.int32, pairs[0][0].shape[1:], 1)
-    aux = jnp.zeros(pairs[0][0].shape[1:], F32)
+def dot_rows(pairs, depth):
+    width, size = pairs[0][0][0].shape
+    lane = lax.broadcasted_iota(jnp.int32, (width, size), 1)
+    table = jnp.zeros((width, size), F32)
     for n, (a, b) in enumerate(pairs):
-        aux = jnp.where(lane == n, jnp.sum(a * b, axis=(0, 2))[:, None], aux)
-    return aux
-
-
-def lane_of(aux, n):
-    return aux[None, :, n : n + 1]
+        product = a[0] * b[0]
+        for x, y in zip(a[1:], b[1:]):
+            product = product + x * y
+        table = jnp.where(lane == n, jnp.sum(product, axis=1, keepdims=True), table)
+    square = jnp.concatenate([table, jnp.zeros((size - width, size), F32)], axis=0)
+    return square.T[:depth]
+
+
+def blocks_in(ref, per, width):
+    return [ref[j * width : (j + 1) * width] for j in range(per)]
+
+
+def put(ref, blocks):
+    width = blocks[0].shape[0]
+    for j, block in enumerate(blocks):
+        ref[j * width : (j + 1) * width] = block
+
+
+def first_update(per, mine, other, raw_ref, gain_ref, w0_out, degree_out, sent_out):
+    width = raw_ref.shape[0] // per
+    deep = per * width
+    raw = blocks_in(raw_ref, per, width)
+    degree = mine[deep:] + other[deep:]
+    degree_out[...] = degree
+    gain = gain_ref[...]
+    w0 = []
+    for j in range(per):
+        cut = slice(j * width, (j + 1) * width)
+        product = mine[cut] + other[cut]
+        w0.append(raw[j] + gain * (degree[j : j + 1] * raw[j] - product))
+    put(w0_out, w0)
+    put(sent_out, w0)
+    sent_out[deep:] = dot_rows([(raw, raw), (raw, w0)], sent_out.shape[0] - deep)
+
+
+def second_update(per, mine, other, raw_ref, w0_ref, degree_ref, gain_ref, q0_out, r1_out, w1_out, sent_out):
+    width = raw_ref.shape[0] // per
+    deep = per * width
+    raw, w0 = blocks_in(raw_ref, per, width), blocks_in(w0_ref, per, width)
+    totals = jnp.concatenate(
+        [mine[deep:], jnp.zeros((mine.shape[1] - mine.shape[0] + deep, mine.shape[1]), F32)]
+    ).T[:width]
+    step0 = totals[:, 0:1] / totals[:, 1:2]
+    degree, gain = degree_ref[...], gain_ref[...]
+    q0, r1, w1, h, dh = [], [], [], [], []
+    for j in range(per):
+        cut = slice(j * width, (j + 1) * width)
+        product = mine[cut] + other[cut]
+        q0.append(w0[j] + gain * (degree[j : j + 1] * w0[j] - product))
+        r1.append(raw[j] - step0 * w0[j])
+        w1.append(w0[j] - step0 * q0[j])
+        h.append(r1[j] - step0 * w1[j])
+        dh.append(degree[j : j + 1] * h[j])
+    put(q0_out, q0)
+    put(r1_out, r1)
+    put(w1_out, w1)
+    put(sent_out, h)
+    pairs = (
+        (r1, r1),
+        (r1, w1),
+        (r1, w0),
+        (h, h),
+        (h, w1),
+        (h, w0),
+        (w1, w1),
+        (w1, w0),
+        (w0, w0),
+        (h, q0),
+        (w1, q0),
+        (w0, q0),
+        (dh, h),
+    )
+    sent_out[deep:] = dot_rows(pairs, sent_out.shape[0] - deep)
+
+
+def update(kernel, per, shapes, *arrays):
+    return pl.pallas_call(
+        functools.partial(kernel, per),
+        in_specs=[VMEM] * len(arrays),
+        out_specs=[VMEM] * len(shapes),
+        out_shape=[pltpu.VMEM(shape, F32) for shape in shapes],
+        compiler_params=pltpu.CompilerParams(vmem_limit_bytes=16 * 2**20),
+    )(*arrays)
 
 
 def build(n_row, n_col):
@@ -258,66 +332,74 @@
         )
         places_other = swap(places)
         gains = strength[None, :, None]
-        gathered = gather(raw)
+        gathered = gather(raw.reshape(per * raw.shape[1], raw.shape[2]))
         values, values_other = lax.optimization_barrier((values, values_other))
         matrix = (places, places_other) + tuple(
             split_blocks(places, places_other, values, values_other)
         )
 
-        mine = collect(apply_blocks(matrix, gathered, True, False))
-        both = mine + swap(mine)
-        degree = both[per, :per, None, :]
-        w0 = raw + gains * (degree * raw - both[:per])
-
-        def with_aux(field, *pairs):
-            return jnp.concatenate([field, dots(*pairs)[None]])
-
-        mine = collect(
-            apply_blocks(matrix, gather(with_aux(w0, (raw, raw), (raw, w0))), False, True)
-        )
-        sums = mine[per]
-        product = mine[:per] + swap(mine[:per])
-        q0 = w0 + gains * (degree * w0 - product)
-        gamma0, delta0 = lane_of(sums, 0), lane_of(sums, 1)
+        width, size = raw.shape[1:]
+        deep = per * width
+
+        def blocks(array):
+            return array[:deep].reshape(per, width, size)
+
+        def row_of(aux, n):
+            return aux[n, :width][None, :, None]
+
+        flat = raw.reshape(deep, size)
+        gain_rows = jnp.broadcast_to(strength[:, None], (width, size))
+        deep_shape, aux_rows = (deep, size), 16
+
+        mine = collect(apply_blocks(matrix, gathered, per, width, True))
+        w0, degree, sent = update(
+            first_update,
+            per,
+            (deep_shape, (8, size), (deep + aux_rows, size)),
+            mine,
+            swap(mine),
+            flat,
+            gain_rows,
+        )
+
+        mine = collect(apply_blocks(matrix, gather(sent), per, width, False))
+        gamma0, delta0 = row_of(mine[deep:], 0), row_of(mine[deep:], 1)
         step0 = gamma0 / delta0
-        r1 = raw - step0 * w0
-        w1 = w0 - step0 * q0
-        h = r1 - step0 * w1
-
-        pairs = (
-            (r1, r1),
-            (r1, w1),
-            (r1, w0),
-            (h, h),
-            (h, w1),
-            (h, w0),
-            (w1, w1),
-            (w1, w0),
-            (w0, w0),
-            (h, q0),
-            (w1, q0),
-            (w0, q0),
-            (degree * h, h),
-        )
-        gathered = gather(with_aux(h, *pairs))
-        crossed = swap(jnp.concatenate(gathered[1:]))
-        crossed = [gathered[0]] + jnp.split(crossed, parts - 1)
-        sent = apply_blocks(matrix, gathered, False, True)
+        q0, r1, w1, sent = update(
+            second_update,
+            per,
+            (deep_shape,) * 3 + ((deep + aux_rows, size),),
+            mine,
+            swap(mine[:deep]),
+            flat,
+            w0,
+            degree,
+            gain_rows,
+        )
+        h = blocks(sent)
+        w0, q0, r1, w1 = blocks(w0), blocks(q0), blocks(r1), blocks(w1)
+        degree = degree[:per, None, :]
+        n_pairs = 13
+        gathered = gather(sent)
+        crossed = swap(jnp.concatenate([part[:deep] for part in gathered[1:]]))
+        crossed = [gathered[0][:deep]] + jnp.split(crossed, parts - 1)
+        sent = apply_blocks(matrix, gathered, per, width, False)
         cross = sum(
-            jnp.sum(out[:per] * part[:per], axis=(0, 2)) for out, part in zip(sent, crossed)
-        )
-        lane = lax.broadcasted_iota(jnp.int32, h.shape[1:], 1)
-        cross = jnp.where(lane == len(pairs), cross[:, None], 0.0)
-        sent = [jnp.concatenate([out[:per], (out[per] + cross)[None]]) for out in sent]
-        mine = collect(sent)
-        sums = mine[per]
+            jnp.sum(blocks(out) * blocks(part), axis=(0, 2)) for out, part in zip(sent, crossed)
+        )
+        after = sent[0].shape[0] - deep - n_pairs - 1
+        cross = lax.pad(
+            cross[None], 0.0, ((deep + n_pairs, after, 0), (0, size - width, 0))
+        )
+        mine = collect([out + cross for out in sent])
+        sums = mine[deep:]
         tail = sum(gather(sums))
-        product = mine[:per] + swap(mine[:per])
+        product = blocks(mine) + blocks(swap(mine[:deep]))
         qh = h + gains * (degree * h - product)
         g11, r1w1, r1w0, hh, hw1, hw0, w11, w10, w00, a_h0, a_10, a_00, hdh = (
-            lane_of(sums, n) for n in range(len(pairs))
-        )
-        a_hh = hh + gains * (hdh - 2.0 * lane_of(tail, len(pairs)))
+            row_of(sums, n) for n in range(n_pairs)
+        )
+        a_hh = hh + gains * (hdh - 2.0 * row_of(tail, n_pairs))
         ratio0 = g11 / gamma0
         curve1 = r1w1 + 2.0 * ratio0 * r1w0 + ratio0 * ratio0 * delta0
         step1 = g11 / curve1

time: 69.3 us -> 67.7 us (0.977)
  other arithmetic: 2.69 us -> 1.29 us
  waiting for transfers between devices: 27.4 us -> 26.1 us
  Pallas kernels: 9.26 us -> 10 us
    ppermute x21, waiting for transfers between devices: 24.8 us -> 22.8 us  [joint(): return lax.ppermute(array, ('row', 'col'), pairs)]
    ppermute x7, waiting for transfers between devices: 2.62 us -> 3.32 us  [swap(): return lax.ppermute(array, 'col', [(c, c ^ 1) for c in range(n_col)])]
    pallas_call x3 -> x5, Pallas kernels: 5.99 us -> 6.55 us  [the longest x3 5.99 us: apply_blocks(): pl.pallas_call(functools.partial(apply_kernel, parts, per, width, with_de...]
  transfers between devices with their start and end apart: 28 -> 28, of which waited for: 22 -> 21; matrix products, arithmetic and copies ran while one was open for 1% -> 0% of each run, Pallas kernels for 8% -> 8%
where the time goes in v5:
time: 67.7 us; the launch traced here: 67.4 us
  starting transfers between devices  28.1 us (42%)
  waiting for transfers between devices  26.1 us (39%)
  Pallas kernels  10 us (15%)
  between operations  1.48 us (2%)
  other arithmetic  1.29 us (2%)
    ppermute x21, starting transfers between devices, joint(): return lax.ppermute(array, ('row', 'col'), pairs)  26.7 us
    ppermute x21, waiting for transfers between devices, joint(): return lax.ppermute(array, ('row', 'col'), pairs)  22.8 us
    pallas_call x3, Pallas kernels, apply_blocks(): pl.pallas_call(functools.partial(apply_kernel, parts, per, width, with_de...  5.99 us
    ppermute x7, waiting for transfers between devices, swap(): return lax.ppermute(array, 'col', [(c, c ^ 1) for c in range(n_col)])  3.32 us
    pallas_call x1, Pallas kernels, split_blocks(): pl.pallas_call(split_kernel, in_specs=[SMEM, SMEM, pl.BlockSpec(memory_sp...  2.62 us
    ppermute x7, starting transfers between devices, swap(): return lax.ppermute(array, 'col', [(c, c ^ 1) for c in range(n_col)])  1.45 us
  transfers between devices with their start and end apart: 28, of which 21 were waited for; matrix products, arithmetic and copies ran while one was open for 0% of the time, Pallas kernels for 8%

profile of v5, /device:TPU:0, one launch (start us, length us, event | category | flops | bytes accessed | tf_op | source)
XLA Modules:
  0.0 67.4 jit_solution(6925937478020202818)
XLA Ops:
  2.7 3.0 %collective-permute-start.3 = (f32[128,128]{1,0:T(8,128)S(1)}, f32[128,128]{1,0:T(8,128)S(1)}, u32[]{:S(2)}, u32[]{:S(2)}) collective-permute-start(f32[128,128]{1,0:T(8,128)S(1)} %bitcast.129), channel_id=1, source_target_pairs={{0,16},{1,5},{2,18},{3,7},{4,20},{5,1},{6,22},{7,3},{8,24},{9,13},... | collective-permute-start | bytes 196616 | tf_op jit(solution)/shard_map/ppermute | solution.py:305
  5.8 1.4 %collective-permute-start.4 = (f32[128,128]{1,0:T(8,128)S(1)}, f32[128,128]{1,0:T(8,128)S(1)}, u32[]{:S(2)}, u32[]{:S(2)}) collective-permute-start(f32[128,128]{1,0:T(8,128)S(1)} %bitcast.130), channel_id=1, source_target_pairs={{0,24},{1,7},{2,26},{3,5},{4,28},{5,3},{6,30},{7,1},{8,16},{9,15},... | collective-permute-start | bytes 196616 | tf_op jit(solution)/shard_map/ppermute | solution.py:305
  8.7 2.6 %shard_map.69 = (bf16[40,256,128]{2,1,0:T(8,128)(2,1)S(1)}, bf16[40,256,128]{2,1,0:T(8,128)(2,1)S(1)}) custom-call(s32[3,40]{1,0:T(4,128)S(1)} %get-tuple-element.30.own_places.refs_0_, s32[3,40]{1,0:T(4,128)S(1)} %collective-permute-done.other_places.refs_1_, f32[40,128,128]{2,1,0:T(8,128)} %bitcast.140, f32[40,128,128]{2,1,0:T(8,128)S(1)} %collective-permute-done.2.other_in), custom_call_target="tpu_custom_call" | custom-call | flops 5242880 | bytes 10485760 | tf_op jit(solution)/shard_map/pallas_call | solution.py:95
  11.5 2.1 %shard_map.70 = (f32[136,128]{1,0:T(8,128)S(1)}, f32[136,128]{1,0:T(8,128)S(1)}, f32[136,128]{1,0:T(8,128)S(1)}, f32[136,128]{1,0:T(8,128)S(1)}) custom-call(s32[3,40]{1,0:T(4,128)S(1)} %get-tuple-element.30.own_places.refs_0_, s32[3,40]{1,0:T(4,128)S(1)} %collective-permute-done.other_places.refs_1_, bf16[40,256,128]{2,1,0:T(8,128)(2,1)S(1)} %get-tuple-element.35.refs_2_, ...), custom_call_target="tpu_custom_call" | custom-call | flops 419430400 | bytes 5242880 | tf_op jit(solution)/shard_map/pallas_call | solution.py:185
  13.6 2.6 %collective-permute-start.8 = (f32[136,128]{1,0:T(8,128)S(1)}, f32[136,128]{1,0:T(8,128)S(1)}, u32[]{:S(2)}, u32[]{:S(2)}) collective-permute-start(f32[136,128]{1,0:T(8,128)S(1)} %get-tuple-element.42), channel_id=1, source_target_pairs={{0,4},{1,17},{2,6},{3,19},{4,0},{5,21},{6,2},{7,23},{8,12},{9,25},... | collective-permute-start | bytes 208904 | tf_op jit(solution)/shard_map/ppermute | solution.py:305
  16.2 1.5 %collective-permute-start.7 = (f32[136,128]{1,0:T(8,128)S(1)}, f32[136,128]{1,0:T(8,128)S(1)}, u32[]{:S(2)}, u32[]{:S(2)}) collective-permute-start(f32[136,128]{1,0:T(8,128)S(1)} %get-tuple-element.41), channel_id=1, source_target_pairs={{0,6},{1,25},{2,4},{3,27},{4,2},{5,29},{6,0},{7,31},{8,14},{9,17},... | collective-permute-start | bytes 208904 | tf_op jit(solution)/shard_map/ppermute | solution.py:305
  18.8 3.6 %collective-permute-done.7 = f32[136,128]{1,0:T(8,128)S(1)} collective-permute-done((f32[136,128]{1,0:T(8,128)S(1)}, f32[136,128]{1,0:T(8,128)S(1)}, u32[]{:S(2)}, u32[]{:S(2)}) %collective-permute-start.7) | collective-permute-done | bytes 69664 | tf_op jit(solution)/shard_map/ppermute | solution.py:305
  22.9 1.2 %collective-permute-done.9.other = f32[136,128]{1,0:T(8,128)S(1)} collective-permute-done((f32[136,128]{1,0:T(8,128)S(1)}, f32[136,128]{1,0:T(8,128)S(1)}, u32[]{:S(2)}, u32[]{:S(2)}) %collective-permute-start.9) | collective-permute-done | bytes 69664 | tf_op jit(solution)/shard_map/ppermute | solution.py:308
  24.3 1.4 %collective-permute-start.10 = (f32[144,128]{1,0:T(8,128)S(1)}, f32[144,128]{1,0:T(8,128)S(1)}, u32[]{:S(2)}, u32[]{:S(2)}) collective-permute-start(f32[144,128]{1,0:T(8,128)S(1)} %get-tuple-element.43.refs_4_), channel_id=1, source_target_pairs={{0,16},{1,5},{2,18},{3,7},{4,20},{5,1},{6,22},{7,3},{8,24},{9,13},... | collective-permute-start | bytes 221192 | tf_op jit(solution)/shard_map/ppermute | solution.py:305
  25.8 1.3 %collective-permute-start.11 = (f32[144,128]{1,0:T(8,128)S(1)}, f32[144,128]{1,0:T(8,128)S(1)}, u32[]{:S(2)}, u32[]{:S(2)}) collective-permute-start(f32[144,128]{1,0:T(8,128)S(1)} %get-tuple-element.43.refs_4_), channel_id=1, source_target_pairs={{0,24},{1,7},{2,26},{3,5},{4,28},{5,3},{6,30},{7,1},{8,16},{9,15},... | collective-permute-start | bytes 221192 | tf_op jit(solution)/shard_map/ppermute | solution.py:305
  28.7 2.3 %collective-permute-done.11.refs_6_ = f32[144,128]{1,0:T(8,128)S(1)} collective-permute-done((f32[144,128]{1,0:T(8,128)S(1)}, f32[144,128]{1,0:T(8,128)S(1)}, u32[]{:S(2)}, u32[]{:S(2)}) %collective-permute-start.11) | collective-permute-done | bytes 73760 | tf_op jit(solution)/shard_map/ppermute | solution.py:305
  31.4 1.9 %shard_map.72 = (f32[144,128]{1,0:T(8,128)S(1)}, f32[144,128]{1,0:T(8,128)S(1)}, f32[144,128]{1,0:T(8,128)S(1)}, f32[144,128]{1,0:T(8,128)S(1)}) custom-call(s32[3,40]{1,0:T(4,128)S(1)} %get-tuple-element.30.own_places.refs_0_, s32[3,40]{1,0:T(4,128)S(1)} %collective-permute-done.other_places.refs_1_, bf16[40,256,128]{2,1,0:T(8,128)(2,1)S(1)} %get-tuple-element.35.refs_2_, ...), custom_call_target="tpu_custom_call" | custom-call | flops 335544320 | bytes 5242880 | tf_op jit(solution)/shard_map/pallas_call | solution.py:185
  33.4 1.3 %collective-permute-start.15 = (f32[144,128]{1,0:T(8,128)S(1)}, f32[144,128]{1,0:T(8,128)S(1)}, u32[]{:S(2)}, u32[]{:S(2)}) collective-permute-start(f32[144,128]{1,0:T(8,128)S(1)} %get-tuple-element.47), channel_id=1, source_target_pairs={{0,4},{1,17},{2,6},{3,19},{4,0},{5,21},{6,2},{7,23},{8,12},{9,25},... | collective-permute-start | bytes 221192 | tf_op jit(solution)/shard_map/ppermute | solution.py:305
  36.9 2.0 %collective-permute-done.15 = f32[144,128]{1,0:T(8,128)S(1)} collective-permute-done((f32[144,128]{1,0:T(8,128)S(1)}, f32[144,128]{1,0:T(8,128)S(1)}, u32[]{:S(2)}, u32[]{:S(2)}) %collective-permute-start.15) | collective-permute-done | bytes 73760 | tf_op jit(solution)/shard_map/ppermute | solution.py:305
  38.9 2.0 %collective-permute-done.14 = f32[144,128]{1,0:T(8,128)S(1)} collective-permute-done((f32[144,128]{1,0:T(8,128)S(1)}, f32[144,128]{1,0:T(8,128)S(1)}, u32[]{:S(2)}, u32[]{:S(2)}) %collective-permute-start.14) | collective-permute-done | bytes 73760 | tf_op jit(solution)/shard_map/ppermute | solution.py:305
  41.1 1.2 %collective-permute-done.16.other = f32[128,128]{1,0:T(8,128)S(1)} collective-permute-done((f32[128,128]{1,0:T(8,128)S(1)}, f32[128,128]{1,0:T(8,128)S(1)}, u32[]{:S(2)}, u32[]{:S(2)}) %collective-permute-start.16) | collective-permute-done | bytes 65568 | tf_op jit(solution)/shard_map/ppermute | solution.py:308
  42.7 1.8 %collective-permute-start.18 = (f32[144,128]{1,0:T(8,128)S(1)}, f32[144,128]{1,0:T(8,128)S(1)}, u32[]{:S(2)}, u32[]{:S(2)}) collective-permute-start(f32[144,128]{1,0:T(8,128)S(1)} %get-tuple-element.50.refs_4_), channel_id=1, source_target_pairs={{0,24},{1,7},{2,26},{3,5},{4,28},{5,3},{6,30},{7,1},{8,16},{9,15},... | collective-permute-start | bytes 221192 | tf_op jit(solution)/shard_map/ppermute | solution.py:305
  46.2 1.8 %collective-permute-done.18.refs_6_ = f32[144,128]{1,0:T(8,128)S(1)} collective-permute-done((f32[144,128]{1,0:T(8,128)S(1)}, f32[144,128]{1,0:T(8,128)S(1)}, u32[]{:S(2)}, u32[]{:S(2)}) %collective-permute-start.18) | collective-permute-done | bytes 73760 | tf_op jit(solution)/shard_map/ppermute | solution.py:305
  49.7 1.9 %shard_map.74 = (f32[144,128]{1,0:T(8,128)S(1)}, f32[144,128]{1,0:T(8,128)S(1)}, f32[144,128]{1,0:T(8,128)S(1)}, f32[144,128]{1,0:T(8,128)S(1)}) custom-call(s32[3,40]{1,0:T(4,128)S(1)} %get-tuple-element.30.own_places.refs_0_, s32[3,40]{1,0:T(4,128)S(1)} %collective-permute-done.other_places.refs_1_, bf16[40,256,128]{2,1,0:T(8,128)(2,1)S(1)} %get-tuple-element.35.refs_2_, ...), custom_call_target="tpu_custom_call" | custom-call | flops 335544320 | bytes 5242880 | tf_op jit(solution)/shard_map/pallas_call | solution.py:185
  52.4 1.2 %collective-permute-start.23 = (f32[144,128]{1,0:T(8,128)S(1)}, f32[144,128]{1,0:T(8,128)S(1)}, u32[]{:S(2)}, u32[]{:S(2)}) collective-permute-start(f32[144,128]{1,0:T(8,128)S(1)} %get-tuple-element.75), channel_id=1, source_target_pairs={{0,4},{1,17},{2,6},{3,19},{4,0},{5,21},{6,2},{7,23},{8,12},{9,25},... | collective-permute-start | bytes 221192 | tf_op jit(solution)/shard_map/ppermute | solution.py:305
  53.6 1.5 %collective-permute-start.22 = (f32[144,128]{1,0:T(8,128)S(1)}, f32[144,128]{1,0:T(8,128)S(1)}, u32[]{:S(2)}, u32[]{:S(2)}) collective-permute-start(f32[144,128]{1,0:T(8,128)S(1)} %get-tuple-element.74), channel_id=1, source_target_pairs={{0,6},{1,25},{2,4},{3,27},{4,2},{5,29},{6,0},{7,31},{8,14},{9,17},... | collective-permute-start | bytes 221192 | tf_op jit(solution)/shard_map/ppermute | solution.py:305
  56.0 2.3 %collective-permute-done.23 = f32[144,128]{1,0:T(8,128)S(1)} collective-permute-done((f32[144,128]{1,0:T(8,128)S(1)}, f32[144,128]{1,0:T(8,128)S(1)}, u32[]{:S(2)}, u32[]{:S(2)}) %collective-permute-start.23) | collective-permute-done | bytes 73760 | tf_op jit(solution)/shard_map/ppermute | solution.py:305
  58.3 1.6 %collective-permute-done.22 = f32[144,128]{1,0:T(8,128)S(1)} collective-permute-done((f32[144,128]{1,0:T(8,128)S(1)}, f32[144,128]{1,0:T(8,128)S(1)}, u32[]{:S(2)}, u32[]{:S(2)}) %collective-permute-start.22) | collective-permute-done | bytes 73760 | tf_op jit(solution)/shard_map/ppermute | solution.py:305
  60.4 2.1 %collective-permute-start.26 = (f32[16,128]{1,0:T(8,128)S(1)}, f32[16,128]{1,0:T(8,128)S(1)}, u32[]{:S(2)}, u32[]{:S(2)}) collective-permute-start(f32[16,128]{1,0:T(8,128)S(1)} %slice.163), channel_id=1, source_target_pairs={{0,24},{1,7},{2,26},{3,5},{4,28},{5,3},{6,30},{7,1},{8,16},{9,15},... | collective-permute-start | bytes 24584 | tf_op jit(solution)/shard_map/ppermute | solution.py:305
  (72 shorter events, 19.9 us)
Async XLA Ops:
  2.7 5.2 %collective-permute-start.2 = (f32[40,128,128]{2,1,0:T(8,128)}, f32[40,128,128]{2,1,0:T(8,128)S(1)}, u32[]{:S(2)}, u32[]{:S(2)}) collective-permute-start(f32[40,128,128]{2,1,0:T(8,128)} %bitcast.139), channel_id=1, source_target_pairs={{0,1},{1,0},{2,3},{3,2},{4,5},{5,4},{6,7},{7,6},{8,9},{9,8},{10,11... | collective-permute-start | bytes 7864328 | tf_op jit(solution)/shard_map/ppermute | solution.py:308
  2.7 8.6 %collective-permute-start.3 = (f32[128,128]{1,0:T(8,128)S(1)}, f32[128,128]{1,0:T(8,128)S(1)}, u32[]{:S(2)}, u32[]{:S(2)}) collective-permute-start(f32[128,128]{1,0:T(8,128)S(1)} %bitcast.129), channel_id=1, source_target_pairs={{0,16},{1,5},{2,18},{3,7},{4,20},{5,1},{6,22},{7,3},{8,24},{9,13},... | collective-permute-start | bytes 196616 | tf_op jit(solution)/shard_map/ppermute | solution.py:305
  5.8 5.6 %collective-permute-start.4 = (f32[128,128]{1,0:T(8,128)S(1)}, f32[128,128]{1,0:T(8,128)S(1)}, u32[]{:S(2)}, u32[]{:S(2)}) collective-permute-start(f32[128,128]{1,0:T(8,128)S(1)} %bitcast.130), channel_id=1, source_target_pairs={{0,24},{1,7},{2,26},{3,5},{4,28},{5,3},{6,30},{7,1},{8,16},{9,15},... | collective-permute-start | bytes 196616 | tf_op jit(solution)/shard_map/ppermute | solution.py:305
  7.2 4.3 %collective-permute-start.5 = (f32[128,128]{1,0:T(8,128)S(1)}, f32[128,128]{1,0:T(8,128)S(1)}, u32[]{:S(2)}, u32[]{:S(2)}) collective-permute-start(f32[128,128]{1,0:T(8,128)S(1)} %bitcast.131), channel_id=1, source_target_pairs={{0,8},{1,3},{2,10},{3,1},{4,12},{5,7},{6,14},{7,5},{8,0},{9,11},{1... | collective-permute-start | bytes 196616 | tf_op jit(solution)/shard_map/ppermute | solution.py:305
  13.6 5.3 %collective-permute-start.8 = (f32[136,128]{1,0:T(8,128)S(1)}, f32[136,128]{1,0:T(8,128)S(1)}, u32[]{:S(2)}, u32[]{:S(2)}) collective-permute-start(f32[136,128]{1,0:T(8,128)S(1)} %get-tuple-element.42), channel_id=1, source_target_pairs={{0,4},{1,17},{2,6},{3,19},{4,0},{5,21},{6,2},{7,23},{8,12},{9,25},... | collective-permute-start | bytes 208904 | tf_op jit(solution)/shard_map/ppermute | solution.py:305
  16.2 6.3 %collective-permute-start.7 = (f32[136,128]{1,0:T(8,128)S(1)}, f32[136,128]{1,0:T(8,128)S(1)}, u32[]{:S(2)}, u32[]{:S(2)}) collective-permute-start(f32[136,128]{1,0:T(8,128)S(1)} %get-tuple-element.41), channel_id=1, source_target_pairs={{0,6},{1,25},{2,4},{3,27},{4,2},{5,29},{6,0},{7,31},{8,14},{9,17},... | collective-permute-start | bytes 208904 | tf_op jit(solution)/shard_map/ppermute | solution.py:305
  17.7 5.1 %collective-permute-start.6 = (f32[136,128]{1,0:T(8,128)S(1)}, f32[136,128]{1,0:T(8,128)S(1)}, u32[]{:S(2)}, u32[]{:S(2)}) collective-permute-start(f32[136,128]{1,0:T(8,128)S(1)} %get-tuple-element.40), channel_id=1, source_target_pairs={{0,2},{1,9},{2,0},{3,11},{4,6},{5,13},{6,4},{7,15},{8,10},{9,1},{1... | collective-permute-start | bytes 208904 | tf_op jit(solution)/shard_map/ppermute | solution.py:305
  24.3 4.4 %collective-permute-start.10 = (f32[144,128]{1,0:T(8,128)S(1)}, f32[144,128]{1,0:T(8,128)S(1)}, u32[]{:S(2)}, u32[]{:S(2)}) collective-permute-start(f32[144,128]{1,0:T(8,128)S(1)} %get-tuple-element.43.refs_4_), channel_id=1, source_target_pairs={{0,16},{1,5},{2,18},{3,7},{4,20},{5,1},{6,22},{7,3},{8,24},{9,13},... | collective-permute-start | bytes 221192 | tf_op jit(solution)/shard_map/ppermute | solution.py:305
  25.8 5.3 %collective-permute-start.11 = (f32[144,128]{1,0:T(8,128)S(1)}, f32[144,128]{1,0:T(8,128)S(1)}, u32[]{:S(2)}, u32[]{:S(2)}) collective-permute-start(f32[144,128]{1,0:T(8,128)S(1)} %get-tuple-element.43.refs_4_), channel_id=1, source_target_pairs={{0,24},{1,7},{2,26},{3,5},{4,28},{5,3},{6,30},{7,1},{8,16},{9,15},... | collective-permute-start | bytes 221192 | tf_op jit(solution)/shard_map/ppermute | solution.py:305
  27.1 4.4 %collective-permute-start.12 = (f32[144,128]{1,0:T(8,128)S(1)}, f32[144,128]{1,0:T(8,128)S(1)}, u32[]{:S(2)}, u32[]{:S(2)}) collective-permute-start(f32[144,128]{1,0:T(8,128)S(1)} %get-tuple-element.43.refs_4_), channel_id=1, source_target_pairs={{0,8},{1,3},{2,10},{3,1},{4,12},{5,7},{6,14},{7,5},{8,0},{9,11},{1... | collective-permute-start | bytes 221192 | tf_op jit(solution)/shard_map/ppermute | solution.py:305
  33.4 5.5 %collective-permute-start.15 = (f32[144,128]{1,0:T(8,128)S(1)}, f32[144,128]{1,0:T(8,128)S(1)}, u32[]{:S(2)}, u32[]{:S(2)}) collective-permute-start(f32[144,128]{1,0:T(8,128)S(1)} %get-tuple-element.47), channel_id=1, source_target_pairs={{0,4},{1,17},{2,6},{3,19},{4,0},{5,21},{6,2},{7,23},{8,12},{9,25},... | collective-permute-start | bytes 221192 | tf_op jit(solution)/shard_map/ppermute | solution.py:305
  34.6 6.3 %collective-permute-start.14 = (f32[144,128]{1,0:T(8,128)S(1)}, f32[144,128]{1,0:T(8,128)S(1)}, u32[]{:S(2)}, u32[]{:S(2)}) collective-permute-start(f32[144,128]{1,0:T(8,128)S(1)} %get-tuple-element.46), channel_id=1, source_target_pairs={{0,6},{1,25},{2,4},{3,27},{4,2},{5,29},{6,0},{7,31},{8,14},{9,17},... | collective-permute-start | bytes 221192 | tf_op jit(solution)/shard_map/ppermute | solution.py:305
  35.8 5.1 %collective-permute-start.13 = (f32[144,128]{1,0:T(8,128)S(1)}, f32[144,128]{1,0:T(8,128)S(1)}, u32[]{:S(2)}, u32[]{:S(2)}) collective-permute-start(f32[144,128]{1,0:T(8,128)S(1)} %get-tuple-element.45), channel_id=1, source_target_pairs={{0,2},{1,9},{2,0},{3,11},{4,6},{5,13},{6,4},{7,15},{8,10},{9,1},{1... | collective-permute-start | bytes 221192 | tf_op jit(solution)/shard_map/ppermute | solution.py:305
  42.7 5.3 %collective-permute-start.18 = (f32[144,128]{1,0:T(8,128)S(1)}, f32[144,128]{1,0:T(8,128)S(1)}, u32[]{:S(2)}, u32[]{:S(2)}) collective-permute-start(f32[144,128]{1,0:T(8,128)S(1)} %get-tuple-element.50.refs_4_), channel_id=1, source_target_pairs={{0,24},{1,7},{2,26},{3,5},{4,28},{5,3},{6,30},{7,1},{8,16},{9,15},... | collective-permute-start | bytes 221192 | tf_op jit(solution)/shard_map/ppermute | solution.py:305
  44.5 4.4 %collective-permute-start.17 = (f32[144,128]{1,0:T(8,128)S(1)}, f32[144,128]{1,0:T(8,128)S(1)}, u32[]{:S(2)}, u32[]{:S(2)}) collective-permute-start(f32[144,128]{1,0:T(8,128)S(1)} %get-tuple-element.50.refs_4_), channel_id=1, source_target_pairs={{0,16},{1,5},{2,18},{3,7},{4,20},{5,1},{6,22},{7,3},{8,24},{9,13},... | collective-permute-start | bytes 221192 | tf_op jit(solution)/shard_map/ppermute | solution.py:305
  45.3 4.4 %collective-permute-start.19 = (f32[144,128]{1,0:T(8,128)S(1)}, f32[144,128]{1,0:T(8,128)S(1)}, u32[]{:S(2)}, u32[]{:S(2)}) collective-permute-start(f32[144,128]{1,0:T(8,128)S(1)} %get-tuple-element.50.refs_4_), channel_id=1, source_target_pairs={{0,8},{1,3},{2,10},{3,1},{4,12},{5,7},{6,14},{7,5},{8,0},{9,11},{1... | collective-permute-start | bytes 221192 | tf_op jit(solution)/shard_map/ppermute | solution.py:305
  49.6 2.3 %collective-permute-start.20 = (f32[384,128]{1,0:T(8,128)S(1)}, f32[384,128]{1,0:T(8,128)S(1)}, u32[]{:S(2)}, u32[]{:S(2)}) collective-permute-start(f32[384,128]{1,0:T(8,128)S(1)} %pad_maximum_fusion), channel_id=1, source_target_pairs={{0,1},{1,0},{2,3},{3,2},{4,5},{5,4},{6,7},{7,6},{8,9},{9,8},{10,11... | collective-permute-start | bytes 589832 | tf_op jit(solution)/shard_map/ppermute | solution.py:308
  52.4 5.9 %collective-permute-start.23 = (f32[144,128]{1,0:T(8,128)S(1)}, f32[144,128]{1,0:T(8,128)S(1)}, u32[]{:S(2)}, u32[]{:S(2)}) collective-permute-start(f32[144,128]{1,0:T(8,128)S(1)} %get-tuple-element.75), channel_id=1, source_target_pairs={{0,4},{1,17},{2,6},{3,19},{4,0},{5,21},{6,2},{7,23},{8,12},{9,25},... | collective-permute-start | bytes 221192 | tf_op jit(solution)/shard_map/ppermute | solution.py:305
  53.6 6.3 %collective-permute-start.22 = (f32[144,128]{1,0:T(8,128)S(1)}, f32[144,128]{1,0:T(8,128)S(1)}, u32[]{:S(2)}, u32[]{:S(2)}) collective-permute-start(f32[144,128]{1,0:T(8,128)S(1)} %get-tuple-element.74), channel_id=1, source_target_pairs={{0,6},{1,25},{2,4},{3,27},{4,2},{5,29},{6,0},{7,31},{8,14},{9,17},... | collective-permute-start | bytes 221192 | tf_op jit(solution)/shard_map/ppermute | solution.py:305
  55.2 5.1 %collective-permute-start.21 = (f32[144,128]{1,0:T(8,128)S(1)}, f32[144,128]{1,0:T(8,128)S(1)}, u32[]{:S(2)}, u32[]{:S(2)}) collective-permute-start(f32[144,128]{1,0:T(8,128)S(1)} %get-tuple-element.73), channel_id=1, source_target_pairs={{0,2},{1,9},{2,0},{3,11},{4,6},{5,13},{6,4},{7,15},{8,10},{9,1},{1... | collective-permute-start | bytes 221192 | tf_op jit(solution)/shard_map/ppermute | solution.py:305
  60.4 4.6 %collective-permute-start.26 = (f32[16,128]{1,0:T(8,128)S(1)}, f32[16,128]{1,0:T(8,128)S(1)}, u32[]{:S(2)}, u32[]{:S(2)}) collective-permute-start(f32[16,128]{1,0:T(8,128)S(1)} %slice.163), channel_id=1, source_target_pairs={{0,24},{1,7},{2,26},{3,5},{4,28},{5,3},{6,30},{7,1},{8,16},{9,15},... | collective-permute-start | bytes 24584 | tf_op jit(solution)/shard_map/ppermute | solution.py:305
  62.5 3.7 %collective-permute-start.25 = (f32[16,128]{1,0:T(8,128)S(1)}, f32[16,128]{1,0:T(8,128)S(1)}, u32[]{:S(2)}, u32[]{:S(2)}) collective-permute-start(f32[16,128]{1,0:T(8,128)S(1)} %slice.163), channel_id=1, source_target_pairs={{0,16},{1,5},{2,18},{3,7},{4,20},{5,1},{6,22},{7,3},{8,24},{9,13},... | collective-permute-start | bytes 24584 | tf_op jit(solution)/shard_map/ppermute | solution.py:305
  62.9 3.7 %collective-permute-start.24 = (f32[16,128]{1,0:T(8,128)S(1)}, f32[16,128]{1,0:T(8,128)S(1)}, u32[]{:S(2)}, u32[]{:S(2)}) collective-permute-start(f32[16,128]{1,0:T(8,128)S(1)} %slice.163), channel_id=1, source_target_pairs={{0,8},{1,3},{2,10},{3,1},{4,12},{5,7},{6,14},{7,5},{8,0},{9,11},{1... | collective-permute-start | bytes 24584 | tf_op jit(solution)/shard_map/ppermute | solution.py:305
  63.9 2.7 %collective-permute-start.27 = (f32[128,128]{1,0:T(8,128)S(1)}, f32[128,128]{1,0:T(8,128)S(1)}, u32[]{:S(2)}, u32[]{:S(2)}) collective-permute-start(f32[128,128]{1,0:T(8,128)S(1)} %slice.173), channel_id=1, source_target_pairs={{0,1},{1,0},{2,3},{3,2},{4,5},{5,4},{6,7},{7,6},{8,9},{9,8},{10,11... | collective-permute-start | bytes 196616 | tf_op jit(solution)/shard_map/ppermute | solution.py:308
  (5 other events, 18.7 us)

commit v6 on v5

--- a/solution.py
+++ b/solution.py
@@ -245,7 +245,10 @@
     deep = per * width
     raw, w0 = blocks_in(raw_ref, per, width), blocks_in(w0_ref, per, width)
     totals = jnp.concatenate(
-        [mine[deep:], jnp.zeros((mine.shape[1] - mine.shape[0] + deep, mine.shape[1]), F32)]
+        [
+            0.5 * (mine[deep:] + other[deep:]),
+            jnp.zeros((mine.shape[1] - mine.shape[0] + deep, mine.shape[1]), F32),
+        ]
     ).T[:width]
     step0 = totals[:, 0:1] / totals[:, 1:2]
     degree, gain = degree_ref[...], gain_ref[...]
@@ -280,6 +283,30 @@
     sent_out[deep:] = dot_rows(pairs, sent_out.shape[0] - deep)
 
 
+def cross_update(per, *refs, place):
+    parts = (len(refs) - 2) // 2
+    sent, (own_ref, crossed_ref), outs = refs[:parts], refs[parts : parts + 2], refs[parts + 2 :]
+    size = own_ref.shape[1]
+    deep = crossed_ref.shape[0] // (parts - 1)
+    width = deep // per
+    total = jnp.zeros((width, size), F32)
+    for part in range(parts):
+        for j in range(per):
+            cut = slice(j * width, (j + 1) * width)
+            if part == 0:
+                field = own_ref[cut]
+            else:
+                first = (part - 1) * deep + j * width
+                field = crossed_ref[first : first + width]
+            total = total + sent[part][cut] * field
+    lane = lax.broadcasted_iota(jnp.int32, (width, size), 1)
+    table = jnp.where(lane == place, jnp.sum(total, axis=1, keepdims=True), 0.0)
+    square = jnp.concatenate([table, jnp.zeros((size - width, size), F32)], axis=0).T
+    for part in range(parts):
+        outs[part][:deep] = sent[part][:deep]
+        outs[part][deep:] = sent[part][deep:] + square[: sent[part].shape[0] - deep]
+
+
 def update(kernel, per, shapes, *arrays):
     return pl.pallas_call(
         functools.partial(kernel, per),
@@ -294,26 +321,26 @@
     n_line = n_col // 2
     parts = max(n_row, n_line)
 
-    def joint(array, offset, row_core):
+    def joint(array, offset, row_core, turn):
         pairs = []
         for r in range(n_row):
             for z in range(n_line):
                 for k in range(2):
                     to_r, to_z = (r ^ offset, z) if k == row_core else (r, z ^ offset)
                     if to_r < n_row and to_z < n_line:
-                        pairs.append((r * n_col + z * 2 + k, to_r * n_col + to_z * 2 + k))
+                        pairs.append((r * n_col + z * 2 + k, to_r * n_col + to_z * 2 + (k ^ turn)))
         return lax.ppermute(array, ("row", "col"), pairs)
 
     def swap(array):
         return lax.ppermute(array, "col", [(c, c ^ 1) for c in range(n_col)])
 
     def gather(field):
-        return [field] + [joint(field, offset, 0) for offset in range(1, parts)]
+        return [field] + [joint(field, offset, 0, 0) for offset in range(1, parts)]
 
     def collect(sent):
         total = sent[0]
         for offset in reversed(far_first(parts)):
-            total = total + joint(sent[offset], offset, 1)
+            total = total + joint(sent[offset], offset, 1, 1)
         return total
 
     def shards(block_values, block_index, block_count, strength, raw_scores):
@@ -363,14 +390,16 @@
         )
 
         mine = collect(apply_blocks(matrix, gather(sent), per, width, False))
-        gamma0, delta0 = row_of(mine[deep:], 0), row_of(mine[deep:], 1)
+        other = swap(mine)
+        sums = 0.5 * (mine[deep:] + other[deep:])
+        gamma0, delta0 = row_of(sums, 0), row_of(sums, 1)
         step0 = gamma0 / delta0
         q0, r1, w1, sent = update(
             second_update,
             per,
             (deep_shape,) * 3 + ((deep + aux_rows, size),),
             mine,
-            swap(mine[:deep]),
+            other,
             flat,
             w0,
             degree,
@@ -382,19 +411,24 @@
         n_pairs = 13
         gathered = gather(sent)
         crossed = swap(jnp.concatenate([part[:deep] for part in gathered[1:]]))
-        crossed = [gathered[0][:deep]] + jnp.split(crossed, parts - 1)
         sent = apply_blocks(matrix, gathered, per, width, False)
-        cross = sum(
-            jnp.sum(blocks(out) * blocks(part), axis=(0, 2)) for out, part in zip(sent, crossed)
-        )
-        after = sent[0].shape[0] - deep - n_pairs - 1
-        cross = lax.pad(
-            cross[None], 0.0, ((deep + n_pairs, after, 0), (0, size - width, 0))
-        )
-        mine = collect([out + cross for out in sent])
-        sums = mine[deep:]
-        tail = sum(gather(sums))
-        product = blocks(mine) + blocks(swap(mine[:deep]))
+        sent = update(
+            functools.partial(cross_update, place=n_pairs),
+            per,
+            (sent[0].shape,) * parts,
+            *sent,
+            gathered[0],
+            crossed,
+        )
+        mine = collect(sent)
+        other = swap(mine)
+        tail = 0.0
+        for offset in reversed(far_first(parts)):
+            tail = tail + joint(mine[deep:], offset, 1, 1)
+        other, tail = lax.optimization_barrier((other, tail))
+        tail = tail + other[deep:]
+        sums = 0.5 * (mine[deep:] + other[deep:])
+        product = blocks(mine) + blocks(other)
         qh = h + gains * (degree * h - product)
         g11, r1w1, r1w0, hh, hw1, hw0, w11, w10, w00, a_h0, a_10, a_00, hdh = (
             row_of(sums, n) for n in range(n_pairs)

time: 67.7 us -> 65.2 us (0.963)
  the two profiles are of different devices: /device:TPU:0 before, /device:TPU:1 now
where the time goes in v6:
time: 65.2 us; the launch traced here: 65 us
  starting transfers between devices  30.5 us (47%)
  waiting for transfers between devices  22 us (34%)
  Pallas kernels  10 us (15%)
  between operations  1.44 us (2%)
  other arithmetic  0.93 us (1%)
    ppermute x21, starting transfers between devices, joint(): return lax.ppermute(array, ('row', 'col'), pairs)  27.6 us
    ppermute x21, waiting for transfers between devices, joint(): return lax.ppermute(array, ('row', 'col'), pairs)  18.6 us
    pallas_call x3, Pallas kernels, apply_blocks(): pl.pallas_call(functools.partial(apply_kernel, parts, per, width, with_de...  6.03 us
    ppermute x7, waiting for transfers between devices, swap(): return lax.ppermute(array, 'col', [(c, c ^ 1) for c in range(n_col)])  3.38 us
    ppermute x7, starting transfers between devices, swap(): return lax.ppermute(array, 'col', [(c, c ^ 1) for c in range(n_col)])  2.94 us
    pallas_call x1, Pallas kernels, split_blocks(): pl.pallas_call(split_kernel, in_specs=[SMEM, SMEM, pl.BlockSpec(memory_sp...  2.38 us
  transfers between devices with their start and end apart: 28, of which 17 were waited for; matrix products, arithmetic and copies ran while one was open for 0% of the time, Pallas kernels for 8%

profile of v6, /device:TPU:1, one launch (start us, length us, event | category | flops | bytes accessed | tf_op | source)
XLA Modules:
  0.0 65.0 jit_solution(9136409992182851030)
XLA Ops:
  2.7 3.4 %collective-permute-start.3 = (f32[128,128]{1,0:T(8,128)S(1)}, f32[128,128]{1,0:T(8,128)S(1)}, u32[]{:S(2)}, u32[]{:S(2)}) collective-permute-start(f32[128,128]{1,0:T(8,128)S(1)} %bitcast.127), channel_id=1, source_target_pairs={{0,16},{1,5},{2,18},{3,7},{4,20},{5,1},{6,22},{7,3},{8,24},{9,13},... | collective-permute-start | bytes 196616 | tf_op jit(solution)/shard_map/ppermute | solution.py:332
  8.6 2.4 %shard_map.69 = (bf16[40,256,128]{2,1,0:T(8,128)(2,1)S(1)}, bf16[40,256,128]{2,1,0:T(8,128)(2,1)S(1)}) custom-call(s32[3,40]{1,0:T(4,128)S(1)} %get-tuple-element.36.own_places.refs_0_, s32[3,40]{1,0:T(4,128)S(1)} %collective-permute-done.other_places.refs_1_, f32[40,128,128]{2,1,0:T(8,128)} %bitcast.138, f32[40,128,128]{2,1,0:T(8,128)S(1)} %collective-permute-done.2.other_in), custom_call_target="tpu_custom_call" | custom-call | flops 5242880 | bytes 10485760 | tf_op jit(solution)/shard_map/pallas_call | solution.py:95
  11.1 2.1 %shard_map.70 = (f32[136,128]{1,0:T(8,128)S(1)}, f32[136,128]{1,0:T(8,128)S(1)}, f32[136,128]{1,0:T(8,128)S(1)}, f32[136,128]{1,0:T(8,128)S(1)}) custom-call(s32[3,40]{1,0:T(4,128)S(1)} %get-tuple-element.36.own_places.refs_0_, s32[3,40]{1,0:T(4,128)S(1)} %collective-permute-done.other_places.refs_1_, bf16[40,256,128]{2,1,0:T(8,128)(2,1)S(1)} %get-tuple-element.41.refs_2_, ...), custom_call_target="tpu_custom_call" | custom-call | flops 419430400 | bytes 5242880 | tf_op jit(solution)/shard_map/pallas_call | solution.py:185
  13.2 1.6 %collective-permute-start.8 = (f32[136,128]{1,0:T(8,128)S(1)}, f32[136,128]{1,0:T(8,128)S(1)}, u32[]{:S(2)}, u32[]{:S(2)}) collective-permute-start(f32[136,128]{1,0:T(8,128)S(1)} %get-tuple-element.48), channel_id=1, source_target_pairs={{0,5},{1,16},{2,7},{3,18},{4,1},{5,20},{6,3},{7,22},{8,13},{9,24},... | collective-permute-start | bytes 208904 | tf_op jit(solution)/shard_map/ppermute | solution.py:332
  14.8 3.4 %collective-permute-start.7 = (f32[136,128]{1,0:T(8,128)S(1)}, f32[136,128]{1,0:T(8,128)S(1)}, u32[]{:S(2)}, u32[]{:S(2)}) collective-permute-start(f32[136,128]{1,0:T(8,128)S(1)} %get-tuple-element.47), channel_id=1, source_target_pairs={{0,7},{1,24},{2,5},{3,26},{4,3},{5,28},{6,1},{7,30},{8,15},{9,16},... | collective-permute-start | bytes 208904 | tf_op jit(solution)/shard_map/ppermute | solution.py:332
  18.2 1.3 %collective-permute-start.6 = (f32[136,128]{1,0:T(8,128)S(1)}, f32[136,128]{1,0:T(8,128)S(1)}, u32[]{:S(2)}, u32[]{:S(2)}) collective-permute-start(f32[136,128]{1,0:T(8,128)S(1)} %get-tuple-element.46), channel_id=1, source_target_pairs={{0,3},{1,8},{2,1},{3,10},{4,7},{5,12},{6,5},{7,14},{8,11},{9,0},{1... | collective-permute-start | bytes 208904 | tf_op jit(solution)/shard_map/ppermute | solution.py:332
  20.4 1.5 %collective-permute-done.6 = f32[136,128]{1,0:T(8,128)S(1)} collective-permute-done((f32[136,128]{1,0:T(8,128)S(1)}, f32[136,128]{1,0:T(8,128)S(1)}, u32[]{:S(2)}, u32[]{:S(2)}) %collective-permute-start.6) | collective-permute-done | bytes 69664 | tf_op jit(solution)/shard_map/ppermute | solution.py:332
  23.6 3.4 %collective-permute-start.11 = (f32[144,128]{1,0:T(8,128)S(1)}, f32[144,128]{1,0:T(8,128)S(1)}, u32[]{:S(2)}, u32[]{:S(2)}) collective-permute-start(f32[144,128]{1,0:T(8,128)S(1)} %get-tuple-element.49.refs_4_), channel_id=1, source_target_pairs={{0,24},{1,7},{2,26},{3,5},{4,28},{5,3},{6,30},{7,1},{8,16},{9,15},... | collective-permute-start | bytes 221192 | tf_op jit(solution)/shard_map/ppermute | solution.py:332
  27.6 1.9 %collective-permute-done.11.refs_6_ = f32[144,128]{1,0:T(8,128)S(1)} collective-permute-done((f32[144,128]{1,0:T(8,128)S(1)}, f32[144,128]{1,0:T(8,128)S(1)}, u32[]{:S(2)}, u32[]{:S(2)}) %collective-permute-start.11) | collective-permute-done | bytes 73760 | tf_op jit(solution)/shard_map/ppermute | solution.py:332
  30.7 2.0 %shard_map.72 = (f32[144,128]{1,0:T(8,128)S(1)}, f32[144,128]{1,0:T(8,128)S(1)}, f32[144,128]{1,0:T(8,128)S(1)}, f32[144,128]{1,0:T(8,128)S(1)}) custom-call(s32[3,40]{1,0:T(4,128)S(1)} %get-tuple-element.36.own_places.refs_0_, s32[3,40]{1,0:T(4,128)S(1)} %collective-permute-done.other_places.refs_1_, bf16[40,256,128]{2,1,0:T(8,128)(2,1)S(1)} %get-tuple-element.41.refs_2_, ...), custom_call_target="tpu_custom_call" | custom-call | flops 335544320 | bytes 5242880 | tf_op jit(solution)/shard_map/pallas_call | solution.py:185
  33.3 1.8 %collective-permute-start.14 = (f32[144,128]{1,0:T(8,128)S(1)}, f32[144,128]{1,0:T(8,128)S(1)}, u32[]{:S(2)}, u32[]{:S(2)}) collective-permute-start(f32[144,128]{1,0:T(8,128)S(1)} %get-tuple-element.52), channel_id=1, source_target_pairs={{0,7},{1,24},{2,5},{3,26},{4,3},{5,28},{6,1},{7,30},{8,15},{9,16},... | collective-permute-start | bytes 221192 | tf_op jit(solution)/shard_map/ppermute | solution.py:332
  36.1 2.9 %collective-permute-done.15 = f32[144,128]{1,0:T(8,128)S(1)} collective-permute-done((f32[144,128]{1,0:T(8,128)S(1)}, f32[144,128]{1,0:T(8,128)S(1)}, u32[]{:S(2)}, u32[]{:S(2)}) %collective-permute-start.15) | collective-permute-done | bytes 73760 | tf_op jit(solution)/shard_map/ppermute | solution.py:332
  39.8 1.3 %collective-permute-done.16.other = f32[144,128]{1,0:T(8,128)S(1)} collective-permute-done((f32[144,128]{1,0:T(8,128)S(1)}, f32[144,128]{1,0:T(8,128)S(1)}, u32[]{:S(2)}, u32[]{:S(2)}) %collective-permute-start.16) | collective-permute-done | bytes 73760 | tf_op jit(solution)/shard_map/ppermute | solution.py:335
  41.5 1.2 %collective-permute-start.18 = (f32[144,128]{1,0:T(8,128)S(1)}, f32[144,128]{1,0:T(8,128)S(1)}, u32[]{:S(2)}, u32[]{:S(2)}) collective-permute-start(f32[144,128]{1,0:T(8,128)S(1)} %get-tuple-element.56.refs_4_), channel_id=1, source_target_pairs={{0,24},{1,7},{2,26},{3,5},{4,28},{5,3},{6,30},{7,1},{8,16},{9,15},... | collective-permute-start | bytes 221192 | tf_op jit(solution)/shard_map/ppermute | solution.py:332
  43.0 2.1 %collective-permute-start.19 = (f32[144,128]{1,0:T(8,128)S(1)}, f32[144,128]{1,0:T(8,128)S(1)}, u32[]{:S(2)}, u32[]{:S(2)}) collective-permute-start(f32[144,128]{1,0:T(8,128)S(1)} %get-tuple-element.56.refs_4_), channel_id=1, source_target_pairs={{0,8},{1,3},{2,10},{3,1},{4,12},{5,7},{6,14},{7,5},{8,0},{9,11},{1... | collective-permute-start | bytes 221192 | tf_op jit(solution)/shard_map/ppermute | solution.py:332
  45.1 1.6 %collective-permute-done.18.refs_6_ = f32[144,128]{1,0:T(8,128)S(1)} collective-permute-done((f32[144,128]{1,0:T(8,128)S(1)}, f32[144,128]{1,0:T(8,128)S(1)}, u32[]{:S(2)}, u32[]{:S(2)}) %collective-permute-start.18) | collective-permute-done | bytes 73760 | tf_op jit(solution)/shard_map/ppermute | solution.py:332
  46.6 1.5 %collective-permute-done.17.refs_5_ = f32[144,128]{1,0:T(8,128)S(1)} collective-permute-done((f32[144,128]{1,0:T(8,128)S(1)}, f32[144,128]{1,0:T(8,128)S(1)}, u32[]{:S(2)}, u32[]{:S(2)}) %collective-permute-start.17) | collective-permute-done | bytes 73760 | tf_op jit(solution)/shard_map/ppermute | solution.py:332
  48.4 2.0 %shard_map.74 = (f32[144,128]{1,0:T(8,128)S(1)}, f32[144,128]{1,0:T(8,128)S(1)}, f32[144,128]{1,0:T(8,128)S(1)}, f32[144,128]{1,0:T(8,128)S(1)}) custom-call(s32[3,40]{1,0:T(4,128)S(1)} %get-tuple-element.36.own_places.refs_0_, s32[3,40]{1,0:T(4,128)S(1)} %collective-permute-done.other_places.refs_1_, bf16[40,256,128]{2,1,0:T(8,128)(2,1)S(1)} %get-tuple-element.41.refs_2_, ...), custom_call_target="tpu_custom_call" | custom-call | flops 335544320 | bytes 5242880 | tf_op jit(solution)/shard_map/pallas_call | solution.py:185
  51.2 1.6 %collective-permute-start.22 = (f32[144,128]{1,0:T(8,128)S(1)}, f32[144,128]{1,0:T(8,128)S(1)}, u32[]{:S(2)}, u32[]{:S(2)}) collective-permute-start(f32[144,128]{1,0:T(8,128)S(1)} %get-tuple-element.63), channel_id=1, source_target_pairs={{0,7},{1,24},{2,5},{3,26},{4,3},{5,28},{6,1},{7,30},{8,15},{9,16},... | collective-permute-start | bytes 221192 | tf_op jit(solution)/shard_map/ppermute | solution.py:332
  52.8 1.3 %collective-permute-start.21 = (f32[144,128]{1,0:T(8,128)S(1)}, f32[144,128]{1,0:T(8,128)S(1)}, u32[]{:S(2)}, u32[]{:S(2)}) collective-permute-start(f32[144,128]{1,0:T(8,128)S(1)} %get-tuple-element.62), channel_id=1, source_target_pairs={{0,3},{1,8},{2,1},{3,10},{4,7},{5,12},{6,5},{7,14},{8,11},{9,0},{1... | collective-permute-start | bytes 221192 | tf_op jit(solution)/shard_map/ppermute | solution.py:332
  54.1 1.9 %collective-permute-done.23 = f32[144,128]{1,0:T(8,128)S(1)} collective-permute-done((f32[144,128]{1,0:T(8,128)S(1)}, f32[144,128]{1,0:T(8,128)S(1)}, u32[]{:S(2)}, u32[]{:S(2)}) %collective-permute-start.23) | collective-permute-done | bytes 73760 | tf_op jit(solution)/shard_map/ppermute | solution.py:332
  57.7 1.5 %collective-permute-start.25 = (f32[16,128]{1,0:T(8,128)S(1)}, f32[16,128]{1,0:T(8,128)S(1)}, u32[]{:S(2)}, u32[]{:S(2)}) collective-permute-start(f32[16,128]{1,0:T(8,128)S(1)} %slice.135), channel_id=1, source_target_pairs={{0,3},{1,8},{2,1},{3,10},{4,7},{5,12},{6,5},{7,14},{8,11},{9,0},{1... | collective-permute-start | bytes 24584 | tf_op jit(solution)/shard_map/ppermute | solution.py:332
  60.0 1.7 %collective-permute-start.24 = (f32[144,128]{1,0:T(8,128)S(1)}, f32[144,128]{1,0:T(8,128)S(1)}, u32[]{:S(2)}, u32[]{:S(2)}) collective-permute-start(f32[144,128]{1,0:T(8,128)S(1)} %add_add_fusion), channel_id=1, source_target_pairs={{0,1},{1,0},{2,3},{3,2},{4,5},{5,4},{6,7},{7,6},{8,9},{9,8},{10,11... | collective-permute-start | bytes 221192 | tf_op jit(solution)/shard_map/ppermute | solution.py:335
  61.7 2.4 %collective-permute-done.26 = f32[16,128]{1,0:T(8,128)S(1)} collective-permute-done((f32[16,128]{1,0:T(8,128)S(1)}, f32[16,128]{1,0:T(8,128)S(1)}, u32[]{:S(2)}, u32[]{:S(2)}) %collective-permute-start.26) | collective-permute-done | bytes 8224 | tf_op jit(solution)/shard_map/ppermute | solution.py:332
  (63 shorter events, 15.9 us)
Async XLA Ops:
  2.3 5.2 %collective-permute-start.2 = (f32[40,128,128]{2,1,0:T(8,128)}, f32[40,128,128]{2,1,0:T(8,128)S(1)}, u32[]{:S(2)}, u32[]{:S(2)}) collective-permute-start(f32[40,128,128]{2,1,0:T(8,128)} %bitcast.137), channel_id=1, source_target_pairs={{0,1},{1,0},{2,3},{3,2},{4,5},{5,4},{6,7},{7,6},{8,9},{9,8},{10,11... | collective-permute-start | bytes 7864328 | tf_op jit(solution)/shard_map/ppermute | solution.py:335
  2.7 8.2 %collective-permute-start.3 = (f32[128,128]{1,0:T(8,128)S(1)}, f32[128,128]{1,0:T(8,128)S(1)}, u32[]{:S(2)}, u32[]{:S(2)}) collective-permute-start(f32[128,128]{1,0:T(8,128)S(1)} %bitcast.127), channel_id=1, source_target_pairs={{0,16},{1,5},{2,18},{3,7},{4,20},{5,1},{6,22},{7,3},{8,24},{9,13},... | collective-permute-start | bytes 196616 | tf_op jit(solution)/shard_map/ppermute | solution.py:332
  6.1 4.9 %collective-permute-start.4 = (f32[128,128]{1,0:T(8,128)S(1)}, f32[128,128]{1,0:T(8,128)S(1)}, u32[]{:S(2)}, u32[]{:S(2)}) collective-permute-start(f32[128,128]{1,0:T(8,128)S(1)} %bitcast.128), channel_id=1, source_target_pairs={{0,24},{1,7},{2,26},{3,5},{4,28},{5,3},{6,30},{7,1},{8,16},{9,15},... | collective-permute-start | bytes 196616 | tf_op jit(solution)/shard_map/ppermute | solution.py:332
  7.2 3.8 %collective-permute-start.5 = (f32[128,128]{1,0:T(8,128)S(1)}, f32[128,128]{1,0:T(8,128)S(1)}, u32[]{:S(2)}, u32[]{:S(2)}) collective-permute-start(f32[128,128]{1,0:T(8,128)S(1)} %bitcast.129), channel_id=1, source_target_pairs={{0,8},{1,3},{2,10},{3,1},{4,12},{5,7},{6,14},{7,5},{8,0},{9,11},{1... | collective-permute-start | bytes 196616 | tf_op jit(solution)/shard_map/ppermute | solution.py:332
  13.2 6.4 %collective-permute-start.8 = (f32[136,128]{1,0:T(8,128)S(1)}, f32[136,128]{1,0:T(8,128)S(1)}, u32[]{:S(2)}, u32[]{:S(2)}) collective-permute-start(f32[136,128]{1,0:T(8,128)S(1)} %get-tuple-element.48), channel_id=1, source_target_pairs={{0,5},{1,16},{2,7},{3,18},{4,1},{5,20},{6,3},{7,22},{8,13},{9,24},... | collective-permute-start | bytes 208904 | tf_op jit(solution)/shard_map/ppermute | solution.py:332
  14.8 5.6 %collective-permute-start.7 = (f32[136,128]{1,0:T(8,128)S(1)}, f32[136,128]{1,0:T(8,128)S(1)}, u32[]{:S(2)}, u32[]{:S(2)}) collective-permute-start(f32[136,128]{1,0:T(8,128)S(1)} %get-tuple-element.47), channel_id=1, source_target_pairs={{0,7},{1,24},{2,5},{3,26},{4,3},{5,28},{6,1},{7,30},{8,15},{9,16},... | collective-permute-start | bytes 208904 | tf_op jit(solution)/shard_map/ppermute | solution.py:332
  18.2 3.7 %collective-permute-start.6 = (f32[136,128]{1,0:T(8,128)S(1)}, f32[136,128]{1,0:T(8,128)S(1)}, u32[]{:S(2)}, u32[]{:S(2)}) collective-permute-start(f32[136,128]{1,0:T(8,128)S(1)} %get-tuple-element.46), channel_id=1, source_target_pairs={{0,3},{1,8},{2,1},{3,10},{4,7},{5,12},{6,5},{7,14},{8,11},{9,0},{1... | collective-permute-start | bytes 208904 | tf_op jit(solution)/shard_map/ppermute | solution.py:332
  23.5 4.1 %collective-permute-start.10 = (f32[144,128]{1,0:T(8,128)S(1)}, f32[144,128]{1,0:T(8,128)S(1)}, u32[]{:S(2)}, u32[]{:S(2)}) collective-permute-start(f32[144,128]{1,0:T(8,128)S(1)} %get-tuple-element.49.refs_4_), channel_id=1, source_target_pairs={{0,16},{1,5},{2,18},{3,7},{4,20},{5,1},{6,22},{7,3},{8,24},{9,13},... | collective-permute-start | bytes 221192 | tf_op jit(solution)/shard_map/ppermute | solution.py:332
  23.6 6.0 %collective-permute-start.11 = (f32[144,128]{1,0:T(8,128)S(1)}, f32[144,128]{1,0:T(8,128)S(1)}, u32[]{:S(2)}, u32[]{:S(2)}) collective-permute-start(f32[144,128]{1,0:T(8,128)S(1)} %get-tuple-element.49.refs_4_), channel_id=1, source_target_pairs={{0,24},{1,7},{2,26},{3,5},{4,28},{5,3},{6,30},{7,1},{8,16},{9,15},... | collective-permute-start | bytes 221192 | tf_op jit(solution)/shard_map/ppermute | solution.py:332
  26.9 3.7 %collective-permute-start.12 = (f32[144,128]{1,0:T(8,128)S(1)}, f32[144,128]{1,0:T(8,128)S(1)}, u32[]{:S(2)}, u32[]{:S(2)}) collective-permute-start(f32[144,128]{1,0:T(8,128)S(1)} %get-tuple-element.49.refs_4_), channel_id=1, source_target_pairs={{0,8},{1,3},{2,10},{3,1},{4,12},{5,7},{6,14},{7,5},{8,0},{9,11},{1... | collective-permute-start | bytes 221192 | tf_op jit(solution)/shard_map/ppermute | solution.py:332
  32.6 6.4 %collective-permute-start.15 = (f32[144,128]{1,0:T(8,128)S(1)}, f32[144,128]{1,0:T(8,128)S(1)}, u32[]{:S(2)}, u32[]{:S(2)}) collective-permute-start(f32[144,128]{1,0:T(8,128)S(1)} %get-tuple-element.53), channel_id=1, source_target_pairs={{0,5},{1,16},{2,7},{3,18},{4,1},{5,20},{6,3},{7,22},{8,13},{9,24},... | collective-permute-start | bytes 221192 | tf_op jit(solution)/shard_map/ppermute | solution.py:332
  33.3 5.7 %collective-permute-start.14 = (f32[144,128]{1,0:T(8,128)S(1)}, f32[144,128]{1,0:T(8,128)S(1)}, u32[]{:S(2)}, u32[]{:S(2)}) collective-permute-start(f32[144,128]{1,0:T(8,128)S(1)} %get-tuple-element.52), channel_id=1, source_target_pairs={{0,7},{1,24},{2,5},{3,26},{4,3},{5,28},{6,1},{7,30},{8,15},{9,16},... | collective-permute-start | bytes 221192 | tf_op jit(solution)/shard_map/ppermute | solution.py:332
  35.1 4.7 %collective-permute-start.13 = (f32[144,128]{1,0:T(8,128)S(1)}, f32[144,128]{1,0:T(8,128)S(1)}, u32[]{:S(2)}, u32[]{:S(2)}) collective-permute-start(f32[144,128]{1,0:T(8,128)S(1)} %get-tuple-element.51), channel_id=1, source_target_pairs={{0,3},{1,8},{2,1},{3,10},{4,7},{5,12},{6,5},{7,14},{8,11},{9,0},{1... | collective-permute-start | bytes 221192 | tf_op jit(solution)/shard_map/ppermute | solution.py:332
  41.5 5.2 %collective-permute-start.18 = (f32[144,128]{1,0:T(8,128)S(1)}, f32[144,128]{1,0:T(8,128)S(1)}, u32[]{:S(2)}, u32[]{:S(2)}) collective-permute-start(f32[144,128]{1,0:T(8,128)S(1)} %get-tuple-element.56.refs_4_), channel_id=1, source_target_pairs={{0,24},{1,7},{2,26},{3,5},{4,28},{5,3},{6,30},{7,1},{8,16},{9,15},... | collective-permute-start | bytes 221192 | tf_op jit(solution)/shard_map/ppermute | solution.py:332
  42.6 5.5 %collective-permute-start.17 = (f32[144,128]{1,0:T(8,128)S(1)}, f32[144,128]{1,0:T(8,128)S(1)}, u32[]{:S(2)}, u32[]{:S(2)}) collective-permute-start(f32[144,128]{1,0:T(8,128)S(1)} %get-tuple-element.56.refs_4_), channel_id=1, source_target_pairs={{0,16},{1,5},{2,18},{3,7},{4,20},{5,1},{6,22},{7,3},{8,24},{9,13},... | collective-permute-start | bytes 221192 | tf_op jit(solution)/shard_map/ppermute | solution.py:332
  43.0 5.1 %collective-permute-start.19 = (f32[144,128]{1,0:T(8,128)S(1)}, f32[144,128]{1,0:T(8,128)S(1)}, u32[]{:S(2)}, u32[]{:S(2)}) collective-permute-start(f32[144,128]{1,0:T(8,128)S(1)} %get-tuple-element.56.refs_4_), channel_id=1, source_target_pairs={{0,8},{1,3},{2,10},{3,1},{4,12},{5,7},{6,14},{7,5},{8,0},{9,11},{1... | collective-permute-start | bytes 221192 | tf_op jit(solution)/shard_map/ppermute | solution.py:332
  48.1 2.2 %collective-permute-start.20 = (f32[384,128]{1,0:T(8,128)S(1)}, f32[384,128]{1,0:T(8,128)S(1)}, u32[]{:S(2)}, u32[]{:S(2)}) collective-permute-start(f32[384,128]{1,0:T(8,128)S(1)} %pad_maximum_fusion), channel_id=1, source_target_pairs={{0,1},{1,0},{2,3},{3,2},{4,5},{5,4},{6,7},{7,6},{8,9},{9,8},{10,11... | collective-permute-start | bytes 589832 | tf_op jit(solution)/shard_map/ppermute | solution.py:335
  50.5 5.5 %collective-permute-start.23 = (f32[144,128]{1,0:T(8,128)S(1)}, f32[144,128]{1,0:T(8,128)S(1)}, u32[]{:S(2)}, u32[]{:S(2)}) collective-permute-start(f32[144,128]{1,0:T(8,128)S(1)} %get-tuple-element.64), channel_id=1, source_target_pairs={{0,5},{1,16},{2,7},{3,18},{4,1},{5,20},{6,3},{7,22},{8,13},{9,24},... | collective-permute-start | bytes 221192 | tf_op jit(solution)/shard_map/ppermute | solution.py:332
  51.2 5.7 %collective-permute-start.22 = (f32[144,128]{1,0:T(8,128)S(1)}, f32[144,128]{1,0:T(8,128)S(1)}, u32[]{:S(2)}, u32[]{:S(2)}) collective-permute-start(f32[144,128]{1,0:T(8,128)S(1)} %get-tuple-element.63), channel_id=1, source_target_pairs={{0,7},{1,24},{2,5},{3,26},{4,3},{5,28},{6,1},{7,30},{8,15},{9,16},... | collective-permute-start | bytes 221192 | tf_op jit(solution)/shard_map/ppermute | solution.py:332
  52.8 4.8 %collective-permute-start.21 = (f32[144,128]{1,0:T(8,128)S(1)}, f32[144,128]{1,0:T(8,128)S(1)}, u32[]{:S(2)}, u32[]{:S(2)}) collective-permute-start(f32[144,128]{1,0:T(8,128)S(1)} %get-tuple-element.62), channel_id=1, source_target_pairs={{0,3},{1,8},{2,1},{3,10},{4,7},{5,12},{6,5},{7,14},{8,11},{9,0},{1... | collective-permute-start | bytes 221192 | tf_op jit(solution)/shard_map/ppermute | solution.py:332
  57.6 4.1 %collective-permute-start.27 = (f32[16,128]{1,0:T(8,128)S(1)}, f32[16,128]{1,0:T(8,128)S(1)}, u32[]{:S(2)}, u32[]{:S(2)}) collective-permute-start(f32[16,128]{1,0:T(8,128)S(1)} %slice.135), channel_id=1, source_target_pairs={{0,5},{1,16},{2,7},{3,18},{4,1},{5,20},{6,3},{7,22},{8,13},{9,24},... | collective-permute-start | bytes 24584 | tf_op jit(solution)/shard_map/ppermute | solution.py:332
  57.7 4.1 %collective-permute-start.25 = (f32[16,128]{1,0:T(8,128)S(1)}, f32[16,128]{1,0:T(8,128)S(1)}, u32[]{:S(2)}, u32[]{:S(2)}) collective-permute-start(f32[16,128]{1,0:T(8,128)S(1)} %slice.135), channel_id=1, source_target_pairs={{0,3},{1,8},{2,1},{3,10},{4,7},{5,12},{6,5},{7,14},{8,11},{9,0},{1... | collective-permute-start | bytes 24584 | tf_op jit(solution)/shard_map/ppermute | solution.py:332
  59.2 4.9 %collective-permute-start.26 = (f32[16,128]{1,0:T(8,128)S(1)}, f32[16,128]{1,0:T(8,128)S(1)}, u32[]{:S(2)}, u32[]{:S(2)}) collective-permute-start(f32[16,128]{1,0:T(8,128)S(1)} %slice.135), channel_id=1, source_target_pairs={{0,7},{1,24},{2,5},{3,26},{4,3},{5,28},{6,1},{7,30},{8,15},{9,16},... | collective-permute-start | bytes 24584 | tf_op jit(solution)/shard_map/ppermute | solution.py:332
  60.0 4.1 %collective-permute-start.24 = (f32[144,128]{1,0:T(8,128)S(1)}, f32[144,128]{1,0:T(8,128)S(1)}, u32[]{:S(2)}, u32[]{:S(2)}) collective-permute-start(f32[144,128]{1,0:T(8,128)S(1)} %add_add_fusion), channel_id=1, source_target_pairs={{0,1},{1,0},{2,3},{3,2},{4,5},{5,4},{6,7},{7,6},{8,9},{9,8},{10,11... | collective-permute-start | bytes 221192 | tf_op jit(solution)/shard_map/ppermute | solution.py:335
  (5 other events, 17.7 us)

commit v7 on v6

--- a/solution.py
+++ b/solution.py
@@ -47,15 +47,21 @@
     )(block_index, block_count, raw)
 
 
-def split_kernel(own_places, other_places, own_hbm, other_in, own_out, other_out, own_in, sems):
+def split_kernel(own_vmem, other_vmem, own_hbm, other_in, own_out, other_out, own_places, other_places, own_in, sems):
     slots, size, _ = own_in.shape
     core = core_here()
     copies = []
     for chunk in range(slots // COPY):
         cut = pl.ds(chunk * COPY, COPY)
         copies.append(pltpu.make_async_copy(own_hbm.at[cut], own_in.at[cut], sems.at[chunk]))
-    for copy in copies:
+    lists = [
+        pltpu.make_async_copy(own_vmem, own_places, sems.at[slots // COPY]),
+        pltpu.make_async_copy(other_vmem, other_places, sems.at[slots // COPY + 1]),
+    ]
+    for copy in lists + copies:
         copy.start()
+    for copy in lists:
+        copy.wait()
 
     def write(turn):
         def sweep(places, source, target, chunk):
@@ -94,12 +100,13 @@
     slots, size, _ = values.shape
     return pl.pallas_call(
         split_kernel,
-        in_specs=[SMEM, SMEM, pl.BlockSpec(memory_space=pltpu.HBM), VMEM],
-        out_specs=[VMEM, VMEM],
-        out_shape=[pltpu.VMEM((slots, 2 * size, size), BF)] * 2,
+        in_specs=[VMEM, VMEM, pl.BlockSpec(memory_space=pltpu.HBM), VMEM],
+        out_specs=[VMEM, VMEM, SMEM, SMEM],
+        out_shape=[pltpu.VMEM((slots, 2 * size, size), BF)] * 2
+        + [pltpu.SMEM(places.shape, jnp.int32)] * 2,
         scratch_shapes=[
             pltpu.VMEM((slots, size, size), F32),
-            pltpu.SemaphoreType.DMA((slots // COPY,)),
+            pltpu.SemaphoreType.DMA((slots // COPY + 2,)),
         ],
         compiler_params=pltpu.CompilerParams(vmem_limit_bytes=16 * 2**20),
         cost_estimate=pl.CostEstimate(
@@ -361,9 +368,8 @@
         gains = strength[None, :, None]
         gathered = gather(raw.reshape(per * raw.shape[1], raw.shape[2]))
         values, values_other = lax.optimization_barrier((values, values_other))
-        matrix = (places, places_other) + tuple(
-            split_blocks(places, places_other, values, values_other)
-        )
+        own, other, places, places_other = split_blocks(places, places_other, values, values_other)
+        matrix = (places, places_other, own, other)
 
         width, size = raw.shape[1:]
         deep = per * width
@@ -423,7 +429,7 @@
         mine = collect(sent)
         other = swap(mine)
         tail = 0.0
-        for offset in reversed(far_first(parts)):
+        for offset in reversed(range(1, parts)):
             tail = tail + joint(mine[deep:], offset, 1, 1)
         other, tail = lax.optimization_barrier((other, tail))
         tail = tail + other[deep:]

time: 65.2 us -> 62 us (0.951)
  the two profiles are of different devices: /device:TPU:1 before, /device:TPU:0 now
where the time goes in v7:
time: 62 us; the launch traced here: 61.3 us
  starting transfers between devices  30.9 us (50%)
  waiting for transfers between devices  19.9 us (32%)
  Pallas kernels  8.05 us (13%)
  between operations  1.44 us (2%)
  other arithmetic  0.93 us (2%)
    ppermute x21, starting transfers between devices, joint(): return lax.ppermute(array, ('row', 'col'), pairs)  28.5 us
    ppermute x21, waiting for transfers between devices, joint(): return lax.ppermute(array, ('row', 'col'), pairs)  16.9 us
    pallas_call x3, Pallas kernels, apply_blocks(): pl.pallas_call(functools.partial(apply_kernel, parts, per, width, with_de...  4.07 us
    ppermute x7, waiting for transfers between devices, swap(): return lax.ppermute(array, 'col', [(c, c ^ 1) for c in range(n_col)])  2.99 us
    ppermute x7, starting transfers between devices, swap(): return lax.ppermute(array, 'col', [(c, c ^ 1) for c in range(n_col)])  2.4 us
    pallas_call x1, Pallas kernels, split_blocks(): pl.pallas_call(split_kernel, in_specs=[VMEM, VMEM, pl.BlockSpec(memory_sp...  2.39 us
  transfers between devices with their start and end apart: 28, of which 20 were waited for; matrix products, arithmetic and copies ran while one was open for 0% of the time, Pallas kernels for 7%

profile of v7, /device:TPU:0, one launch (start us, length us, event | category | flops | bytes accessed | tf_op | source)
XLA Modules:
  0.0 61.3 jit_solution(5325337482493539194)
XLA Ops:
  2.7 3.0 %collective-permute-start.3 = (f32[128,128]{1,0:T(8,128)S(1)}, f32[128,128]{1,0:T(8,128)S(1)}, u32[]{:S(2)}, u32[]{:S(2)}) collective-permute-start(f32[128,128]{1,0:T(8,128)S(1)} %bitcast.127), channel_id=1, source_target_pairs={{0,16},{1,5},{2,18},{3,7},{4,20},{5,1},{6,22},{7,3},{8,24},{9,13},... | collective-permute-start | bytes 196616 | tf_op jit(solution)/shard_map/ppermute | solution.py:339
  5.8 1.4 %collective-permute-start.4 = (f32[128,128]{1,0:T(8,128)S(1)}, f32[128,128]{1,0:T(8,128)S(1)}, u32[]{:S(2)}, u32[]{:S(2)}) collective-permute-start(f32[128,128]{1,0:T(8,128)S(1)} %bitcast.128), channel_id=1, source_target_pairs={{0,24},{1,7},{2,26},{3,5},{4,28},{5,3},{6,30},{7,1},{8,16},{9,15},... | collective-permute-start | bytes 196616 | tf_op jit(solution)/shard_map/ppermute | solution.py:339
  8.7 2.4 %shard_map.69 = (bf16[40,256,128]{2,1,0:T(8,128)(2,1)S(1)}, bf16[40,256,128]{2,1,0:T(8,128)(2,1)S(1)}, s32[3,40]{1,0:T(4,128)S(4)}, s32[3,40]{1,0:T(4,128)S(4)}) custom-call(s32[3,40]{1,0:T(4,128)S(1)} %get-tuple-element.38.own_vmem, s32[3,40]{1,0:T(4,128)S(1)} %collective-permute-done.other_vmem, f32[40,128,128]{2,1,0:T(8,128)} %bitcast.138, ...), custom_call_target="tpu_custom_call" | custom-call | flops 5242880 | bytes 10485760 | tf_op jit(solution)/shard_map/pallas_call | solution.py:101
  11.5 1.5 %shard_map.70 = (f32[136,128]{1,0:T(8,128)S(1)}, f32[136,128]{1,0:T(8,128)S(1)}, f32[136,128]{1,0:T(8,128)S(1)}, f32[136,128]{1,0:T(8,128)S(1)}) custom-call(s32[3,40]{1,0:T(4,128)S(4)} %get-tuple-element.43.refs_0_, s32[3,40]{1,0:T(4,128)S(4)} %get-tuple-element.44.refs_1_, bf16[40,256,128]{2,1,0:T(8,128)(2,1)S(1)} %get-tuple-element.45.refs_2_, ...), custom_call_target="tpu_custom_call" | custom-call | flops 419430400 | bytes 5242880 | tf_op jit(solution)/shard_map/pallas_call | solution.py:192
  12.9 2.0 %collective-permute-start.8 = (f32[136,128]{1,0:T(8,128)S(1)}, f32[136,128]{1,0:T(8,128)S(1)}, u32[]{:S(2)}, u32[]{:S(2)}) collective-permute-start(f32[136,128]{1,0:T(8,128)S(1)} %get-tuple-element.52), channel_id=1, source_target_pairs={{0,5},{1,16},{2,7},{3,18},{4,1},{5,20},{6,3},{7,22},{8,13},{9,24},... | collective-permute-start | bytes 208904 | tf_op jit(solution)/shard_map/ppermute | solution.py:339
  14.9 2.9 %collective-permute-start.7 = (f32[136,128]{1,0:T(8,128)S(1)}, f32[136,128]{1,0:T(8,128)S(1)}, u32[]{:S(2)}, u32[]{:S(2)}) collective-permute-start(f32[136,128]{1,0:T(8,128)S(1)} %get-tuple-element.51), channel_id=1, source_target_pairs={{0,7},{1,24},{2,5},{3,26},{4,3},{5,28},{6,1},{7,30},{8,15},{9,16},... | collective-permute-start | bytes 208904 | tf_op jit(solution)/shard_map/ppermute | solution.py:339
  18.6 1.1 %collective-permute-done.7 = f32[136,128]{1,0:T(8,128)S(1)} collective-permute-done((f32[136,128]{1,0:T(8,128)S(1)}, f32[136,128]{1,0:T(8,128)S(1)}, u32[]{:S(2)}, u32[]{:S(2)}) %collective-permute-start.7) | collective-permute-done | bytes 69664 | tf_op jit(solution)/shard_map/ppermute | solution.py:339
  19.8 1.8 %collective-permute-done.6 = f32[136,128]{1,0:T(8,128)S(1)} collective-permute-done((f32[136,128]{1,0:T(8,128)S(1)}, f32[136,128]{1,0:T(8,128)S(1)}, u32[]{:S(2)}, u32[]{:S(2)}) %collective-permute-start.6) | collective-permute-done | bytes 69664 | tf_op jit(solution)/shard_map/ppermute | solution.py:339
  21.7 1.2 %collective-permute-done.9.other = f32[136,128]{1,0:T(8,128)S(1)} collective-permute-done((f32[136,128]{1,0:T(8,128)S(1)}, f32[136,128]{1,0:T(8,128)S(1)}, u32[]{:S(2)}, u32[]{:S(2)}) %collective-permute-start.9) | collective-permute-done | bytes 69664 | tf_op jit(solution)/shard_map/ppermute | solution.py:342
  24.0 1.4 %collective-permute-start.11 = (f32[144,128]{1,0:T(8,128)S(1)}, f32[144,128]{1,0:T(8,128)S(1)}, u32[]{:S(2)}, u32[]{:S(2)}) collective-permute-start(f32[144,128]{1,0:T(8,128)S(1)} %get-tuple-element.53.refs_4_), channel_id=1, source_target_pairs={{0,24},{1,7},{2,26},{3,5},{4,28},{5,3},{6,30},{7,1},{8,16},{9,15},... | collective-permute-start | bytes 221192 | tf_op jit(solution)/shard_map/ppermute | solution.py:339
  25.4 1.2 %collective-permute-start.12 = (f32[144,128]{1,0:T(8,128)S(1)}, f32[144,128]{1,0:T(8,128)S(1)}, u32[]{:S(2)}, u32[]{:S(2)}) collective-permute-start(f32[144,128]{1,0:T(8,128)S(1)} %get-tuple-element.53.refs_4_), channel_id=1, source_target_pairs={{0,8},{1,3},{2,10},{3,1},{4,12},{5,7},{6,14},{7,5},{8,0},{9,11},{1... | collective-permute-start | bytes 221192 | tf_op jit(solution)/shard_map/ppermute | solution.py:339
  27.5 1.7 %collective-permute-done.11.refs_6_ = f32[144,128]{1,0:T(8,128)S(1)} collective-permute-done((f32[144,128]{1,0:T(8,128)S(1)}, f32[144,128]{1,0:T(8,128)S(1)}, u32[]{:S(2)}, u32[]{:S(2)}) %collective-permute-start.11) | collective-permute-done | bytes 73760 | tf_op jit(solution)/shard_map/ppermute | solution.py:339
  29.8 1.3 %shard_map.72 = (f32[144,128]{1,0:T(8,128)S(1)}, f32[144,128]{1,0:T(8,128)S(1)}, f32[144,128]{1,0:T(8,128)S(1)}, f32[144,128]{1,0:T(8,128)S(1)}) custom-call(s32[3,40]{1,0:T(4,128)S(4)} %get-tuple-element.43.refs_0_, s32[3,40]{1,0:T(4,128)S(4)} %get-tuple-element.44.refs_1_, bf16[40,256,128]{2,1,0:T(8,128)(2,1)S(1)} %get-tuple-element.45.refs_2_, ...), custom_call_target="tpu_custom_call" | custom-call | flops 335544320 | bytes 5242880 | tf_op jit(solution)/shard_map/pallas_call | solution.py:192
  31.3 2.6 %collective-permute-start.14 = (f32[144,128]{1,0:T(8,128)S(1)}, f32[144,128]{1,0:T(8,128)S(1)}, u32[]{:S(2)}, u32[]{:S(2)}) collective-permute-start(f32[144,128]{1,0:T(8,128)S(1)} %get-tuple-element.56), channel_id=1, source_target_pairs={{0,7},{1,24},{2,5},{3,26},{4,3},{5,28},{6,1},{7,30},{8,15},{9,16},... | collective-permute-start | bytes 221192 | tf_op jit(solution)/shard_map/ppermute | solution.py:339
  34.9 1.1 %collective-permute-done.14 = f32[144,128]{1,0:T(8,128)S(1)} collective-permute-done((f32[144,128]{1,0:T(8,128)S(1)}, f32[144,128]{1,0:T(8,128)S(1)}, u32[]{:S(2)}, u32[]{:S(2)}) %collective-permute-start.14) | collective-permute-done | bytes 73760 | tf_op jit(solution)/shard_map/ppermute | solution.py:339
  36.0 1.7 %collective-permute-done.13 = f32[144,128]{1,0:T(8,128)S(1)} collective-permute-done((f32[144,128]{1,0:T(8,128)S(1)}, f32[144,128]{1,0:T(8,128)S(1)}, u32[]{:S(2)}, u32[]{:S(2)}) %collective-permute-start.13) | collective-permute-done | bytes 73760 | tf_op jit(solution)/shard_map/ppermute | solution.py:339
  39.7 1.4 %collective-permute-start.18 = (f32[144,128]{1,0:T(8,128)S(1)}, f32[144,128]{1,0:T(8,128)S(1)}, u32[]{:S(2)}, u32[]{:S(2)}) collective-permute-start(f32[144,128]{1,0:T(8,128)S(1)} %get-tuple-element.60.refs_4_), channel_id=1, source_target_pairs={{0,24},{1,7},{2,26},{3,5},{4,28},{5,3},{6,30},{7,1},{8,16},{9,15},... | collective-permute-start | bytes 221192 | tf_op jit(solution)/shard_map/ppermute | solution.py:339
  42.0 1.2 %collective-permute-start.19 = (f32[144,128]{1,0:T(8,128)S(1)}, f32[144,128]{1,0:T(8,128)S(1)}, u32[]{:S(2)}, u32[]{:S(2)}) collective-permute-start(f32[144,128]{1,0:T(8,128)S(1)} %get-tuple-element.60.refs_4_), channel_id=1, source_target_pairs={{0,8},{1,3},{2,10},{3,1},{4,12},{5,7},{6,14},{7,5},{8,0},{9,11},{1... | collective-permute-start | bytes 221192 | tf_op jit(solution)/shard_map/ppermute | solution.py:339
  43.2 1.8 %collective-permute-done.18.refs_6_ = f32[144,128]{1,0:T(8,128)S(1)} collective-permute-done((f32[144,128]{1,0:T(8,128)S(1)}, f32[144,128]{1,0:T(8,128)S(1)}, u32[]{:S(2)}, u32[]{:S(2)}) %collective-permute-start.18) | collective-permute-done | bytes 73760 | tf_op jit(solution)/shard_map/ppermute | solution.py:339
  46.8 1.3 %shard_map.74 = (f32[144,128]{1,0:T(8,128)S(1)}, f32[144,128]{1,0:T(8,128)S(1)}, f32[144,128]{1,0:T(8,128)S(1)}, f32[144,128]{1,0:T(8,128)S(1)}) custom-call(s32[3,40]{1,0:T(4,128)S(4)} %get-tuple-element.43.refs_0_, s32[3,40]{1,0:T(4,128)S(4)} %get-tuple-element.44.refs_1_, bf16[40,256,128]{2,1,0:T(8,128)(2,1)S(1)} %get-tuple-element.45.refs_2_, ...), custom_call_target="tpu_custom_call" | custom-call | flops 335544320 | bytes 5242880 | tf_op jit(solution)/shard_map/pallas_call | solution.py:192
  49.2 1.9 %collective-permute-start.22 = (f32[144,128]{1,0:T(8,128)S(1)}, f32[144,128]{1,0:T(8,128)S(1)}, u32[]{:S(2)}, u32[]{:S(2)}) collective-permute-start(f32[144,128]{1,0:T(8,128)S(1)} %get-tuple-element.67), channel_id=1, source_target_pairs={{0,7},{1,24},{2,5},{3,26},{4,3},{5,28},{6,1},{7,30},{8,15},{9,16},... | collective-permute-start | bytes 221192 | tf_op jit(solution)/shard_map/ppermute | solution.py:339
  52.1 1.8 %collective-permute-done.22 = f32[144,128]{1,0:T(8,128)S(1)} collective-permute-done((f32[144,128]{1,0:T(8,128)S(1)}, f32[144,128]{1,0:T(8,128)S(1)}, u32[]{:S(2)}, u32[]{:S(2)}) %collective-permute-start.22) | collective-permute-done | bytes 73760 | tf_op jit(solution)/shard_map/ppermute | solution.py:339
  55.7 1.6 %collective-permute-start.25 = (f32[16,128]{1,0:T(8,128)S(1)}, f32[16,128]{1,0:T(8,128)S(1)}, u32[]{:S(2)}, u32[]{:S(2)}) collective-permute-start(f32[16,128]{1,0:T(8,128)S(1)} %slice.135), channel_id=1, source_target_pairs={{0,7},{1,24},{2,5},{3,26},{4,3},{5,28},{6,1},{7,30},{8,15},{9,16},... | collective-permute-start | bytes 24584 | tf_op jit(solution)/shard_map/ppermute | solution.py:339
  57.3 1.6 %collective-permute-start.26 = (f32[16,128]{1,0:T(8,128)S(1)}, f32[16,128]{1,0:T(8,128)S(1)}, u32[]{:S(2)}, u32[]{:S(2)}) collective-permute-start(f32[16,128]{1,0:T(8,128)S(1)} %slice.135), channel_id=1, source_target_pairs={{0,5},{1,16},{2,7},{3,18},{4,1},{5,20},{6,3},{7,22},{8,13},{9,24},... | collective-permute-start | bytes 24584 | tf_op jit(solution)/shard_map/ppermute | solution.py:339
  (63 shorter events, 18.8 us)
Async XLA Ops:
  0.6 2.0 %collective-permute-start.1 = (f32[2,32,128]{2,1,0:T(8,128)}, f32[2,32,128]{2,1,0:T(8,128)S(1)}, u32[]{:S(2)}, u32[]{:S(2)}) collective-permute-start(f32[2,32,128]{2,1,0:T(8,128)} %raw_ref.1), channel_id=1, source_target_pairs={{0,1},{1,0},{2,3},{3,2},{4,5},{5,4},{6,7},{7,6},{8,9},{9,8},{10,11... | collective-permute-start | bytes 98312 | tf_op jit(solution)/shard_map/ppermute | solution.py:342
  2.7 5.2 %collective-permute-start.2 = (f32[40,128,128]{2,1,0:T(8,128)}, f32[40,128,128]{2,1,0:T(8,128)S(1)}, u32[]{:S(2)}, u32[]{:S(2)}) collective-permute-start(f32[40,128,128]{2,1,0:T(8,128)} %bitcast.137), channel_id=1, source_target_pairs={{0,1},{1,0},{2,3},{3,2},{4,5},{5,4},{6,7},{7,6},{8,9},{9,8},{10,11... | collective-permute-start | bytes 7864328 | tf_op jit(solution)/shard_map/ppermute | solution.py:342
  2.7 8.4 %collective-permute-start.3 = (f32[128,128]{1,0:T(8,128)S(1)}, f32[128,128]{1,0:T(8,128)S(1)}, u32[]{:S(2)}, u32[]{:S(2)}) collective-permute-start(f32[128,128]{1,0:T(8,128)S(1)} %bitcast.127), channel_id=1, source_target_pairs={{0,16},{1,5},{2,18},{3,7},{4,20},{5,1},{6,22},{7,3},{8,24},{9,13},... | collective-permute-start | bytes 196616 | tf_op jit(solution)/shard_map/ppermute | solution.py:339
  5.8 5.4 %collective-permute-start.4 = (f32[128,128]{1,0:T(8,128)S(1)}, f32[128,128]{1,0:T(8,128)S(1)}, u32[]{:S(2)}, u32[]{:S(2)}) collective-permute-start(f32[128,128]{1,0:T(8,128)S(1)} %bitcast.128), channel_id=1, source_target_pairs={{0,24},{1,7},{2,26},{3,5},{4,28},{5,3},{6,30},{7,1},{8,16},{9,15},... | collective-permute-start | bytes 196616 | tf_op jit(solution)/shard_map/ppermute | solution.py:339
  7.2 4.3 %collective-permute-start.5 = (f32[128,128]{1,0:T(8,128)S(1)}, f32[128,128]{1,0:T(8,128)S(1)}, u32[]{:S(2)}, u32[]{:S(2)}) collective-permute-start(f32[128,128]{1,0:T(8,128)S(1)} %bitcast.129), channel_id=1, source_target_pairs={{0,8},{1,3},{2,10},{3,1},{4,12},{5,7},{6,14},{7,5},{8,0},{9,11},{1... | collective-permute-start | bytes 196616 | tf_op jit(solution)/shard_map/ppermute | solution.py:339
  12.9 5.7 %collective-permute-start.8 = (f32[136,128]{1,0:T(8,128)S(1)}, f32[136,128]{1,0:T(8,128)S(1)}, u32[]{:S(2)}, u32[]{:S(2)}) collective-permute-start(f32[136,128]{1,0:T(8,128)S(1)} %get-tuple-element.52), channel_id=1, source_target_pairs={{0,5},{1,16},{2,7},{3,18},{4,1},{5,20},{6,3},{7,22},{8,13},{9,24},... | collective-permute-start | bytes 208904 | tf_op jit(solution)/shard_map/ppermute | solution.py:339
  14.9 4.9 %collective-permute-start.7 = (f32[136,128]{1,0:T(8,128)S(1)}, f32[136,128]{1,0:T(8,128)S(1)}, u32[]{:S(2)}, u32[]{:S(2)}) collective-permute-start(f32[136,128]{1,0:T(8,128)S(1)} %get-tuple-element.51), channel_id=1, source_target_pairs={{0,7},{1,24},{2,5},{3,26},{4,3},{5,28},{6,1},{7,30},{8,15},{9,16},... | collective-permute-start | bytes 208904 | tf_op jit(solution)/shard_map/ppermute | solution.py:339
  17.8 3.7 %collective-permute-start.6 = (f32[136,128]{1,0:T(8,128)S(1)}, f32[136,128]{1,0:T(8,128)S(1)}, u32[]{:S(2)}, u32[]{:S(2)}) collective-permute-start(f32[136,128]{1,0:T(8,128)S(1)} %get-tuple-element.50), channel_id=1, source_target_pairs={{0,3},{1,8},{2,1},{3,10},{4,7},{5,12},{6,5},{7,14},{8,11},{9,0},{1... | collective-permute-start | bytes 208904 | tf_op jit(solution)/shard_map/ppermute | solution.py:339
  23.1 4.4 %collective-permute-start.10 = (f32[144,128]{1,0:T(8,128)S(1)}, f32[144,128]{1,0:T(8,128)S(1)}, u32[]{:S(2)}, u32[]{:S(2)}) collective-permute-start(f32[144,128]{1,0:T(8,128)S(1)} %get-tuple-element.53.refs_4_), channel_id=1, source_target_pairs={{0,16},{1,5},{2,18},{3,7},{4,20},{5,1},{6,22},{7,3},{8,24},{9,13},... | collective-permute-start | bytes 221192 | tf_op jit(solution)/shard_map/ppermute | solution.py:339
  24.0 5.3 %collective-permute-start.11 = (f32[144,128]{1,0:T(8,128)S(1)}, f32[144,128]{1,0:T(8,128)S(1)}, u32[]{:S(2)}, u32[]{:S(2)}) collective-permute-start(f32[144,128]{1,0:T(8,128)S(1)} %get-tuple-element.53.refs_4_), channel_id=1, source_target_pairs={{0,24},{1,7},{2,26},{3,5},{4,28},{5,3},{6,30},{7,1},{8,16},{9,15},... | collective-permute-start | bytes 221192 | tf_op jit(solution)/shard_map/ppermute | solution.py:339
  25.4 4.4 %collective-permute-start.12 = (f32[144,128]{1,0:T(8,128)S(1)}, f32[144,128]{1,0:T(8,128)S(1)}, u32[]{:S(2)}, u32[]{:S(2)}) collective-permute-start(f32[144,128]{1,0:T(8,128)S(1)} %get-tuple-element.53.refs_4_), channel_id=1, source_target_pairs={{0,8},{1,3},{2,10},{3,1},{4,12},{5,7},{6,14},{7,5},{8,0},{9,11},{1... | collective-permute-start | bytes 221192 | tf_op jit(solution)/shard_map/ppermute | solution.py:339
  31.1 3.8 %collective-permute-start.15 = (f32[144,128]{1,0:T(8,128)S(1)}, f32[144,128]{1,0:T(8,128)S(1)}, u32[]{:S(2)}, u32[]{:S(2)}) collective-permute-start(f32[144,128]{1,0:T(8,128)S(1)} %get-tuple-element.57), channel_id=1, source_target_pairs={{0,5},{1,16},{2,7},{3,18},{4,1},{5,20},{6,3},{7,22},{8,13},{9,24},... | collective-permute-start | bytes 221192 | tf_op jit(solution)/shard_map/ppermute | solution.py:339
  31.3 4.7 %collective-permute-start.14 = (f32[144,128]{1,0:T(8,128)S(1)}, f32[144,128]{1,0:T(8,128)S(1)}, u32[]{:S(2)}, u32[]{:S(2)}) collective-permute-start(f32[144,128]{1,0:T(8,128)S(1)} %get-tuple-element.56), channel_id=1, source_target_pairs={{0,7},{1,24},{2,5},{3,26},{4,3},{5,28},{6,1},{7,30},{8,15},{9,16},... | collective-permute-start | bytes 221192 | tf_op jit(solution)/shard_map/ppermute | solution.py:339
  33.9 3.8 %collective-permute-start.13 = (f32[144,128]{1,0:T(8,128)S(1)}, f32[144,128]{1,0:T(8,128)S(1)}, u32[]{:S(2)}, u32[]{:S(2)}) collective-permute-start(f32[144,128]{1,0:T(8,128)S(1)} %get-tuple-element.55), channel_id=1, source_target_pairs={{0,3},{1,8},{2,1},{3,10},{4,7},{5,12},{6,5},{7,14},{8,11},{9,0},{1... | collective-permute-start | bytes 221192 | tf_op jit(solution)/shard_map/ppermute | solution.py:339
  39.7 5.3 %collective-permute-start.18 = (f32[144,128]{1,0:T(8,128)S(1)}, f32[144,128]{1,0:T(8,128)S(1)}, u32[]{:S(2)}, u32[]{:S(2)}) collective-permute-start(f32[144,128]{1,0:T(8,128)S(1)} %get-tuple-element.60.refs_4_), channel_id=1, source_target_pairs={{0,24},{1,7},{2,26},{3,5},{4,28},{5,3},{6,30},{7,1},{8,16},{9,15},... | collective-permute-start | bytes 221192 | tf_op jit(solution)/shard_map/ppermute | solution.py:339
  41.1 4.7 %collective-permute-start.17 = (f32[144,128]{1,0:T(8,128)S(1)}, f32[144,128]{1,0:T(8,128)S(1)}, u32[]{:S(2)}, u32[]{:S(2)}) collective-permute-start(f32[144,128]{1,0:T(8,128)S(1)} %get-tuple-element.60.refs_4_), channel_id=1, source_target_pairs={{0,16},{1,5},{2,18},{3,7},{4,20},{5,1},{6,22},{7,3},{8,24},{9,13},... | collective-permute-start | bytes 221192 | tf_op jit(solution)/shard_map/ppermute | solution.py:339
  42.0 4.4 %collective-permute-start.19 = (f32[144,128]{1,0:T(8,128)S(1)}, f32[144,128]{1,0:T(8,128)S(1)}, u32[]{:S(2)}, u32[]{:S(2)}) collective-permute-start(f32[144,128]{1,0:T(8,128)S(1)} %get-tuple-element.60.refs_4_), channel_id=1, source_target_pairs={{0,8},{1,3},{2,10},{3,1},{4,12},{5,7},{6,14},{7,5},{8,0},{9,11},{1... | collective-permute-start | bytes 221192 | tf_op jit(solution)/shard_map/ppermute | solution.py:339
  46.4 1.7 %collective-permute-start.20 = (f32[384,128]{1,0:T(8,128)S(1)}, f32[384,128]{1,0:T(8,128)S(1)}, u32[]{:S(2)}, u32[]{:S(2)}) collective-permute-start(f32[384,128]{1,0:T(8,128)S(1)} %pad_maximum_fusion), channel_id=1, source_target_pairs={{0,1},{1,0},{2,3},{3,2},{4,5},{5,4},{6,7},{7,6},{8,9},{9,8},{10,11... | collective-permute-start | bytes 589832 | tf_op jit(solution)/shard_map/ppermute | solution.py:342
  48.3 3.8 %collective-permute-start.23 = (f32[144,128]{1,0:T(8,128)S(1)}, f32[144,128]{1,0:T(8,128)S(1)}, u32[]{:S(2)}, u32[]{:S(2)}) collective-permute-start(f32[144,128]{1,0:T(8,128)S(1)} %get-tuple-element.68), channel_id=1, source_target_pairs={{0,5},{1,16},{2,7},{3,18},{4,1},{5,20},{6,3},{7,22},{8,13},{9,24},... | collective-permute-start | bytes 221192 | tf_op jit(solution)/shard_map/ppermute | solution.py:339
  49.2 4.7 %collective-permute-start.22 = (f32[144,128]{1,0:T(8,128)S(1)}, f32[144,128]{1,0:T(8,128)S(1)}, u32[]{:S(2)}, u32[]{:S(2)}) collective-permute-start(f32[144,128]{1,0:T(8,128)S(1)} %get-tuple-element.67), channel_id=1, source_target_pairs={{0,7},{1,24},{2,5},{3,26},{4,3},{5,28},{6,1},{7,30},{8,15},{9,16},... | collective-permute-start | bytes 221192 | tf_op jit(solution)/shard_map/ppermute | solution.py:339
  51.1 3.8 %collective-permute-start.21 = (f32[144,128]{1,0:T(8,128)S(1)}, f32[144,128]{1,0:T(8,128)S(1)}, u32[]{:S(2)}, u32[]{:S(2)}) collective-permute-start(f32[144,128]{1,0:T(8,128)S(1)} %get-tuple-element.66), channel_id=1, source_target_pairs={{0,3},{1,8},{2,1},{3,10},{4,7},{5,12},{6,5},{7,14},{8,11},{9,0},{1... | collective-permute-start | bytes 221192 | tf_op jit(solution)/shard_map/ppermute | solution.py:339
  54.9 4.1 %collective-permute-start.27 = (f32[16,128]{1,0:T(8,128)S(1)}, f32[16,128]{1,0:T(8,128)S(1)}, u32[]{:S(2)}, u32[]{:S(2)}) collective-permute-start(f32[16,128]{1,0:T(8,128)S(1)} %slice.135), channel_id=1, source_target_pairs={{0,3},{1,8},{2,1},{3,10},{4,7},{5,12},{6,5},{7,14},{8,11},{9,0},{1... | collective-permute-start | bytes 24584 | tf_op jit(solution)/shard_map/ppermute | solution.py:339
  55.7 4.0 %collective-permute-start.25 = (f32[16,128]{1,0:T(8,128)S(1)}, f32[16,128]{1,0:T(8,128)S(1)}, u32[]{:S(2)}, u32[]{:S(2)}) collective-permute-start(f32[16,128]{1,0:T(8,128)S(1)} %slice.135), channel_id=1, source_target_pairs={{0,7},{1,24},{2,5},{3,26},{4,3},{5,28},{6,1},{7,30},{8,15},{9,16},... | collective-permute-start | bytes 24584 | tf_op jit(solution)/shard_map/ppermute | solution.py:339
  57.3 3.1 %collective-permute-start.26 = (f32[16,128]{1,0:T(8,128)S(1)}, f32[16,128]{1,0:T(8,128)S(1)}, u32[]{:S(2)}, u32[]{:S(2)}) collective-permute-start(f32[16,128]{1,0:T(8,128)S(1)} %slice.135), channel_id=1, source_target_pairs={{0,5},{1,16},{2,7},{3,18},{4,1},{5,20},{6,3},{7,22},{8,13},{9,24},... | collective-permute-start | bytes 24584 | tf_op jit(solution)/shard_map/ppermute | solution.py:339
  (5 other events, 17.2 us)

commit v8 on v7

--- a/solution.py
+++ b/solution.py
@@ -455,6 +455,11 @@
         curve2 = curve2 + 2.0 * (e * a_h1 + f * a_h0 + e * f * a_10)
         curve2 = curve2 + 2.0 * ratio1 * (r2w1 + ratio0 * r2w0) + ratio1 * ratio1 * curve1
         step2 = g22 / curve2
+
+        def pick(field):
+            return jnp.where(core == 0, field[:seg], field[seg:])
+
+        raw, r1, w0, w1, h, q0, qh = (pick(field) for field in (raw, r1, w0, w1, h, q0, qh))
         p1 = r1 + ratio0 * raw
         s1 = w1 + ratio0 * w0
         r2 = h + e * w1 + f * w0
@@ -463,10 +468,7 @@
         smoothed = step0 * raw + step1 * p1 + step2 * p2
         residual = r2 - step2 * s2
 
-        def pick(field):
-            return jnp.where(core == 0, field[:seg], field[seg:])
-
-        return (pick(smoothed), pick(residual))
+        return (smoothed, residual)
 
     return shards
 

time: 62 us -> 62.1 us (level)
  transfers between devices with their start and end apart: 28 -> 28, of which waited for: 20 -> 19; matrix products, arithmetic and copies ran while one was open for 0% -> 0% of each run, Pallas kernels for 7% -> 7%
where the time goes in v8:
time: 62.1 us; the launch traced here: 61.4 us
  starting transfers between devices  31 us (50%)
  waiting for transfers between devices  19.9 us (32%)
  Pallas kernels  7.92 us (13%)
  between operations  1.45 us (2%)
  other arithmetic  0.99 us (2%)
    ppermute x21, starting transfers between devices, joint(): return lax.ppermute(array, ('row', 'col'), pairs)  28.7 us
    ppermute x21, waiting for transfers between devices, joint(): return lax.ppermute(array, ('row', 'col'), pairs)  16.9 us
    pallas_call x3, Pallas kernels, apply_blocks(): pl.pallas_call(functools.partial(apply_kernel, parts, per, width, with_de...  4.07 us
    ppermute x7, waiting for transfers between devices, swap(): return lax.ppermute(array, 'col', [(c, c ^ 1) for c in range(n_col)])  2.99 us
    ppermute x7, starting transfers between devices, swap(): return lax.ppermute(array, 'col', [(c, c ^ 1) for c in range(n_col)])  2.32 us
    pallas_call x1, Pallas kernels, split_blocks(): pl.pallas_call(split_kernel, in_specs=[VMEM, VMEM, pl.BlockSpec(memory_sp...  2.25 us
  transfers between devices with their start and end apart: 28, of which 19 were waited for; matrix products, arithmetic and copies ran while one was open for 0% of the time, Pallas kernels for 7%

profile of v8, /device:TPU:0, one launch (start us, length us, event | category | flops | bytes accessed | tf_op | source)
XLA Modules:
  0.0 61.4 jit_solution(17850219993262358799)
XLA Ops:
  2.7 3.0 %collective-permute-start.3 = (f32[128,128]{1,0:T(8,128)S(1)}, f32[128,128]{1,0:T(8,128)S(1)}, u32[]{:S(2)}, u32[]{:S(2)}) collective-permute-start(f32[128,128]{1,0:T(8,128)S(1)} %bitcast.128), channel_id=1, source_target_pairs={{0,16},{1,5},{2,18},{3,7},{4,20},{5,1},{6,22},{7,3},{8,24},{9,13},... | collective-permute-start | bytes 196616 | tf_op jit(solution)/shard_map/ppermute | solution.py:339
  5.8 1.4 %collective-permute-start.4 = (f32[128,128]{1,0:T(8,128)S(1)}, f32[128,128]{1,0:T(8,128)S(1)}, u32[]{:S(2)}, u32[]{:S(2)}) collective-permute-start(f32[128,128]{1,0:T(8,128)S(1)} %bitcast.129), channel_id=1, source_target_pairs={{0,24},{1,7},{2,26},{3,5},{4,28},{5,3},{6,30},{7,1},{8,16},{9,15},... | collective-permute-start | bytes 196616 | tf_op jit(solution)/shard_map/ppermute | solution.py:339
  8.7 2.3 %shard_map.69 = (bf16[40,256,128]{2,1,0:T(8,128)(2,1)S(1)}, bf16[40,256,128]{2,1,0:T(8,128)(2,1)S(1)}, s32[3,40]{1,0:T(4,128)S(4)}, s32[3,40]{1,0:T(4,128)S(4)}) custom-call(s32[3,40]{1,0:T(4,128)S(1)} %get-tuple-element.38.own_vmem, s32[3,40]{1,0:T(4,128)S(1)} %collective-permute-done.other_vmem, f32[40,128,128]{2,1,0:T(8,128)} %bitcast.135, ...), custom_call_target="tpu_custom_call" | custom-call | flops 5242880 | bytes 10485760 | tf_op jit(solution)/shard_map/pallas_call | solution.py:101
  11.5 1.5 %shard_map.70 = (f32[136,128]{1,0:T(8,128)S(1)}, f32[136,128]{1,0:T(8,128)S(1)}, f32[136,128]{1,0:T(8,128)S(1)}, f32[136,128]{1,0:T(8,128)S(1)}) custom-call(s32[3,40]{1,0:T(4,128)S(4)} %get-tuple-element.43.refs_0_, s32[3,40]{1,0:T(4,128)S(4)} %get-tuple-element.44.refs_1_, bf16[40,256,128]{2,1,0:T(8,128)(2,1)S(1)} %get-tuple-element.45.refs_2_, ...), custom_call_target="tpu_custom_call" | custom-call | flops 419430400 | bytes 5242880 | tf_op jit(solution)/shard_map/pallas_call | solution.py:192
  12.9 1.9 %collective-permute-start.8 = (f32[136,128]{1,0:T(8,128)S(1)}, f32[136,128]{1,0:T(8,128)S(1)}, u32[]{:S(2)}, u32[]{:S(2)}) collective-permute-start(f32[136,128]{1,0:T(8,128)S(1)} %get-tuple-element.52), channel_id=1, source_target_pairs={{0,5},{1,16},{2,7},{3,18},{4,1},{5,20},{6,3},{7,22},{8,13},{9,24},... | collective-permute-start | bytes 208904 | tf_op jit(solution)/shard_map/ppermute | solution.py:339
  14.9 3.0 %collective-permute-start.7 = (f32[136,128]{1,0:T(8,128)S(1)}, f32[136,128]{1,0:T(8,128)S(1)}, u32[]{:S(2)}, u32[]{:S(2)}) collective-permute-start(f32[136,128]{1,0:T(8,128)S(1)} %get-tuple-element.51), channel_id=1, source_target_pairs={{0,7},{1,24},{2,5},{3,26},{4,3},{5,28},{6,1},{7,30},{8,15},{9,16},... | collective-permute-start | bytes 208904 | tf_op jit(solution)/shard_map/ppermute | solution.py:339
  18.6 1.1 %collective-permute-done.7 = f32[136,128]{1,0:T(8,128)S(1)} collective-permute-done((f32[136,128]{1,0:T(8,128)S(1)}, f32[136,128]{1,0:T(8,128)S(1)}, u32[]{:S(2)}, u32[]{:S(2)}) %collective-permute-start.7) | collective-permute-done | bytes 69664 | tf_op jit(solution)/shard_map/ppermute | solution.py:339
  19.8 1.8 %collective-permute-done.6 = f32[136,128]{1,0:T(8,128)S(1)} collective-permute-done((f32[136,128]{1,0:T(8,128)S(1)}, f32[136,128]{1,0:T(8,128)S(1)}, u32[]{:S(2)}, u32[]{:S(2)}) %collective-permute-start.6) | collective-permute-done | bytes 69664 | tf_op jit(solution)/shard_map/ppermute | solution.py:339
  21.7 1.2 %collective-permute-done.9.other = f32[136,128]{1,0:T(8,128)S(1)} collective-permute-done((f32[136,128]{1,0:T(8,128)S(1)}, f32[136,128]{1,0:T(8,128)S(1)}, u32[]{:S(2)}, u32[]{:S(2)}) %collective-permute-start.9) | collective-permute-done | bytes 69664 | tf_op jit(solution)/shard_map/ppermute | solution.py:342
  23.9 1.6 %collective-permute-start.11 = (f32[144,128]{1,0:T(8,128)S(1)}, f32[144,128]{1,0:T(8,128)S(1)}, u32[]{:S(2)}, u32[]{:S(2)}) collective-permute-start(f32[144,128]{1,0:T(8,128)S(1)} %get-tuple-element.53.refs_4_), channel_id=1, source_target_pairs={{0,24},{1,7},{2,26},{3,5},{4,28},{5,3},{6,30},{7,1},{8,16},{9,15},... | collective-permute-start | bytes 221192 | tf_op jit(solution)/shard_map/ppermute | solution.py:339
  25.5 1.2 %collective-permute-start.12 = (f32[144,128]{1,0:T(8,128)S(1)}, f32[144,128]{1,0:T(8,128)S(1)}, u32[]{:S(2)}, u32[]{:S(2)}) collective-permute-start(f32[144,128]{1,0:T(8,128)S(1)} %get-tuple-element.53.refs_4_), channel_id=1, source_target_pairs={{0,8},{1,3},{2,10},{3,1},{4,12},{5,7},{6,14},{7,5},{8,0},{9,11},{1... | collective-permute-start | bytes 221192 | tf_op jit(solution)/shard_map/ppermute | solution.py:339
  27.5 1.6 %collective-permute-done.11.refs_6_ = f32[144,128]{1,0:T(8,128)S(1)} collective-permute-done((f32[144,128]{1,0:T(8,128)S(1)}, f32[144,128]{1,0:T(8,128)S(1)}, u32[]{:S(2)}, u32[]{:S(2)}) %collective-permute-start.11) | collective-permute-done | bytes 73760 | tf_op jit(solution)/shard_map/ppermute | solution.py:339
  29.8 1.3 %shard_map.72 = (f32[144,128]{1,0:T(8,128)S(1)}, f32[144,128]{1,0:T(8,128)S(1)}, f32[144,128]{1,0:T(8,128)S(1)}, f32[144,128]{1,0:T(8,128)S(1)}) custom-call(s32[3,40]{1,0:T(4,128)S(4)} %get-tuple-element.43.refs_0_, s32[3,40]{1,0:T(4,128)S(4)} %get-tuple-element.44.refs_1_, bf16[40,256,128]{2,1,0:T(8,128)(2,1)S(1)} %get-tuple-element.45.refs_2_, ...), custom_call_target="tpu_custom_call" | custom-call | flops 335544320 | bytes 5242880 | tf_op jit(solution)/shard_map/pallas_call | solution.py:192
  31.3 2.4 %collective-permute-start.14 = (f32[144,128]{1,0:T(8,128)S(1)}, f32[144,128]{1,0:T(8,128)S(1)}, u32[]{:S(2)}, u32[]{:S(2)}) collective-permute-start(f32[144,128]{1,0:T(8,128)S(1)} %get-tuple-element.56), channel_id=1, source_target_pairs={{0,7},{1,24},{2,5},{3,26},{4,3},{5,28},{6,1},{7,30},{8,15},{9,16},... | collective-permute-start | bytes 221192 | tf_op jit(solution)/shard_map/ppermute | solution.py:339
  34.9 1.1 %collective-permute-done.14 = f32[144,128]{1,0:T(8,128)S(1)} collective-permute-done((f32[144,128]{1,0:T(8,128)S(1)}, f32[144,128]{1,0:T(8,128)S(1)}, u32[]{:S(2)}, u32[]{:S(2)}) %collective-permute-start.14) | collective-permute-done | bytes 73760 | tf_op jit(solution)/shard_map/ppermute | solution.py:339
  36.0 1.5 %collective-permute-done.13 = f32[144,128]{1,0:T(8,128)S(1)} collective-permute-done((f32[144,128]{1,0:T(8,128)S(1)}, f32[144,128]{1,0:T(8,128)S(1)}, u32[]{:S(2)}, u32[]{:S(2)}) %collective-permute-start.13) | collective-permute-done | bytes 73760 | tf_op jit(solution)/shard_map/ppermute | solution.py:339
  40.6 1.6 %collective-permute-start.18 = (f32[144,128]{1,0:T(8,128)S(1)}, f32[144,128]{1,0:T(8,128)S(1)}, u32[]{:S(2)}, u32[]{:S(2)}) collective-permute-start(f32[144,128]{1,0:T(8,128)S(1)} %get-tuple-element.60.refs_4_), channel_id=1, source_target_pairs={{0,24},{1,7},{2,26},{3,5},{4,28},{5,3},{6,30},{7,1},{8,16},{9,15},... | collective-permute-start | bytes 221192 | tf_op jit(solution)/shard_map/ppermute | solution.py:339
  43.3 2.6 %collective-permute-done.18.refs_6_ = f32[144,128]{1,0:T(8,128)S(1)} collective-permute-done((f32[144,128]{1,0:T(8,128)S(1)}, f32[144,128]{1,0:T(8,128)S(1)}, u32[]{:S(2)}, u32[]{:S(2)}) %collective-permute-start.18) | collective-permute-done | bytes 73760 | tf_op jit(solution)/shard_map/ppermute | solution.py:339
  46.8 1.3 %shard_map.74 = (f32[144,128]{1,0:T(8,128)S(1)}, f32[144,128]{1,0:T(8,128)S(1)}, f32[144,128]{1,0:T(8,128)S(1)}, f32[144,128]{1,0:T(8,128)S(1)}) custom-call(s32[3,40]{1,0:T(4,128)S(4)} %get-tuple-element.43.refs_0_, s32[3,40]{1,0:T(4,128)S(4)} %get-tuple-element.44.refs_1_, bf16[40,256,128]{2,1,0:T(8,128)(2,1)S(1)} %get-tuple-element.45.refs_2_, ...), custom_call_target="tpu_custom_call" | custom-call | flops 335544320 | bytes 5242880 | tf_op jit(solution)/shard_map/pallas_call | solution.py:192
  49.1 1.8 %collective-permute-start.22 = (f32[144,128]{1,0:T(8,128)S(1)}, f32[144,128]{1,0:T(8,128)S(1)}, u32[]{:S(2)}, u32[]{:S(2)}) collective-permute-start(f32[144,128]{1,0:T(8,128)S(1)} %get-tuple-element.67), channel_id=1, source_target_pairs={{0,7},{1,24},{2,5},{3,26},{4,3},{5,28},{6,1},{7,30},{8,15},{9,16},... | collective-permute-start | bytes 221192 | tf_op jit(solution)/shard_map/ppermute | solution.py:339
  52.1 1.7 %collective-permute-done.22 = f32[144,128]{1,0:T(8,128)S(1)} collective-permute-done((f32[144,128]{1,0:T(8,128)S(1)}, f32[144,128]{1,0:T(8,128)S(1)}, u32[]{:S(2)}, u32[]{:S(2)}) %collective-permute-start.22) | collective-permute-done | bytes 73760 | tf_op jit(solution)/shard_map/ppermute | solution.py:339
  54.7 1.3 %collective-permute-start.27 = (f32[16,128]{1,0:T(8,128)S(1)}, f32[16,128]{1,0:T(8,128)S(1)}, u32[]{:S(2)}, u32[]{:S(2)}) collective-permute-start(f32[16,128]{1,0:T(8,128)S(1)} %slice.189), channel_id=1, source_target_pairs={{0,3},{1,8},{2,1},{3,10},{4,7},{5,12},{6,5},{7,14},{8,11},{9,0},{1... | collective-permute-start | bytes 24584 | tf_op jit(solution)/shard_map/ppermute | solution.py:339
  56.0 1.3 %collective-permute-start.25 = (f32[16,128]{1,0:T(8,128)S(1)}, f32[16,128]{1,0:T(8,128)S(1)}, u32[]{:S(2)}, u32[]{:S(2)}) collective-permute-start(f32[16,128]{1,0:T(8,128)S(1)} %slice.189), channel_id=1, source_target_pairs={{0,7},{1,24},{2,5},{3,26},{4,3},{5,28},{6,1},{7,30},{8,15},{9,16},... | collective-permute-start | bytes 24584 | tf_op jit(solution)/shard_map/ppermute | solution.py:339
  57.3 1.8 %collective-permute-start.26 = (f32[16,128]{1,0:T(8,128)S(1)}, f32[16,128]{1,0:T(8,128)S(1)}, u32[]{:S(2)}, u32[]{:S(2)}) collective-permute-start(f32[16,128]{1,0:T(8,128)S(1)} %slice.189), channel_id=1, source_target_pairs={{0,5},{1,16},{2,7},{3,18},{4,1},{5,20},{6,3},{7,22},{8,13},{9,24},... | collective-permute-start | bytes 24584 | tf_op jit(solution)/shard_map/ppermute | solution.py:339
  (66 shorter events, 18.5 us)
Async XLA Ops:
  0.6 2.0 %collective-permute-start.1 = (f32[2,32,128]{2,1,0:T(8,128)}, f32[2,32,128]{2,1,0:T(8,128)S(1)}, u32[]{:S(2)}, u32[]{:S(2)}) collective-permute-start(f32[2,32,128]{2,1,0:T(8,128)} %raw_ref.1), channel_id=1, source_target_pairs={{0,1},{1,0},{2,3},{3,2},{4,5},{5,4},{6,7},{7,6},{8,9},{9,8},{10,11... | collective-permute-start | bytes 98312 | tf_op jit(solution)/shard_map/ppermute | solution.py:342
  2.7 5.2 %collective-permute-start.2 = (f32[40,128,128]{2,1,0:T(8,128)}, f32[40,128,128]{2,1,0:T(8,128)S(1)}, u32[]{:S(2)}, u32[]{:S(2)}) collective-permute-start(f32[40,128,128]{2,1,0:T(8,128)} %bitcast.134), channel_id=1, source_target_pairs={{0,1},{1,0},{2,3},{3,2},{4,5},{5,4},{6,7},{7,6},{8,9},{9,8},{10,11... | collective-permute-start | bytes 7864328 | tf_op jit(solution)/shard_map/ppermute | solution.py:342
  2.7 8.2 %collective-permute-start.3 = (f32[128,128]{1,0:T(8,128)S(1)}, f32[128,128]{1,0:T(8,128)S(1)}, u32[]{:S(2)}, u32[]{:S(2)}) collective-permute-start(f32[128,128]{1,0:T(8,128)S(1)} %bitcast.128), channel_id=1, source_target_pairs={{0,16},{1,5},{2,18},{3,7},{4,20},{5,1},{6,22},{7,3},{8,24},{9,13},... | collective-permute-start | bytes 196616 | tf_op jit(solution)/shard_map/ppermute | solution.py:339
  5.8 5.2 %collective-permute-start.4 = (f32[128,128]{1,0:T(8,128)S(1)}, f32[128,128]{1,0:T(8,128)S(1)}, u32[]{:S(2)}, u32[]{:S(2)}) collective-permute-start(f32[128,128]{1,0:T(8,128)S(1)} %bitcast.129), channel_id=1, source_target_pairs={{0,24},{1,7},{2,26},{3,5},{4,28},{5,3},{6,30},{7,1},{8,16},{9,15},... | collective-permute-start | bytes 196616 | tf_op jit(solution)/shard_map/ppermute | solution.py:339
  7.2 4.3 %collective-permute-start.5 = (f32[128,128]{1,0:T(8,128)S(1)}, f32[128,128]{1,0:T(8,128)S(1)}, u32[]{:S(2)}, u32[]{:S(2)}) collective-permute-start(f32[128,128]{1,0:T(8,128)S(1)} %bitcast.130), channel_id=1, source_target_pairs={{0,8},{1,3},{2,10},{3,1},{4,12},{5,7},{6,14},{7,5},{8,0},{9,11},{1... | collective-permute-start | bytes 196616 | tf_op jit(solution)/shard_map/ppermute | solution.py:339
  12.9 5.7 %collective-permute-start.8 = (f32[136,128]{1,0:T(8,128)S(1)}, f32[136,128]{1,0:T(8,128)S(1)}, u32[]{:S(2)}, u32[]{:S(2)}) collective-permute-start(f32[136,128]{1,0:T(8,128)S(1)} %get-tuple-element.52), channel_id=1, source_target_pairs={{0,5},{1,16},{2,7},{3,18},{4,1},{5,20},{6,3},{7,22},{8,13},{9,24},... | collective-permute-start | bytes 208904 | tf_op jit(solution)/shard_map/ppermute | solution.py:339
  14.9 4.9 %collective-permute-start.7 = (f32[136,128]{1,0:T(8,128)S(1)}, f32[136,128]{1,0:T(8,128)S(1)}, u32[]{:S(2)}, u32[]{:S(2)}) collective-permute-start(f32[136,128]{1,0:T(8,128)S(1)} %get-tuple-element.51), channel_id=1, source_target_pairs={{0,7},{1,24},{2,5},{3,26},{4,3},{5,28},{6,1},{7,30},{8,15},{9,16},... | collective-permute-start | bytes 208904 | tf_op jit(solution)/shard_map/ppermute | solution.py:339
  17.8 3.7 %collective-permute-start.6 = (f32[136,128]{1,0:T(8,128)S(1)}, f32[136,128]{1,0:T(8,128)S(1)}, u32[]{:S(2)}, u32[]{:S(2)}) collective-permute-start(f32[136,128]{1,0:T(8,128)S(1)} %get-tuple-element.50), channel_id=1, source_target_pairs={{0,3},{1,8},{2,1},{3,10},{4,7},{5,12},{6,5},{7,14},{8,11},{9,0},{1... | collective-permute-start | bytes 208904 | tf_op jit(solution)/shard_map/ppermute | solution.py:339
  23.2 4.4 %collective-permute-start.10 = (f32[144,128]{1,0:T(8,128)S(1)}, f32[144,128]{1,0:T(8,128)S(1)}, u32[]{:S(2)}, u32[]{:S(2)}) collective-permute-start(f32[144,128]{1,0:T(8,128)S(1)} %get-tuple-element.53.refs_4_), channel_id=1, source_target_pairs={{0,16},{1,5},{2,18},{3,7},{4,20},{5,1},{6,22},{7,3},{8,24},{9,13},... | collective-permute-start | bytes 221192 | tf_op jit(solution)/shard_map/ppermute | solution.py:339
  23.9 5.3 %collective-permute-start.11 = (f32[144,128]{1,0:T(8,128)S(1)}, f32[144,128]{1,0:T(8,128)S(1)}, u32[]{:S(2)}, u32[]{:S(2)}) collective-permute-start(f32[144,128]{1,0:T(8,128)S(1)} %get-tuple-element.53.refs_4_), channel_id=1, source_target_pairs={{0,24},{1,7},{2,26},{3,5},{4,28},{5,3},{6,30},{7,1},{8,16},{9,15},... | collective-permute-start | bytes 221192 | tf_op jit(solution)/shard_map/ppermute | solution.py:339
  25.5 4.4 %collective-permute-start.12 = (f32[144,128]{1,0:T(8,128)S(1)}, f32[144,128]{1,0:T(8,128)S(1)}, u32[]{:S(2)}, u32[]{:S(2)}) collective-permute-start(f32[144,128]{1,0:T(8,128)S(1)} %get-tuple-element.53.refs_4_), channel_id=1, source_target_pairs={{0,8},{1,3},{2,10},{3,1},{4,12},{5,7},{6,14},{7,5},{8,0},{9,11},{1... | collective-permute-start | bytes 221192 | tf_op jit(solution)/shard_map/ppermute | solution.py:339
  31.1 3.8 %collective-permute-start.15 = (f32[144,128]{1,0:T(8,128)S(1)}, f32[144,128]{1,0:T(8,128)S(1)}, u32[]{:S(2)}, u32[]{:S(2)}) collective-permute-start(f32[144,128]{1,0:T(8,128)S(1)} %get-tuple-element.57), channel_id=1, source_target_pairs={{0,5},{1,16},{2,7},{3,18},{4,1},{5,20},{6,3},{7,22},{8,13},{9,24},... | collective-permute-start | bytes 221192 | tf_op jit(solution)/shard_map/ppermute | solution.py:339
  31.3 4.7 %collective-permute-start.14 = (f32[144,128]{1,0:T(8,128)S(1)}, f32[144,128]{1,0:T(8,128)S(1)}, u32[]{:S(2)}, u32[]{:S(2)}) collective-permute-start(f32[144,128]{1,0:T(8,128)S(1)} %get-tuple-element.56), channel_id=1, source_target_pairs={{0,7},{1,24},{2,5},{3,26},{4,3},{5,28},{6,1},{7,30},{8,15},{9,16},... | collective-permute-start | bytes 221192 | tf_op jit(solution)/shard_map/ppermute | solution.py:339
  33.8 3.8 %collective-permute-start.13 = (f32[144,128]{1,0:T(8,128)S(1)}, f32[144,128]{1,0:T(8,128)S(1)}, u32[]{:S(2)}, u32[]{:S(2)}) collective-permute-start(f32[144,128]{1,0:T(8,128)S(1)} %get-tuple-element.55), channel_id=1, source_target_pairs={{0,3},{1,8},{2,1},{3,10},{4,7},{5,12},{6,5},{7,14},{8,11},{9,0},{1... | collective-permute-start | bytes 221192 | tf_op jit(solution)/shard_map/ppermute | solution.py:339
  37.6 1.7 %collective-permute-start.16 = (f32[144,128]{1,0:T(8,128)S(1)}, f32[144,128]{1,0:T(8,128)S(1)}, u32[]{:S(2)}, u32[]{:S(2)}) collective-permute-start(f32[144,128]{1,0:T(8,128)S(1)} %add_add_fusion.1.mine), channel_id=1, source_target_pairs={{0,1},{1,0},{2,3},{3,2},{4,5},{5,4},{6,7},{7,6},{8,9},{9,8},{10,11... | collective-permute-start | bytes 221192 | tf_op jit(solution)/shard_map/ppermute | solution.py:342
  39.7 6.2 %collective-permute-start.17 = (f32[144,128]{1,0:T(8,128)S(1)}, f32[144,128]{1,0:T(8,128)S(1)}, u32[]{:S(2)}, u32[]{:S(2)}) collective-permute-start(f32[144,128]{1,0:T(8,128)S(1)} %get-tuple-element.60.refs_4_), channel_id=1, source_target_pairs={{0,16},{1,5},{2,18},{3,7},{4,20},{5,1},{6,22},{7,3},{8,24},{9,13},... | collective-permute-start | bytes 221192 | tf_op jit(solution)/shard_map/ppermute | solution.py:339
  40.6 5.3 %collective-permute-start.18 = (f32[144,128]{1,0:T(8,128)S(1)}, f32[144,128]{1,0:T(8,128)S(1)}, u32[]{:S(2)}, u32[]{:S(2)}) collective-permute-start(f32[144,128]{1,0:T(8,128)S(1)} %get-tuple-element.60.refs_4_), channel_id=1, source_target_pairs={{0,24},{1,7},{2,26},{3,5},{4,28},{5,3},{6,30},{7,1},{8,16},{9,15},... | collective-permute-start | bytes 221192 | tf_op jit(solution)/shard_map/ppermute | solution.py:339
  42.2 4.4 %collective-permute-start.19 = (f32[144,128]{1,0:T(8,128)S(1)}, f32[144,128]{1,0:T(8,128)S(1)}, u32[]{:S(2)}, u32[]{:S(2)}) collective-permute-start(f32[144,128]{1,0:T(8,128)S(1)} %get-tuple-element.60.refs_4_), channel_id=1, source_target_pairs={{0,8},{1,3},{2,10},{3,1},{4,12},{5,7},{6,14},{7,5},{8,0},{9,11},{1... | collective-permute-start | bytes 221192 | tf_op jit(solution)/shard_map/ppermute | solution.py:339
  48.3 3.8 %collective-permute-start.23 = (f32[144,128]{1,0:T(8,128)S(1)}, f32[144,128]{1,0:T(8,128)S(1)}, u32[]{:S(2)}, u32[]{:S(2)}) collective-permute-start(f32[144,128]{1,0:T(8,128)S(1)} %get-tuple-element.68), channel_id=1, source_target_pairs={{0,5},{1,16},{2,7},{3,18},{4,1},{5,20},{6,3},{7,22},{8,13},{9,24},... | collective-permute-start | bytes 221192 | tf_op jit(solution)/shard_map/ppermute | solution.py:339
  49.1 4.7 %collective-permute-start.22 = (f32[144,128]{1,0:T(8,128)S(1)}, f32[144,128]{1,0:T(8,128)S(1)}, u32[]{:S(2)}, u32[]{:S(2)}) collective-permute-start(f32[144,128]{1,0:T(8,128)S(1)} %get-tuple-element.67), channel_id=1, source_target_pairs={{0,7},{1,24},{2,5},{3,26},{4,3},{5,28},{6,1},{7,30},{8,15},{9,16},... | collective-permute-start | bytes 221192 | tf_op jit(solution)/shard_map/ppermute | solution.py:339
  50.9 3.8 %collective-permute-start.21 = (f32[144,128]{1,0:T(8,128)S(1)}, f32[144,128]{1,0:T(8,128)S(1)}, u32[]{:S(2)}, u32[]{:S(2)}) collective-permute-start(f32[144,128]{1,0:T(8,128)S(1)} %get-tuple-element.66), channel_id=1, source_target_pairs={{0,3},{1,8},{2,1},{3,10},{4,7},{5,12},{6,5},{7,14},{8,11},{9,0},{1... | collective-permute-start | bytes 221192 | tf_op jit(solution)/shard_map/ppermute | solution.py:339
  54.7 4.5 %collective-permute-start.27 = (f32[16,128]{1,0:T(8,128)S(1)}, f32[16,128]{1,0:T(8,128)S(1)}, u32[]{:S(2)}, u32[]{:S(2)}) collective-permute-start(f32[16,128]{1,0:T(8,128)S(1)} %slice.189), channel_id=1, source_target_pairs={{0,3},{1,8},{2,1},{3,10},{4,7},{5,12},{6,5},{7,14},{8,11},{9,0},{1... | collective-permute-start | bytes 24584 | tf_op jit(solution)/shard_map/ppermute | solution.py:339
  56.0 4.0 %collective-permute-start.25 = (f32[16,128]{1,0:T(8,128)S(1)}, f32[16,128]{1,0:T(8,128)S(1)}, u32[]{:S(2)}, u32[]{:S(2)}) collective-permute-start(f32[16,128]{1,0:T(8,128)S(1)} %slice.189), channel_id=1, source_target_pairs={{0,7},{1,24},{2,5},{3,26},{4,3},{5,28},{6,1},{7,30},{8,15},{9,16},... | collective-permute-start | bytes 24584 | tf_op jit(solution)/shard_map/ppermute | solution.py:339
  57.3 3.1 %collective-permute-start.26 = (f32[16,128]{1,0:T(8,128)S(1)}, f32[16,128]{1,0:T(8,128)S(1)}, u32[]{:S(2)}, u32[]{:S(2)}) collective-permute-start(f32[16,128]{1,0:T(8,128)S(1)} %slice.189), channel_id=1, source_target_pairs={{0,5},{1,16},{2,7},{3,18},{4,1},{5,20},{6,3},{7,22},{8,13},{9,24},... | collective-permute-start | bytes 24584 | tf_op jit(solution)/shard_map/ppermute | solution.py:339
  (5 other events, 17.1 us)
